TPU v7x, 32 devices: a whole 2x2x4 slice. The times are simulated.
32 devices in a mesh: grp: 2 (over y), blk: 8 (over z, x), chan: 2 (over core).
Axes of the slice: x: 2, y: 2, z: 4, core: 2. Of those that a mesh axis runs over, the one named last changes fastest.
Arguments:
- record: bfloat16 [16, 10000, 191], P(('grp', 'blk'), 'chan'), parts along dimension 0, may hold values from -300 to 300, as said below
- templates: bfloat16 [8, 512, 128], P('blk', 'chan'), may hold values from -6 to 6
- offsets: int32 [8], P('blk'), may hold values from 0 to 9488
- valid_counts: int32 [8], P('blk'), may hold values from 256 to 512
Outputs:
- detection: float32 [16, 8, 64], P(('grp', 'blk'), None, 'chan'), parts along dimension 0
There are 2 independent parts, one for each index of `grp`. A program takes and returns all parts, laid end to end along the dimension named above; an argument that names none is the same for every part. Nothing has to cross between parts.
Inputs may be any that keep to these rules, and one draw needn't show every extreme that they name: Each record value comes from a noise draw scaled by a channel gain and a time envelope.
All inputs are finite; a program needn't handle non-finite values.
Results may differ from a plain program's by a relative error of at most 0.005.
Values may be sent and summed in bfloat16 or wider, within the bound.
No kernel may reach another device: no remote copies, remote signals or barrier semaphores. Data moves between devices by JAX's collectives and lax.ppermute only.
A program may use at most 64 MiB of HBM per device.

v0:
```python
import functools

import jax
import jax.numpy as jnp
from jax import lax
from jax.experimental import pallas as pl
from jax.experimental.pallas import tpu as pltpu
from jax.sharding import PartitionSpec as P

LANES = 128
META = 16
CHUNK = 8


def pack_kernel(off_ref, cnt_ref, tmpl_ref, out_ref):
    rows, taps = tmpl_ref.shape
    out_ref[:taps, :] = jnp.transpose(tmpl_ref[...].astype(jnp.float32)).astype(out_ref.dtype)
    lane = lax.broadcasted_iota(jnp.int32, (META, rows), 1)
    off, cnt = off_ref[0], cnt_ref[0]
    level = lax.broadcasted_iota(jnp.int32, (META, rows), 0)
    value = jnp.where(lane == 0, off, cnt)
    meta = jnp.where(level == 0, value >> 8, value & 255)
    out_ref[taps:, :] = meta.astype(jnp.float32).astype(out_ref.dtype)


def pack(templates, offsets, counts):
    rows, taps = templates.shape
    return pl.pallas_call(
        pack_kernel,
        out_shape=jax.ShapeDtypeStruct((taps + META, rows), templates.dtype),
        in_specs=[
            pl.BlockSpec(memory_space=pltpu.SMEM),
            pl.BlockSpec(memory_space=pltpu.SMEM),
            pl.BlockSpec(memory_space=pltpu.VMEM),
        ],
        out_specs=pl.BlockSpec(memory_space=pltpu.VMEM),
        name="pack",
    )(offsets, counts, templates)


def score_kernel(taps, shifts, places, *refs):
    n = len(places)
    mine, theirs = refs[:2]
    packed = refs[2 : 2 + n]
    keep_ref, send_ref, tmpl, pair, gains, ints_v, ints, tails, rows_f, diff_f, sums, total, sem = refs[2 + n :]
    samples, channels = mine.shape
    width = packed[0].shape[1]
    groups = width // LANES
    whole_tiles = channels // LANES
    rest = channels - whole_tiles * LANES
    chan = lax.axis_index("chan")
    blocks = shifts // 8
    steps = taps // 8
    lane_row = lax.broadcasted_iota(jnp.int32, (1, LANES), 1)

    for i in range(n):
        meta = packed[i][taps:, :LANES].astype(jnp.float32)
        ints_v[i : i + 1, :] = (meta[:1] * 256.0 + meta[1:2]).astype(jnp.int32)
    to_scalars = pltpu.make_async_copy(ints_v, ints, sem)
    to_scalars.start()
    for i in range(n):
        for g in range(groups):
            block = packed[i][:taps, g * LANES : (g + 1) * LANES].astype(jnp.float32)
            tmpl[i * groups + g, :taps, :] = block
            tiles = [block[8 * a : 8 * a + 8] for a in range(steps)]
            energy = jnp.zeros((8, LANES), jnp.float32)
            for a in range(0, steps, 2):
                pair[i * groups + g, 4 * a : 4 * a + 8, :] = tiles[a] + tiles[a + 1]
                energy = energy + (tiles[a] * tiles[a] + tiles[a + 1] * tiles[a + 1])
            gains[i * groups + g : i * groups + g + 1, :] = jnp.sum(energy, axis=0, keepdims=True)
    if rest:
        tails[0, :, :rest] = mine[:, whole_tiles * LANES :]
        tails[1, :, :rest] = theirs[:, whole_tiles * LANES :]
    rows_f[(samples // 8) * 8 :, :] = jnp.zeros_like(rows_f[(samples // 8) * 8 :, :])
    to_scalars.wait()
    for i in range(n):
        count = jnp.full((1, LANES), ints[i, 1], jnp.int32)
        ratio = jnp.sqrt(taps / count.astype(jnp.float32)) * (1.0 / taps)
        for g in range(groups):
            at = i * groups + g
            gain = lax.rsqrt(gains[at : at + 1, :] / taps + 1e-06) * ratio
            gains[at : at + 1, :] = jnp.where(lane_row + (chan * width + g * LANES) < count, gain, 0.0)

    wide = lax.broadcasted_iota(jnp.int32, (samples, LANES), 1)

    def turned(low, high, turn):
        mixed = jnp.where(wide < turn, high.astype(jnp.float32), low.astype(jnp.float32))
        return pltpu.roll(mixed, (LANES - turn) & (LANES - 1), 1)

    def item(index, _):
        i, g = index // groups, index % groups
        first = ints[i, 0] + chan * width + g * LANES
        split = channels - first
        half = jnp.where(split > 0, 0, 1)
        local = first - half * channels
        tile = local >> 7
        fast = ((split >= LANES) | (split <= 0)) & (tile + 1 < whole_tiles)

        for source, here in ((mine, half == chan), (theirs, half != chan)):

            @pl.when(fast & here)
            def _():
                at = pl.multiple_of(tile * LANES, LANES)
                rows_f[:samples, :] = turned(
                    source[:, pl.ds(at, LANES)], source[:, pl.ds(at + LANES, LANES)], local & (LANES - 1)
                )

        @pl.when(jnp.logical_not(fast))
        def _():
            sides = []
            for side in range(2):
                begin = first - side * channels
                turn = begin & (LANES - 1)
                found = []
                for m in range(2):
                    want = (begin >> 7) + m
                    at = pl.multiple_of(jnp.clip(want, 0, whole_tiles - 1) * LANES, LANES)
                    value = jnp.where(
                        chan == side,
                        mine[:, pl.ds(at, LANES)].astype(jnp.float32),
                        theirs[:, pl.ds(at, LANES)].astype(jnp.float32),
                    )
                    if rest:
                        tail = tails[jnp.where(chan == side, 0, 1)].astype(jnp.float32)
                        value = jnp.where(want >= whole_tiles, tail, value)
                    found.append(value)
                sides.append(turned(found[0], found[1], turn))
            rows_f[:samples, :] = jnp.where(wide < split, sides[0], sides[1])

        held = [rows_f[8 * m : 8 * m + 8, :] for m in range(steps + blocks)]
        for m in range(steps + blocks - 1):
            diff_f[8 * m : 8 * m + 8, :] = held[m] - held[m + 1]
        level = [v * v for v in held]
        span = 1
        while span < steps:
            level = [level[m] + level[m + span] for m in range(len(level) - span)]
            span *= 2
        for m in range(blocks + 1):
            sums[8 * m : 8 * m + 8, :] = level[m]

        half_blocks, half_steps = blocks // 2, steps // 2
        reach = half_blocks + half_steps - 1

        def conv(twice, carry):
            lists = [list(part) for part in carry]
            one, two, three, window = lists
            for extra in range(2):
                q = 2 * twice + extra
                for b in range(blocks):
                    window[b] = window[b] + sums[pl.ds(8 * b + q, 8), :]
                even = [diff_f[pl.ds(16 * m + q, 8), :] for m in range(reach)]
                odd = [rows_f[pl.ds(16 * m + 8 + q, 8), :] for m in range(reach)]
                next_even = [diff_f[pl.ds(16 * m + 8 + q, 8), :] for m in range(reach)]
                for a in range(half_steps):
                    t0 = tmpl[index, pl.ds(16 * a + q, 8, stride=0), :]
                    t1 = tmpl[index, pl.ds(16 * a + 8 + q, 8, stride=0), :]
                    both = pair[index, pl.ds(8 * a + q, 8, stride=0), :]
                    for b in range(half_blocks):
                        one[b] = one[b] + t0 * even[a + b]
                        two[b] = two[b] + both * odd[a + b]
                        three[b] = three[b] + t1 * next_even[a + b]
            return tuple(tuple(part) for part in lists)

        zero = jnp.zeros((8, LANES), jnp.float32)
        start = ((zero,) * half_blocks,) * 3 + ((zero,) * blocks,)
        one, two, three, window = lax.fori_loop(0, 4, conv, start)
        gain = gains[pl.ds(index, 8, stride=0), :]
        for b in range(blocks):
            product = one[b // 2] + two[b // 2] if b % 2 == 0 else two[b // 2] - three[b // 2]
            value = product * lax.rsqrt(window[b] / taps + 1e-06) * gain
            at = pl.multiple_of(i * shifts + 8 * b, 8)
            total[pl.ds(at, 8), :] = jnp.where(g == 0, value, total[pl.ds(at, 8), :] + value)
        return 0

    lax.fori_loop(0, n * groups, item, 0)
    stacked = lax.dot_general(
        jnp.ones((8, LANES), jnp.float32), total[...], (((1,), (1,)), ((), ())),
        precision=lax.Precision.HIGHEST, preferred_element_type=jnp.float32,
    )
    sub = lax.broadcasted_iota(jnp.int32, (n, shifts), 0)
    blk = lax.axis_index("blk")
    result = jnp.zeros((n, shifts), jnp.float32)
    for i in range(n):
        at = places[i][0] if places[i][1] else blk ^ places[i][0]
        result = jnp.where(sub == at, stacked[:1, i * shifts : (i + 1) * shifts], result)
    left, right = result[:, : shifts // 2], result[:, shifts // 2 :]
    keep_ref[...] = jnp.where(chan == 0, left, right)
    send_ref[...] = jnp.where(chan == 0, right, left)


def score(records, packed, places, taps, shifts):
    n = len(packed)
    samples, channels = records[0].shape
    width = packed[0].shape[1]
    groups = width // LANES
    items = n * groups
    padded = -(-samples // 8) * 8
    vmem = pl.BlockSpec(memory_space=pltpu.VMEM)
    out = jax.ShapeDtypeStruct((n, shifts // 2), jnp.float32)
    return pl.pallas_call(
        functools.partial(score_kernel, taps, shifts, places),
        out_shape=(out, out),
        in_specs=[vmem] * (2 + n),
        out_specs=(vmem, vmem),
        scratch_shapes=[
            pltpu.VMEM((items, taps + 8, LANES), jnp.float32),
            pltpu.VMEM((items, taps // 2 + 8, LANES), jnp.float32),
            pltpu.VMEM((-(-items // 8) * 8 + 8, LANES), jnp.float32),
            pltpu.VMEM((n, LANES), jnp.int32),
            pltpu.SMEM((n, LANES), jnp.int32),
            pltpu.VMEM((2, samples, LANES), records[0].dtype),
            pltpu.VMEM((padded, LANES), jnp.float32),
            pltpu.VMEM((padded, LANES), jnp.float32),
            pltpu.VMEM((shifts + 8, LANES), jnp.float32),
            pltpu.VMEM((n * shifts, LANES), jnp.float32),
            pltpu.SemaphoreType.DMA,
        ],
        compiler_params=pltpu.CompilerParams(vmem_limit_bytes=32 * 2**20),
        cost_estimate=pl.CostEstimate(
            flops=2 * n * width * taps * shifts, bytes_accessed=n * width * samples * 4, transcendentals=0
        ),
        name="score",
    )(*records, *packed)


def exchange(value, axis, size, mask):
    return lax.ppermute(value, axis, [(i, i ^ mask) for i in range(size)])


def on_device(mesh_shape, record, templates, offsets, counts):
    blk = mesh_shape["blk"]
    taps = templates.shape[2]
    shifts = record.shape[2] - taps + 1
    packed = pack(templates[0], offsets, counts)
    mine = jnp.transpose(record[0])
    packed, mine = lax.optimization_barrier((packed, mine))
    if blk == CHUNK:
        held = {0: packed}
        for mask in (4, 2, 1):
            held[mask] = exchange(packed, "blk", blk, mask)
        theirs = exchange(mine, "chan", 2, 1)
        held[6] = exchange(held[4], "blk", blk, 2)
        for mask in (4, 2, 6):
            held[mask + 1] = exchange(held[mask], "blk", blk, 1)
        keep, send = score(
            (mine, theirs), [held[m] for m in range(blk)], [(m, False) for m in range(blk)], taps, shifts
        )
    else:
        theirs = exchange(mine, "chan", 2, 1)
        every = lax.all_gather(packed, "blk", axis=0, tiled=False)
        keeps, sends = [], []
        for at in range(0, blk, CHUNK):
            size = min(CHUNK, blk - at)
            keep, send = score(
                (mine, theirs), [every[at + i] for i in range(size)],
                [(i, True) for i in range(size)], taps, shifts,
            )
            keeps.append(keep)
            sends.append(send)
        keep, send = jnp.concatenate(keeps, axis=0), jnp.concatenate(sends, axis=0)
    return (keep + exchange(send, "chan", 2, 1))[None]


def solution(mesh):
    in_specs = (P(("grp", "blk"), "chan", None), P("blk", "chan", None), P("blk"), P("blk"))
    out_specs = P(("grp", "blk"), None, "chan")
    return jax.shard_map(
        functools.partial(on_device, dict(mesh.shape)),
        mesh=mesh, in_specs=in_specs, out_specs=out_specs, check_vma=False,
    )
```

profile of v0, /device:TPU:0, one launch (start us, length us, event | category | flops | bytes accessed | tf_op | source)
XLA Modules:
  0.0 33.9 jit_solution(17796468587079031494)
XLA Ops:
  1.3 1.6 %pack.1.refs_2_ = bf16[144,256]{1,0:T(8,128)(2,1)} custom-call(s32[1]{0:T(128)S(6)} %copy.5.off_ref, s32[1]{0:T(128)S(6)} %copy.6.cnt_ref, bf16[256,128]{1,0:T(8,128)(2,1)} %bitcast.8), custom_call_target="tpu_custom_call" | custom-call | tf_op jit(solution)/shard_map/pack/pallas_call | solution.py:28
  2.9 0.5 %collective-permute-start = (bf16[191,5000]{1,0:T(8,128)(2,1)}, bf16[191,5000]{1,0:T(8,128)(2,1)S(1)}, u32[]{:S(2)}, u32[]{:S(2)}) collective-permute-start(bf16[191,5000]{1,0:T(8,128)(2,1)} %bitcast.6), channel_id=1, source_target_pairs={{0,1},{1,0},{2,3},{3,2},{4,5},{5,4},{6,7},{7,6},{8,9},{9,8},{10,11... | collective-permute-start | bytes 5730008 | tf_op jit(solution)/shard_map/ppermute | solution.py:227
  3.3 3.6 %collective-permute-start.4 = (bf16[144,256]{1,0:T(8,128)(2,1)}, bf16[144,256]{1,0:T(8,128)(2,1)S(1)}, u32[]{:S(2)}, u32[]{:S(2)}) collective-permute-start(bf16[144,256]{1,0:T(8,128)(2,1)} %pack.1.refs_2_), channel_id=1, source_target_pairs={{0,8},{2,10},{4,12},{6,14},{8,0},{10,2},{12,4},{14,6},{1,9},{3,11}... | collective-permute-start | bytes 221192 | tf_op jit(solution)/shard_map/ppermute | solution.py:227
  6.9 1.6 %collective-permute-start.2 = (bf16[144,256]{1,0:T(8,128)(2,1)}, bf16[144,256]{1,0:T(8,128)(2,1)S(1)}, u32[]{:S(2)}, u32[]{:S(2)}) collective-permute-start(bf16[144,256]{1,0:T(8,128)(2,1)} %pack.1.refs_2_), channel_id=1, source_target_pairs={{0,4},{2,6},{4,0},{6,2},{8,12},{10,14},{12,8},{14,10},{1,5},{3,7},... | collective-permute-start | bytes 221192 | tf_op jit(solution)/shard_map/ppermute | solution.py:227
  8.5 3.3 %collective-permute-done.4.refs_6_ = bf16[144,256]{1,0:T(8,128)(2,1)S(1)} collective-permute-done((bf16[144,256]{1,0:T(8,128)(2,1)}, bf16[144,256]{1,0:T(8,128)(2,1)S(1)}, u32[]{:S(2)}, u32[]{:S(2)}) %collective-permute-start.4) | collective-permute-done | bytes 73760 | tf_op jit(solution)/shard_map/ppermute | solution.py:227
  11.7 0.7 %collective-permute-start.6 = (bf16[144,256]{1,0:T(8,128)(2,1)S(1)}, bf16[144,256]{1,0:T(8,128)(2,1)S(1)}, u32[]{:S(2)}, u32[]{:S(2)}) collective-permute-start(bf16[144,256]{1,0:T(8,128)(2,1)S(1)} %collective-permute-done.4.refs_6_), channel_id=1, source_target_pairs={{0,4},{2,6},{4,0},{6,2},{8,12},{10,14},{12,8},{14,10},{1,5},{3,7},... | collective-permute-start | bytes 221192 | tf_op jit(solution)/shard_map/ppermute | solution.py:227
  12.5 1.5 %collective-permute-start.1 = (bf16[144,256]{1,0:T(8,128)(2,1)}, bf16[144,256]{1,0:T(8,128)(2,1)S(1)}, u32[]{:S(2)}, u32[]{:S(2)}) collective-permute-start(bf16[144,256]{1,0:T(8,128)(2,1)} %pack.1.refs_2_), channel_id=1, source_target_pairs={{0,2},{2,0},{4,6},{6,4},{8,10},{10,8},{12,14},{14,12},{1,3},{3,1},... | collective-permute-start | bytes 221192 | tf_op jit(solution)/shard_map/ppermute | solution.py:227
  14.0 0.5 %collective-permute-start.5 = (bf16[144,256]{1,0:T(8,128)(2,1)S(1)}, bf16[144,256]{1,0:T(8,128)(2,1)S(1)}, u32[]{:S(2)}, u32[]{:S(2)}) collective-permute-start(bf16[144,256]{1,0:T(8,128)(2,1)S(1)} %collective-permute-done.4.refs_6_), channel_id=1, source_target_pairs={{0,2},{2,0},{4,6},{6,4},{8,10},{10,8},{12,14},{14,12},{1,3},{3,1},... | collective-permute-start | bytes 221192 | tf_op jit(solution)/shard_map/ppermute | solution.py:227
  14.5 0.0 collective-permute-done.2.refs_4_
  14.5 1.5 %collective-permute-start.3 = (bf16[144,256]{1,0:T(8,128)(2,1)S(1)}, bf16[144,256]{1,0:T(8,128)(2,1)S(1)}, u32[]{:S(2)}, u32[]{:S(2)}) collective-permute-start(bf16[144,256]{1,0:T(8,128)(2,1)S(1)} %collective-permute-done.2.refs_4_), channel_id=1, source_target_pairs={{0,2},{2,0},{4,6},{6,4},{8,10},{10,8},{12,14},{14,12},{1,3},{3,1},... | collective-permute-start | bytes 221192 | tf_op jit(solution)/shard_map/ppermute | solution.py:227
  16.0 0.1 collective-permute-done.6.refs_8_
  16.1 1.5 %collective-permute-start.7 = (bf16[144,256]{1,0:T(8,128)(2,1)S(1)}, bf16[144,256]{1,0:T(8,128)(2,1)S(1)}, u32[]{:S(2)}, u32[]{:S(2)}) collective-permute-start(bf16[144,256]{1,0:T(8,128)(2,1)S(1)} %collective-permute-done.6.refs_8_), channel_id=1, source_target_pairs={{0,2},{2,0},{4,6},{6,4},{8,10},{10,8},{12,14},{14,12},{1,3},{3,1},... | collective-permute-start | bytes 221192 | tf_op jit(solution)/shard_map/ppermute | solution.py:227
  17.6 0.2 collective-permute-done.1.refs_3_
  17.8 1.6 %collective-permute-done.5.refs_7_ = bf16[144,256]{1,0:T(8,128)(2,1)S(1)} collective-permute-done((bf16[144,256]{1,0:T(8,128)(2,1)S(1)}, bf16[144,256]{1,0:T(8,128)(2,1)S(1)}, u32[]{:S(2)}, u32[]{:S(2)}) %collective-permute-start.5) | collective-permute-done | bytes 73760 | tf_op jit(solution)/shard_map/ppermute | solution.py:227
  19.4 1.4 %collective-permute-done.3.refs_5_ = bf16[144,256]{1,0:T(8,128)(2,1)S(1)} collective-permute-done((bf16[144,256]{1,0:T(8,128)(2,1)S(1)}, bf16[144,256]{1,0:T(8,128)(2,1)S(1)}, u32[]{:S(2)}, u32[]{:S(2)}) %collective-permute-start.3) | collective-permute-done | bytes 73760 | tf_op jit(solution)/shard_map/ppermute | solution.py:227
  20.8 0.8 %collective-permute-done.7.refs_9_ = bf16[144,256]{1,0:T(8,128)(2,1)S(1)} collective-permute-done((bf16[144,256]{1,0:T(8,128)(2,1)S(1)}, bf16[144,256]{1,0:T(8,128)(2,1)S(1)}, u32[]{:S(2)}, u32[]{:S(2)}) %collective-permute-start.7) | collective-permute-done | bytes 73760 | tf_op jit(solution)/shard_map/ppermute | solution.py:227
  21.6 0.0 collective-permute-done.refs_1_
  21.6 0.0 copy-start
  21.6 1.5 %copy-done = bf16[1,5000,191]{1,2,0:T(8,128)(2,1)S(1)} copy-done((bf16[1,5000,191]{1,2,0:T(8,128)(2,1)S(1)}, bf16[1,5000,191]{1,2,0:T(8,128)(2,1)}, u32[]{:S(2)}) %copy-start) | copy-done | bytes 1910024
  23.1 0.0 copy-start.1
  23.1 0.9 %copy-done.1 = bf16[144,256]{1,0:T(8,128)(2,1)S(1)} copy-done((bf16[144,256]{1,0:T(8,128)(2,1)S(1)}, bf16[144,256]{1,0:T(8,128)(2,1)}, u32[]{:S(2)}) %copy-start.1) | copy-done | bytes 73752
  24.0 8.1 %score.1 = (f32[8,32]{1,0:T(8,128)S(1)}, f32[8,32]{1,0:T(8,128)S(1)}) custom-call(bf16[191,5000]{1,0:T(8,128)(2,1)S(1)} %bitcast.7, bf16[191,5000]{1,0:T(8,128)(2,1)S(1)} %collective-permute-done.refs_1_, bf16[144,256]{1,0:T(8,128)(2,1)S(1)} %copy-done.1, bf16[144,256]{1,0:T(8,128)(2,1)S(1)} %collective-permute-done.1.refs_3_, ...), custom_call_target="tpu_custom_call" | custom-call | flops 33554432 | bytes 1564672 | tf_op jit(solution)/shard_map/score/pallas_call | solution.py:200
  32.1 0.1 collective-permute-start.8
  32.2 1.2 %collective-permute-done.8 = f32[8,32]{1,0:T(8,128)S(1)} collective-permute-done((f32[8,32]{1,0:T(8,128)S(1)}, f32[8,32]{1,0:T(8,128)S(1)}, u32[]{:S(2)}, u32[]{:S(2)}) %collective-permute-start.8) | collective-permute-done | bytes 1056 | tf_op jit(solution)/shard_map/ppermute | solution.py:227
  33.3 0.6 %add_bitcast_fusion = f32[1,8,32]{2,1,0:T(8,128)} fusion(f32[8,32]{1,0:T(8,128)S(1)} %get-tuple-element.11, f32[8,32]{1,0:T(8,128)S(1)} %collective-permute-done.8), kind=kLoop, calls=%fused_computation | loop fusion | flops 256 | bytes 3072 | tf_op jit(solution)/shard_map/broadcast_in_dim | solution.py:261
Async XLA Ops:
  2.9 18.7 %collective-permute-start = (bf16[191,5000]{1,0:T(8,128)(2,1)}, bf16[191,5000]{1,0:T(8,128)(2,1)S(1)}, u32[]{:S(2)}, u32[]{:S(2)}) collective-permute-start(bf16[191,5000]{1,0:T(8,128)(2,1)} %bitcast.6), channel_id=1, source_target_pairs={{0,1},{1,0},{2,3},{3,2},{4,5},{5,4},{6,7},{7,6},{8,9},{9,8},{10,11... | collective-permute-start | bytes 5730008 | tf_op jit(solution)/shard_map/ppermute | solution.py:227
  3.3 8.4 %collective-permute-start.4 = (bf16[144,256]{1,0:T(8,128)(2,1)}, bf16[144,256]{1,0:T(8,128)(2,1)S(1)}, u32[]{:S(2)}, u32[]{:S(2)}) collective-permute-start(bf16[144,256]{1,0:T(8,128)(2,1)} %pack.1.refs_2_), channel_id=1, source_target_pairs={{0,8},{2,10},{4,12},{6,14},{8,0},{10,2},{12,4},{14,6},{1,9},{3,11}... | collective-permute-start | bytes 221192 | tf_op jit(solution)/shard_map/ppermute | solution.py:227
  6.9 7.6 %collective-permute-start.2 = (bf16[144,256]{1,0:T(8,128)(2,1)}, bf16[144,256]{1,0:T(8,128)(2,1)S(1)}, u32[]{:S(2)}, u32[]{:S(2)}) collective-permute-start(bf16[144,256]{1,0:T(8,128)(2,1)} %pack.1.refs_2_), channel_id=1, source_target_pairs={{0,4},{2,6},{4,0},{6,2},{8,12},{10,14},{12,8},{14,10},{1,5},{3,7},... | collective-permute-start | bytes 221192 | tf_op jit(solution)/shard_map/ppermute | solution.py:227
  11.7 4.4 %collective-permute-start.6 = (bf16[144,256]{1,0:T(8,128)(2,1)S(1)}, bf16[144,256]{1,0:T(8,128)(2,1)S(1)}, u32[]{:S(2)}, u32[]{:S(2)}) collective-permute-start(bf16[144,256]{1,0:T(8,128)(2,1)S(1)} %collective-permute-done.4.refs_6_), channel_id=1, source_target_pairs={{0,4},{2,6},{4,0},{6,2},{8,12},{10,14},{12,8},{14,10},{1,5},{3,7},... | collective-permute-start | bytes 221192 | tf_op jit(solution)/shard_map/ppermute | solution.py:227
  12.5 5.4 %collective-permute-start.1 = (bf16[144,256]{1,0:T(8,128)(2,1)}, bf16[144,256]{1,0:T(8,128)(2,1)S(1)}, u32[]{:S(2)}, u32[]{:S(2)}) collective-permute-start(bf16[144,256]{1,0:T(8,128)(2,1)} %pack.1.refs_2_), channel_id=1, source_target_pairs={{0,2},{2,0},{4,6},{6,4},{8,10},{10,8},{12,14},{14,12},{1,3},{3,1},... | collective-permute-start | bytes 221192 | tf_op jit(solution)/shard_map/ppermute | solution.py:227
  14.0 5.4 %collective-permute-start.5 = (bf16[144,256]{1,0:T(8,128)(2,1)S(1)}, bf16[144,256]{1,0:T(8,128)(2,1)S(1)}, u32[]{:S(2)}, u32[]{:S(2)}) collective-permute-start(bf16[144,256]{1,0:T(8,128)(2,1)S(1)} %collective-permute-done.4.refs_6_), channel_id=1, source_target_pairs={{0,2},{2,0},{4,6},{6,4},{8,10},{10,8},{12,14},{14,12},{1,3},{3,1},... | collective-permute-start | bytes 221192 | tf_op jit(solution)/shard_map/ppermute | solution.py:227
  14.5 6.3 %collective-permute-start.3 = (bf16[144,256]{1,0:T(8,128)(2,1)S(1)}, bf16[144,256]{1,0:T(8,128)(2,1)S(1)}, u32[]{:S(2)}, u32[]{:S(2)}) collective-permute-start(bf16[144,256]{1,0:T(8,128)(2,1)S(1)} %collective-permute-done.2.refs_4_), channel_id=1, source_target_pairs={{0,2},{2,0},{4,6},{6,4},{8,10},{10,8},{12,14},{14,12},{1,3},{3,1},... | collective-permute-start | bytes 221192 | tf_op jit(solution)/shard_map/ppermute | solution.py:227
  16.1 5.5 %collective-permute-start.7 = (bf16[144,256]{1,0:T(8,128)(2,1)S(1)}, bf16[144,256]{1,0:T(8,128)(2,1)S(1)}, u32[]{:S(2)}, u32[]{:S(2)}) collective-permute-start(bf16[144,256]{1,0:T(8,128)(2,1)S(1)} %collective-permute-done.6.refs_8_), channel_id=1, source_target_pairs={{0,2},{2,0},{4,6},{6,4},{8,10},{10,8},{12,14},{14,12},{1,3},{3,1},... | collective-permute-start | bytes 221192 | tf_op jit(solution)/shard_map/ppermute | solution.py:227
  21.6 1.5 %copy-start = (bf16[1,5000,191]{1,2,0:T(8,128)(2,1)S(1)}, bf16[1,5000,191]{1,2,0:T(8,128)(2,1)}, u32[]{:S(2)}) copy-start(bf16[1,5000,191]{1,2,0:T(8,128)(2,1)} %param.4) | copy-start | bytes 5730004
  23.1 0.9 %copy-start.1 = (bf16[144,256]{1,0:T(8,128)(2,1)S(1)}, bf16[144,256]{1,0:T(8,128)(2,1)}, u32[]{:S(2)}) copy-start(bf16[144,256]{1,0:T(8,128)(2,1)} %pack.1.refs_2_) | copy-start | bytes 221188
  32.1 1.2 %collective-permute-start.8 = (f32[8,32]{1,0:T(8,128)S(1)}, f32[8,32]{1,0:T(8,128)S(1)}, u32[]{:S(2)}, u32[]{:S(2)}) collective-permute-start(f32[8,32]{1,0:T(8,128)S(1)} %get-tuple-element.12), channel_id=1, source_target_pairs={{0,1},{1,0},{2,3},{3,2},{4,5},{5,4},{6,7},{7,6},{8,9},{9,8},{10,11... | collective-permute-start | bytes 3080 | tf_op jit(solution)/shard_map/ppermute | solution.py:227
where the time goes:
time: 34.2 us; the launch traced here: 33.9 us
  starting transfers between devices  11.5 us (34%)
  Pallas kernels  9.63 us (28%)
  waiting for transfers between devices  8.48 us (25%)
  local copies, waits for them, and re-layouts  2.43 us (7%)
  between operations  1.32 us (4%)
  other arithmetic  0.6 us (2%)
    ppermute x9, starting transfers between devices, exchange(): return lax.ppermute(value, axis, [(i, i ^ mask) for i in range(size)])  11.5 us
    ppermute x9, waiting for transfers between devices, exchange(): return lax.ppermute(value, axis, [(i, i ^ mask) for i in range(size)])  8.48 us
    pallas_call x1, Pallas kernels, score(): pl.pallas_call(functools.partial(score_kernel, taps, shifts, places), out...  8.05 us
    unnamed x4, local copies, waits for them, and re-layouts  2.43 us
    pallas_call x1, Pallas kernels, pack(): pl.pallas_call(pack_kernel, out_shape=jax.ShapeDtypeStruct((taps + META,...  1.57 us
  transfers between devices with their start and end apart: 9, of which 7 were waited for; matrix products, arithmetic and copies ran while one was open for 0% of the time, Pallas kernels for 0%

commit v1 on v0

--- a/solution.py
+++ b/solution.py
@@ -12,37 +12,44 @@
 CHUNK = 8
 
 
-def pack_kernel(off_ref, cnt_ref, tmpl_ref, out_ref):
+def pack_kernel(off_ref, cnt_ref, tmpl_ref, out_ref, own_ref):
     rows, taps = tmpl_ref.shape
-    out_ref[:taps, :] = jnp.transpose(tmpl_ref[...].astype(jnp.float32)).astype(out_ref.dtype)
+    turned = jnp.transpose(tmpl_ref[...].astype(jnp.float32)).astype(out_ref.dtype)
+    out_ref[:taps, :] = turned
+    own_ref[:taps, :] = turned
     lane = lax.broadcasted_iota(jnp.int32, (META, rows), 1)
     off, cnt = off_ref[0], cnt_ref[0]
     level = lax.broadcasted_iota(jnp.int32, (META, rows), 0)
     value = jnp.where(lane == 0, off, cnt)
     meta = jnp.where(level == 0, value >> 8, value & 255)
-    out_ref[taps:, :] = meta.astype(jnp.float32).astype(out_ref.dtype)
+    meta = meta.astype(jnp.float32).astype(out_ref.dtype)
+    out_ref[taps:, :] = meta
+    own_ref[taps:, :] = meta
 
 
 def pack(templates, offsets, counts):
     rows, taps = templates.shape
     return pl.pallas_call(
         pack_kernel,
-        out_shape=jax.ShapeDtypeStruct((taps + META, rows), templates.dtype),
+        out_shape=(jax.ShapeDtypeStruct((taps + META, rows), templates.dtype),) * 2,
         in_specs=[
             pl.BlockSpec(memory_space=pltpu.SMEM),
             pl.BlockSpec(memory_space=pltpu.SMEM),
             pl.BlockSpec(memory_space=pltpu.VMEM),
         ],
-        out_specs=pl.BlockSpec(memory_space=pltpu.VMEM),
+        out_specs=(pl.BlockSpec(memory_space=pltpu.VMEM),) * 2,
+        cost_estimate=pl.CostEstimate(flops=4 * 10**9, bytes_accessed=10**7, transcendentals=0),
         name="pack",
     )(offsets, counts, templates)
 
 
-def score_kernel(taps, shifts, places, *refs):
+def score_kernel(taps, shifts, places, more, last, *refs):
     n = len(places)
     mine, theirs = refs[:2]
     packed = refs[2 : 2 + n]
-    keep_ref, send_ref, tmpl, pair, gains, ints_v, ints, tails, rows_f, diff_f, sums, total, sem = refs[2 + n :]
+    at = 2 + n + more
+    prev_ref, outs = refs[2 + n : at], refs[at : at + 1 + last]
+    tmpl, pair, gains, ints_v, ints, tails, rows_f, diff_f, sums, total, sem = refs[at + 1 + last :]
     samples, channels = mine.shape
     width = packed[0].shape[1]
     groups = width // LANES
@@ -141,29 +148,25 @@
         half_blocks, half_steps = blocks // 2, steps // 2
         reach = half_blocks + half_steps - 1
 
-        def conv(twice, carry):
-            lists = [list(part) for part in carry]
-            one, two, three, window = lists
-            for extra in range(2):
-                q = 2 * twice + extra
-                for b in range(blocks):
-                    window[b] = window[b] + sums[pl.ds(8 * b + q, 8), :]
-                even = [diff_f[pl.ds(16 * m + q, 8), :] for m in range(reach)]
-                odd = [rows_f[pl.ds(16 * m + 8 + q, 8), :] for m in range(reach)]
-                next_even = [diff_f[pl.ds(16 * m + 8 + q, 8), :] for m in range(reach)]
-                for a in range(half_steps):
-                    t0 = tmpl[index, pl.ds(16 * a + q, 8, stride=0), :]
-                    t1 = tmpl[index, pl.ds(16 * a + 8 + q, 8, stride=0), :]
-                    both = pair[index, pl.ds(8 * a + q, 8, stride=0), :]
-                    for b in range(half_blocks):
-                        one[b] = one[b] + t0 * even[a + b]
-                        two[b] = two[b] + both * odd[a + b]
-                        three[b] = three[b] + t1 * next_even[a + b]
-            return tuple(tuple(part) for part in lists)
-
         zero = jnp.zeros((8, LANES), jnp.float32)
-        start = ((zero,) * half_blocks,) * 3 + ((zero,) * blocks,)
-        one, two, three, window = lax.fori_loop(0, 4, conv, start)
+        one, two, three = ([zero] * half_blocks for _ in range(3))
+        window = [zero] * blocks
+        origin = index >> 16
+        for q in range(8):
+            row = origin + q
+            for b in range(blocks):
+                window[b] = window[b] + sums[pl.ds(8 * b + row, 8), :]
+            even = [diff_f[pl.ds(16 * m + row, 8), :] for m in range(reach)]
+            odd = [rows_f[pl.ds(16 * m + 8 + row, 8), :] for m in range(reach)]
+            next_even = [diff_f[pl.ds(16 * m + 8 + row, 8), :] for m in range(reach)]
+            for a in range(half_steps):
+                t0 = tmpl[index, pl.ds(16 * a + row, 8, stride=0), :]
+                t1 = tmpl[index, pl.ds(16 * a + 8 + row, 8, stride=0), :]
+                both = pair[index, pl.ds(8 * a + row, 8, stride=0), :]
+                for b in range(half_blocks):
+                    one[b] = one[b] + t0 * even[a + b]
+                    two[b] = two[b] + both * odd[a + b]
+                    three[b] = three[b] + t1 * next_even[a + b]
         gain = gains[pl.ds(index, 8, stride=0), :]
         for b in range(blocks):
             product = one[b // 2] + two[b // 2] if b % 2 == 0 else two[b // 2] - three[b // 2]
@@ -173,22 +176,30 @@
         return 0
 
     lax.fori_loop(0, n * groups, item, 0)
-    stacked = lax.dot_general(
-        jnp.ones((8, LANES), jnp.float32), total[...], (((1,), (1,)), ((), ())),
-        precision=lax.Precision.HIGHEST, preferred_element_type=jnp.float32,
-    )
-    sub = lax.broadcasted_iota(jnp.int32, (n, shifts), 0)
+    rest_f = total[...]
+    stacked = jnp.zeros((8, n * shifts), jnp.float32)
+    for _ in range(3):
+        term = rest_f.astype(jnp.bfloat16)
+        rest_f = rest_f - term.astype(jnp.float32)
+        stacked = stacked + lax.dot_general(
+            jnp.ones((8, LANES), jnp.bfloat16), term, (((1,), (1,)), ((), ())),
+            preferred_element_type=jnp.float32,
+        )
+    result = prev_ref[0][...] if more else jnp.zeros(outs[0].shape[:1] + (shifts,), jnp.float32)
+    sub = lax.broadcasted_iota(jnp.int32, result.shape, 0)
     blk = lax.axis_index("blk")
-    result = jnp.zeros((n, shifts), jnp.float32)
-    for i in range(n):
-        at = places[i][0] if places[i][1] else blk ^ places[i][0]
-        result = jnp.where(sub == at, stacked[:1, i * shifts : (i + 1) * shifts], result)
+    for i in range(n):
+        row = places[i][0] if places[i][1] else blk ^ places[i][0]
+        result = jnp.where(sub == row, stacked[:1, i * shifts : (i + 1) * shifts], result)
+    if not last:
+        outs[0][...] = result
+        return
     left, right = result[:, : shifts // 2], result[:, shifts // 2 :]
-    keep_ref[...] = jnp.where(chan == 0, left, right)
-    send_ref[...] = jnp.where(chan == 0, right, left)
-
-
-def score(records, packed, places, taps, shifts):
+    outs[0][...] = jnp.where(chan == 0, left, right)
+    outs[1][...] = jnp.where(chan == 0, right, left)
+
+
+def score(records, packed, places, templates, taps, shifts, prev=(), last=True):
     n = len(packed)
     samples, channels = records[0].shape
     width = packed[0].shape[1]
@@ -196,12 +207,15 @@
     items = n * groups
     padded = -(-samples // 8) * 8
     vmem = pl.BlockSpec(memory_space=pltpu.VMEM)
-    out = jax.ShapeDtypeStruct((n, shifts // 2), jnp.float32)
+    if last:
+        out_shape = (jax.ShapeDtypeStruct((templates, shifts // 2), jnp.float32),) * 2
+    else:
+        out_shape = (jax.ShapeDtypeStruct((templates, shifts), jnp.float32),)
     return pl.pallas_call(
-        functools.partial(score_kernel, taps, shifts, places),
-        out_shape=(out, out),
-        in_specs=[vmem] * (2 + n),
-        out_specs=(vmem, vmem),
+        functools.partial(score_kernel, taps, shifts, places, len(prev), int(last)),
+        out_shape=out_shape,
+        in_specs=[vmem] * (2 + n + len(prev)),
+        out_specs=(vmem,) * len(out_shape),
         scratch_shapes=[
             pltpu.VMEM((items, taps + 8, LANES), jnp.float32),
             pltpu.VMEM((items, taps // 2 + 8, LANES), jnp.float32),
@@ -220,7 +234,7 @@
             flops=2 * n * width * taps * shifts, bytes_accessed=n * width * samples * 4, transcendentals=0
         ),
         name="score",
-    )(*records, *packed)
+    )(*records, *packed, *prev)
 
 
 def exchange(value, axis, size, mask):
@@ -231,20 +245,25 @@
     blk = mesh_shape["blk"]
     taps = templates.shape[2]
     shifts = record.shape[2] - taps + 1
-    packed = pack(templates[0], offsets, counts)
+    packed, own = pack(templates[0], offsets, counts)
     mine = jnp.transpose(record[0])
     packed, mine = lax.optimization_barrier((packed, mine))
     if blk == CHUNK:
-        held = {0: packed}
-        for mask in (4, 2, 1):
+        held = {0: own}
+        for mask in (4, 1, 2):
             held[mask] = exchange(packed, "blk", blk, mask)
         theirs = exchange(mine, "chan", 2, 1)
+        held[3] = exchange(held[1], "blk", blk, 2)
         held[6] = exchange(held[4], "blk", blk, 2)
-        for mask in (4, 2, 6):
-            held[mask + 1] = exchange(held[mask], "blk", blk, 1)
-        keep, send = score(
-            (mine, theirs), [held[m] for m in range(blk)], [(m, False) for m in range(blk)], taps, shifts
-        )
+        held[5] = exchange(held[4], "blk", blk, 1)
+        held[7] = exchange(held[6], "blk", blk, 1)
+        rows = ()
+        for masks, last in (((0, 1, 2, 4), False), ((3, 5, 6, 7), True)):
+            rows = score(
+                (mine, theirs), [held[m] for m in masks], [(m, False) for m in masks],
+                blk, taps, shifts, rows, last,
+            )
+        keep, send = rows
     else:
         theirs = exchange(mine, "chan", 2, 1)
         every = lax.all_gather(packed, "blk", axis=0, tiled=False)
@@ -253,7 +272,7 @@
             size = min(CHUNK, blk - at)
             keep, send = score(
                 (mine, theirs), [every[at + i] for i in range(size)],
-                [(i, True) for i in range(size)], taps, shifts,
+                [(i, True) for i in range(size)], size, taps, shifts,
             )
             keeps.append(keep)
             sends.append(send)

time: 34.2 us -> 29.6 us (0.87)
  waiting for transfers between devices: 8.48 us -> 5.01 us
  local copies, waits for them, and re-layouts: 2.43 us -> 0.89 us
    ppermute x9, waiting for transfers between devices: 8.48 us -> 5.01 us  [exchange(): return lax.ppermute(value, axis, [(i, i ^ mask) for i in range(size)])]
    unnamed x4, local copies, waits for them, and re-layouts: 2.43 us -> 0.89 us
    pallas_call x2 -> x3, Pallas kernels: 9.63 us -> 9.83 us  [the longest x2 8.08 us: score(): pl.pallas_call(functools.partial(score_kernel, taps, shifts, places, len(...]
  transfers between devices with their start and end apart: 9 -> 9, of which waited for: 7 -> 3; matrix products, arithmetic and copies ran while one was open for 0% -> 0% of each run, Pallas kernels for 0% -> 14%
where the time goes in v1:
time: 29.6 us; the launch traced here: 29.4 us
  starting transfers between devices  11.7 us (40%)
  Pallas kernels  9.83 us (33%)
  waiting for transfers between devices  5.01 us (17%)
  between operations  1.36 us (5%)
  local copies, waits for them, and re-layouts  0.89 us (3%)
  other arithmetic  0.6 us (2%)
    ppermute x9, starting transfers between devices, exchange(): return lax.ppermute(value, axis, [(i, i ^ mask) for i in range(size)])  11.7 us
    pallas_call x2, Pallas kernels, score(): pl.pallas_call(functools.partial(score_kernel, taps, shifts, places, len(...  8.08 us
    ppermute x9, waiting for transfers between devices, exchange(): return lax.ppermute(value, axis, [(i, i ^ mask) for i in range(size)])  5.01 us
    pallas_call x1, Pallas kernels, pack(): pl.pallas_call(pack_kernel, out_shape=(jax.ShapeDtypeStruct((taps + META,...  1.74 us
    unnamed x4, local copies, waits for them, and re-layouts  0.89 us
    broadcast_in_dim x1, other arithmetic, on_device(): return (keep + exchange(send, 'chan', 2, 1))[None]  0.6 us
  transfers between devices with their start and end apart: 9, of which 3 were waited for; matrix products, arithmetic and copies ran while one was open for 0% of the time, Pallas kernels for 14%

profile of v1, /device:TPU:0, one launch (start us, length us, event | category | flops | bytes accessed | tf_op | source)
XLA Modules:
  0.0 29.4 jit_solution(17629767582314684258)
XLA Ops:
  1.3 0.0 copy-start
  1.3 1.7 %pack.1 = (bf16[144,256]{1,0:T(8,128)(2,1)}, bf16[144,256]{1,0:T(8,128)(2,1)}) custom-call(s32[1]{0:T(128)S(6)} %copy.5.off_ref, s32[1]{0:T(128)S(6)} %copy.6.cnt_ref, bf16[256,128]{1,0:T(8,128)(2,1)} %bitcast.9), custom_call_target="tpu_custom_call" | custom-call | flops 4000000000 | bytes 10000000 | tf_op jit(solution)/shard_map/pack/pallas_call | solution.py:32
  3.1 0.0 copy-done
  3.1 0.5 %collective-permute-start = (bf16[191,5000]{1,0:T(8,128)(2,1)S(1)}, bf16[191,5000]{1,0:T(8,128)(2,1)S(1)}, u32[]{:S(2)}, u32[]{:S(2)}) collective-permute-start(bf16[191,5000]{1,0:T(8,128)(2,1)S(1)} %bitcast.6), channel_id=1, source_target_pairs={{0,1},{1,0},{2,3},{3,2},{4,5},{5,4},{6,7},{7,6},{8,9},{9,8},{10,11... | collective-permute-start | bytes 5730008 | tf_op jit(solution)/shard_map/ppermute | solution.py:241
  3.5 3.6 %collective-permute-start.3 = (bf16[144,256]{1,0:T(8,128)(2,1)}, bf16[144,256]{1,0:T(8,128)(2,1)S(1)}, u32[]{:S(2)}, u32[]{:S(2)}) collective-permute-start(bf16[144,256]{1,0:T(8,128)(2,1)} %get-tuple-element.13), channel_id=1, source_target_pairs={{0,8},{2,10},{4,12},{6,14},{8,0},{10,2},{12,4},{14,6},{1,9},{3,11}... | collective-permute-start | bytes 221192 | tf_op jit(solution)/shard_map/ppermute | solution.py:241
  7.1 1.5 %collective-permute-start.1 = (bf16[144,256]{1,0:T(8,128)(2,1)}, bf16[144,256]{1,0:T(8,128)(2,1)S(1)}, u32[]{:S(2)}, u32[]{:S(2)}) collective-permute-start(bf16[144,256]{1,0:T(8,128)(2,1)} %get-tuple-element.13), channel_id=1, source_target_pairs={{0,2},{2,0},{4,6},{6,4},{8,10},{10,8},{12,14},{14,12},{1,3},{3,1},... | collective-permute-start | bytes 221192 | tf_op jit(solution)/shard_map/ppermute | solution.py:241
  8.6 3.2 %collective-permute-done.3.refs_5_ = bf16[144,256]{1,0:T(8,128)(2,1)S(1)} collective-permute-done((bf16[144,256]{1,0:T(8,128)(2,1)}, bf16[144,256]{1,0:T(8,128)(2,1)S(1)}, u32[]{:S(2)}, u32[]{:S(2)}) %collective-permute-start.3) | collective-permute-done | bytes 73760 | tf_op jit(solution)/shard_map/ppermute | solution.py:241
  11.8 0.8 %collective-permute-start.5 = (bf16[144,256]{1,0:T(8,128)(2,1)S(1)}, bf16[144,256]{1,0:T(8,128)(2,1)S(1)}, u32[]{:S(2)}, u32[]{:S(2)}) collective-permute-start(bf16[144,256]{1,0:T(8,128)(2,1)S(1)} %collective-permute-done.3.refs_5_), channel_id=1, source_target_pairs={{0,4},{2,6},{4,0},{6,2},{8,12},{10,14},{12,8},{14,10},{1,5},{3,7},... | collective-permute-start | bytes 221192 | tf_op jit(solution)/shard_map/ppermute | solution.py:241
  12.7 1.2 %collective-permute-start.7 = (bf16[144,256]{1,0:T(8,128)(2,1)}, bf16[144,256]{1,0:T(8,128)(2,1)S(1)}, u32[]{:S(2)}, u32[]{:S(2)}) collective-permute-start(bf16[144,256]{1,0:T(8,128)(2,1)} %get-tuple-element.13), channel_id=1, source_target_pairs={{0,4},{2,6},{4,0},{6,2},{8,12},{10,14},{12,8},{14,10},{1,5},{3,7},... | collective-permute-start | bytes 221192 | tf_op jit(solution)/shard_map/ppermute | solution.py:241
  13.8 1.5 %collective-permute-start.4 = (bf16[144,256]{1,0:T(8,128)(2,1)S(1)}, bf16[144,256]{1,0:T(8,128)(2,1)S(1)}, u32[]{:S(2)}, u32[]{:S(2)}) collective-permute-start(bf16[144,256]{1,0:T(8,128)(2,1)S(1)} %collective-permute-done.3.refs_5_), channel_id=1, source_target_pairs={{0,2},{2,0},{4,6},{6,4},{8,10},{10,8},{12,14},{14,12},{1,3},{3,1},... | collective-permute-start | bytes 221192 | tf_op jit(solution)/shard_map/ppermute | solution.py:241
  15.4 0.0 collective-permute-done.1.refs_3_
  15.4 0.8 %collective-permute-start.2 = (bf16[144,256]{1,0:T(8,128)(2,1)S(1)}, bf16[144,256]{1,0:T(8,128)(2,1)S(1)}, u32[]{:S(2)}, u32[]{:S(2)}) collective-permute-start(bf16[144,256]{1,0:T(8,128)(2,1)S(1)} %collective-permute-done.1.refs_3_), channel_id=1, source_target_pairs={{0,4},{2,6},{4,0},{6,2},{8,12},{10,14},{12,8},{14,10},{1,5},{3,7},... | collective-permute-start | bytes 221192 | tf_op jit(solution)/shard_map/ppermute | solution.py:241
  16.2 0.6 %collective-permute-done.5.refs_4_ = bf16[144,256]{1,0:T(8,128)(2,1)S(1)} collective-permute-done((bf16[144,256]{1,0:T(8,128)(2,1)S(1)}, bf16[144,256]{1,0:T(8,128)(2,1)S(1)}, u32[]{:S(2)}, u32[]{:S(2)}) %collective-permute-start.5) | collective-permute-done | bytes 73760 | tf_op jit(solution)/shard_map/ppermute | solution.py:241
  16.8 1.7 %collective-permute-start.6 = (bf16[144,256]{1,0:T(8,128)(2,1)S(1)}, bf16[144,256]{1,0:T(8,128)(2,1)S(1)}, u32[]{:S(2)}, u32[]{:S(2)}) collective-permute-start(bf16[144,256]{1,0:T(8,128)(2,1)S(1)} %collective-permute-done.5.refs_4_), channel_id=1, source_target_pairs={{0,2},{2,0},{4,6},{6,4},{8,10},{10,8},{12,14},{14,12},{1,3},{3,1},... | collective-permute-start | bytes 221192 | tf_op jit(solution)/shard_map/ppermute | solution.py:241
  18.5 0.0 collective-permute-done.7.refs_4_
  18.5 0.0 collective-permute-done.refs_1_
  18.5 0.0 copy-start.1
  18.5 0.9 %copy-done.1 = bf16[144,256]{1,0:T(8,128)(2,1)S(1)} copy-done((bf16[144,256]{1,0:T(8,128)(2,1)S(1)}, bf16[144,256]{1,0:T(8,128)(2,1)}, u32[]{:S(2)}) %copy-start.1) | copy-done | bytes 73752
  19.4 4.0 %score.2.refs_6_ = f32[8,64]{1,0:T(8,128)S(1)} custom-call(bf16[191,5000]{1,0:T(8,128)(2,1)S(1)} %bitcast.7, bf16[191,5000]{1,0:T(8,128)(2,1)S(1)} %collective-permute-done.refs_1_, bf16[144,256]{1,0:T(8,128)(2,1)S(1)} %copy-done.1, bf16[144,256]{1,0:T(8,128)(2,1)S(1)} %collective-permute-done.1.refs_3_, ...), custom_call_target="tpu_custom_call" | custom-call | flops 16777216 | bytes 782336 | tf_op jit(solution)/shard_map/score/pallas_call | solution.py:214
  23.4 0.0 collective-permute-done.4.refs_3_
  23.4 0.0 collective-permute-done.2.refs_2_
  23.4 0.0 collective-permute-done.6.refs_5_
  23.4 4.1 %score.3 = (f32[8,32]{1,0:T(8,128)S(1)}, f32[8,32]{1,0:T(8,128)S(1)}) custom-call(bf16[191,5000]{1,0:T(8,128)(2,1)S(1)} %bitcast.8, bf16[191,5000]{1,0:T(8,128)(2,1)S(1)} %collective-permute-done.refs_1_, bf16[144,256]{1,0:T(8,128)(2,1)S(1)} %collective-permute-done.2.refs_2_, bf16[144,256]{1,0:T(8,128)(2,1)S(1)} %collective-permute-done.4.refs_3_, ...), custom_call_target="tpu_custom_call" | custom-call | flops 16777216 | bytes 782336 | tf_op jit(solution)/shard_map/score/pallas_call | solution.py:214
  27.5 0.1 collective-permute-start.8
  27.6 1.2 %collective-permute-done.8 = f32[8,32]{1,0:T(8,128)S(1)} collective-permute-done((f32[8,32]{1,0:T(8,128)S(1)}, f32[8,32]{1,0:T(8,128)S(1)}, u32[]{:S(2)}, u32[]{:S(2)}) %collective-permute-start.8) | collective-permute-done | bytes 1056 | tf_op jit(solution)/shard_map/ppermute | solution.py:241
  28.8 0.6 %add_bitcast_fusion = f32[1,8,32]{2,1,0:T(8,128)} fusion(f32[8,32]{1,0:T(8,128)S(1)} %get-tuple-element.15, f32[8,32]{1,0:T(8,128)S(1)} %collective-permute-done.8), kind=kLoop, calls=%fused_computation | loop fusion | flops 256 | bytes 3072 | tf_op jit(solution)/shard_map/broadcast_in_dim | solution.py:280
Async XLA Ops:
  1.3 1.8 %copy-start = (bf16[1,5000,191]{1,2,0:T(8,128)(2,1)S(1)}, bf16[1,5000,191]{1,2,0:T(8,128)(2,1)}, u32[]{:S(2)}) copy-start(bf16[1,5000,191]{1,2,0:T(8,128)(2,1)} %param.4) | copy-start | bytes 5730004
  3.1 15.5 %collective-permute-start = (bf16[191,5000]{1,0:T(8,128)(2,1)S(1)}, bf16[191,5000]{1,0:T(8,128)(2,1)S(1)}, u32[]{:S(2)}, u32[]{:S(2)}) collective-permute-start(bf16[191,5000]{1,0:T(8,128)(2,1)S(1)} %bitcast.6), channel_id=1, source_target_pairs={{0,1},{1,0},{2,3},{3,2},{4,5},{5,4},{6,7},{7,6},{8,9},{9,8},{10,11... | collective-permute-start | bytes 5730008 | tf_op jit(solution)/shard_map/ppermute | solution.py:241
  3.5 8.3 %collective-permute-start.3 = (bf16[144,256]{1,0:T(8,128)(2,1)}, bf16[144,256]{1,0:T(8,128)(2,1)S(1)}, u32[]{:S(2)}, u32[]{:S(2)}) collective-permute-start(bf16[144,256]{1,0:T(8,128)(2,1)} %get-tuple-element.13), channel_id=1, source_target_pairs={{0,8},{2,10},{4,12},{6,14},{8,0},{10,2},{12,4},{14,6},{1,9},{3,11}... | collective-permute-start | bytes 221192 | tf_op jit(solution)/shard_map/ppermute | solution.py:241
  7.1 8.3 %collective-permute-start.1 = (bf16[144,256]{1,0:T(8,128)(2,1)}, bf16[144,256]{1,0:T(8,128)(2,1)S(1)}, u32[]{:S(2)}, u32[]{:S(2)}) collective-permute-start(bf16[144,256]{1,0:T(8,128)(2,1)} %get-tuple-element.13), channel_id=1, source_target_pairs={{0,2},{2,0},{4,6},{6,4},{8,10},{10,8},{12,14},{14,12},{1,3},{3,1},... | collective-permute-start | bytes 221192 | tf_op jit(solution)/shard_map/ppermute | solution.py:241
  11.8 5.0 %collective-permute-start.5 = (bf16[144,256]{1,0:T(8,128)(2,1)S(1)}, bf16[144,256]{1,0:T(8,128)(2,1)S(1)}, u32[]{:S(2)}, u32[]{:S(2)}) collective-permute-start(bf16[144,256]{1,0:T(8,128)(2,1)S(1)} %collective-permute-done.3.refs_5_), channel_id=1, source_target_pairs={{0,4},{2,6},{4,0},{6,2},{8,12},{10,14},{12,8},{14,10},{1,5},{3,7},... | collective-permute-start | bytes 221192 | tf_op jit(solution)/shard_map/ppermute | solution.py:241
  12.7 5.9 %collective-permute-start.7 = (bf16[144,256]{1,0:T(8,128)(2,1)}, bf16[144,256]{1,0:T(8,128)(2,1)S(1)}, u32[]{:S(2)}, u32[]{:S(2)}) collective-permute-start(bf16[144,256]{1,0:T(8,128)(2,1)} %get-tuple-element.13), channel_id=1, source_target_pairs={{0,4},{2,6},{4,0},{6,2},{8,12},{10,14},{12,8},{14,10},{1,5},{3,7},... | collective-permute-start | bytes 221192 | tf_op jit(solution)/shard_map/ppermute | solution.py:241
  13.8 9.6 %collective-permute-start.4 = (bf16[144,256]{1,0:T(8,128)(2,1)S(1)}, bf16[144,256]{1,0:T(8,128)(2,1)S(1)}, u32[]{:S(2)}, u32[]{:S(2)}) collective-permute-start(bf16[144,256]{1,0:T(8,128)(2,1)S(1)} %collective-permute-done.3.refs_5_), channel_id=1, source_target_pairs={{0,2},{2,0},{4,6},{6,4},{8,10},{10,8},{12,14},{14,12},{1,3},{3,1},... | collective-permute-start | bytes 221192 | tf_op jit(solution)/shard_map/ppermute | solution.py:241
  15.4 8.0 %collective-permute-start.2 = (bf16[144,256]{1,0:T(8,128)(2,1)S(1)}, bf16[144,256]{1,0:T(8,128)(2,1)S(1)}, u32[]{:S(2)}, u32[]{:S(2)}) collective-permute-start(bf16[144,256]{1,0:T(8,128)(2,1)S(1)} %collective-permute-done.1.refs_3_), channel_id=1, source_target_pairs={{0,4},{2,6},{4,0},{6,2},{8,12},{10,14},{12,8},{14,10},{1,5},{3,7},... | collective-permute-start | bytes 221192 | tf_op jit(solution)/shard_map/ppermute | solution.py:241
  16.8 6.6 %collective-permute-start.6 = (bf16[144,256]{1,0:T(8,128)(2,1)S(1)}, bf16[144,256]{1,0:T(8,128)(2,1)S(1)}, u32[]{:S(2)}, u32[]{:S(2)}) collective-permute-start(bf16[144,256]{1,0:T(8,128)(2,1)S(1)} %collective-permute-done.5.refs_4_), channel_id=1, source_target_pairs={{0,2},{2,0},{4,6},{6,4},{8,10},{10,8},{12,14},{14,12},{1,3},{3,1},... | collective-permute-start | bytes 221192 | tf_op jit(solution)/shard_map/ppermute | solution.py:241
  18.5 0.9 %copy-start.1 = (bf16[144,256]{1,0:T(8,128)(2,1)S(1)}, bf16[144,256]{1,0:T(8,128)(2,1)}, u32[]{:S(2)}) copy-start(bf16[144,256]{1,0:T(8,128)(2,1)} %get-tuple-element.14.refs_2_) | copy-start | bytes 221188
  27.5 1.2 %collective-permute-start.8 = (f32[8,32]{1,0:T(8,128)S(1)}, f32[8,32]{1,0:T(8,128)S(1)}, u32[]{:S(2)}, u32[]{:S(2)}) collective-permute-start(f32[8,32]{1,0:T(8,128)S(1)} %get-tuple-element.16), channel_id=1, source_target_pairs={{0,1},{1,0},{2,3},{3,2},{4,5},{5,4},{6,7},{7,6},{8,9},{9,8},{10,11... | collective-permute-start | bytes 3080 | tf_op jit(solution)/shard_map/ppermute | solution.py:241

commit v2 on v1

--- a/solution.py
+++ b/solution.py
@@ -10,6 +10,7 @@
 LANES = 128
 META = 16
 CHUNK = 8
+PITCH = 9
 
 
 def pack_kernel(off_ref, cnt_ref, tmpl_ref, out_ref, own_ref):
@@ -39,6 +40,7 @@
         ],
         out_specs=(pl.BlockSpec(memory_space=pltpu.VMEM),) * 2,
         cost_estimate=pl.CostEstimate(flops=4 * 10**9, bytes_accessed=10**7, transcendentals=0),
+        compiler_params=pltpu.CompilerParams(vmem_limit_bytes=4 * 2**20),
         name="pack",
     )(offsets, counts, templates)
 
@@ -49,7 +51,7 @@
     packed = refs[2 : 2 + n]
     at = 2 + n + more
     prev_ref, outs = refs[2 + n : at], refs[at : at + 1 + last]
-    tmpl, pair, gains, ints_v, ints, tails, rows_f, diff_f, sums, total, sem = refs[at + 1 + last :]
+    tmpl, gains, ints_v, ints, tails, rows_f, pitched, sums, total, sem = refs[at + 1 + last :]
     samples, channels = mine.shape
     width = packed[0].shape[1]
     groups = width // LANES
@@ -72,7 +74,6 @@
             tiles = [block[8 * a : 8 * a + 8] for a in range(steps)]
             energy = jnp.zeros((8, LANES), jnp.float32)
             for a in range(0, steps, 2):
-                pair[i * groups + g, 4 * a : 4 * a + 8, :] = tiles[a] + tiles[a + 1]
                 energy = energy + (tiles[a] * tiles[a] + tiles[a + 1] * tiles[a + 1])
             gains[i * groups + g : i * groups + g + 1, :] = jnp.sum(energy, axis=0, keepdims=True)
     if rest:
@@ -134,49 +135,65 @@
                 sides.append(turned(found[0], found[1], turn))
             rows_f[:samples, :] = jnp.where(wide < split, sides[0], sides[1])
 
+        origin = index >> 16
         held = [rows_f[8 * m : 8 * m + 8, :] for m in range(steps + blocks)]
-        for m in range(steps + blocks - 1):
-            diff_f[8 * m : 8 * m + 8, :] = held[m] - held[m + 1]
+        for m in range(steps + blocks):
+            pitched[pl.ds(origin + PITCH * m, 8), :] = held[m]
+
         level = [v * v for v in held]
         span = 1
         while span < steps:
             level = [level[m] + level[m + span] for m in range(len(level) - span)]
             span *= 2
         for m in range(blocks + 1):
-            sums[8 * m : 8 * m + 8, :] = level[m]
-
-        half_blocks, half_steps = blocks // 2, steps // 2
-        reach = half_blocks + half_steps - 1
+            sums[pl.ds(origin + PITCH * m, 8), :] = level[m]
+
+        def spread(ref, m):
+            return ref[pl.ds(m + m // 8, 8, stride=PITCH), :]
+
+        near = [spread(sums, m) for m in range(15)]
+        before, after = [near[7]], [near[8]]
+        for m in range(1, 8):
+            before.append(before[-1] + near[7 - m])
+        for m in range(1, 7):
+            after.append(after[-1] + near[8 + m])
+        window = [before[7]] + [before[7 - b] + after[b - 1] for b in range(1, 8)]
 
         zero = jnp.zeros((8, LANES), jnp.float32)
-        one, two, three = ([zero] * half_blocks for _ in range(3))
-        window = [zero] * blocks
-        origin = index >> 16
-        for q in range(8):
-            row = origin + q
-            for b in range(blocks):
-                window[b] = window[b] + sums[pl.ds(8 * b + row, 8), :]
-            even = [diff_f[pl.ds(16 * m + row, 8), :] for m in range(reach)]
-            odd = [rows_f[pl.ds(16 * m + 8 + row, 8), :] for m in range(reach)]
-            next_even = [diff_f[pl.ds(16 * m + 8 + row, 8), :] for m in range(reach)]
-            for a in range(half_steps):
-                t0 = tmpl[index, pl.ds(16 * a + row, 8, stride=0), :]
-                t1 = tmpl[index, pl.ds(16 * a + 8 + row, 8, stride=0), :]
-                both = pair[index, pl.ds(8 * a + row, 8, stride=0), :]
-                for b in range(half_blocks):
-                    one[b] = one[b] + t0 * even[a + b]
-                    two[b] = two[b] + both * odd[a + b]
-                    three[b] = three[b] + t1 * next_even[a + b]
+        one, two, three = ([zero] * 4 for _ in range(3))
+        data = [spread(pitched, m) for m in range(7)]
+        even = [data[2 * m] - data[2 * m + 1] for m in range(3)]
+        odd = [data[2 * m + 1] for m in range(3)]
+        next_even = [data[2 * m + 1] - data[2 * m + 2] for m in range(3)]
+        current = data[6]
+        for a in range(taps // 2):
+            middle, following = spread(pitched, 2 * a + 7), spread(pitched, 2 * a + 8)
+            even.append(current - middle)
+            odd.append(middle)
+            next_even.append(middle - following)
+            current = following
+            t0 = tmpl[index, pl.ds(2 * a, 8, stride=0), :]
+            t1 = tmpl[index, pl.ds(2 * a + 1, 8, stride=0), :]
+            both = t0 + t1
+            for b in range(4):
+                one[b] = one[b] + t0 * even[a + b]
+                two[b] = two[b] + both * odd[a + b]
+                three[b] = three[b] + t1 * next_even[a + b]
         gain = gains[pl.ds(index, 8, stride=0), :]
-        for b in range(blocks):
+        for b in range(8):
             product = one[b // 2] + two[b // 2] if b % 2 == 0 else two[b // 2] - three[b // 2]
             value = product * lax.rsqrt(window[b] / taps + 1e-06) * gain
-            at = pl.multiple_of(i * shifts + 8 * b, 8)
-            total[pl.ds(at, 8), :] = jnp.where(g == 0, value, total[pl.ds(at, 8), :] + value)
+            total[pl.ds((i * groups + g) * shifts + b, 8, stride=8), :] = value
         return 0
 
     lax.fori_loop(0, n * groups, item, 0)
-    rest_f = total[...]
+    rest_f = jnp.concatenate(
+        [
+            sum(total[(i * groups + g) * shifts : (i * groups + g + 1) * shifts, :] for g in range(groups))
+            for i in range(n)
+        ],
+        axis=0,
+    )
     stacked = jnp.zeros((8, n * shifts), jnp.float32)
     for _ in range(3):
         term = rest_f.astype(jnp.bfloat16)
@@ -218,15 +235,14 @@
         out_specs=(vmem,) * len(out_shape),
         scratch_shapes=[
             pltpu.VMEM((items, taps + 8, LANES), jnp.float32),
-            pltpu.VMEM((items, taps // 2 + 8, LANES), jnp.float32),
             pltpu.VMEM((-(-items // 8) * 8 + 8, LANES), jnp.float32),
             pltpu.VMEM((n, LANES), jnp.int32),
             pltpu.SMEM((n, LANES), jnp.int32),
             pltpu.VMEM((2, samples, LANES), records[0].dtype),
             pltpu.VMEM((padded, LANES), jnp.float32),
-            pltpu.VMEM((padded, LANES), jnp.float32),
-            pltpu.VMEM((shifts + 8, LANES), jnp.float32),
-            pltpu.VMEM((n * shifts, LANES), jnp.float32),
+            pltpu.VMEM((padded // 8 * PITCH + 8, LANES), jnp.float32),
+            pltpu.VMEM(((shifts // 8 + 2) * PITCH, LANES), jnp.float32),
+            pltpu.VMEM((items * shifts + 8, LANES), jnp.float32),
             pltpu.SemaphoreType.DMA,
         ],
         compiler_params=pltpu.CompilerParams(vmem_limit_bytes=32 * 2**20),
@@ -253,6 +269,8 @@
         for mask in (4, 1, 2):
             held[mask] = exchange(packed, "blk", blk, mask)
         theirs = exchange(mine, "chan", 2, 1)
+        near = lax.optimization_barrier((held[4], held[1], held[2]))
+        held[4], held[1], held[2] = near
         held[3] = exchange(held[1], "blk", blk, 2)
         held[6] = exchange(held[4], "blk", blk, 2)
         held[5] = exchange(held[4], "blk", blk, 1)

time: 29.6 us -> 29.9 us (1.010)
  local copies, waits for them, and re-layouts: 0.89 us -> 2.27 us
  Pallas kernels: 9.83 us -> 8.49 us
  waiting for transfers between devices: 5.01 us -> 6.04 us
  starting transfers between devices: 11.7 us -> 11 us
    pallas_call x1, Pallas kernels: 1.74 us -> 0.1 us  [pack(): pl.pallas_call(pack_kernel, out_shape=(jax.ShapeDtypeStruct((taps + META,...]
    unnamed x4, local copies, waits for them, and re-layouts: 0.89 us -> 2.27 us
    ppermute x9, waiting for transfers between devices: 5.01 us -> 6.04 us  [exchange(): return lax.ppermute(value, axis, [(i, i ^ mask) for i in range(size)])]
    ppermute x9, starting transfers between devices: 11.7 us -> 11 us  [exchange(): return lax.ppermute(value, axis, [(i, i ^ mask) for i in range(size)])]
    pallas_call x2, Pallas kernels: 8.08 us -> 8.39 us  [score(): pl.pallas_call(functools.partial(score_kernel, taps, shifts, places, len(...]
  transfers between devices with their start and end apart: 9 -> 9, of which waited for: 3 -> 4; matrix products, arithmetic and copies ran while one was open for 0% -> 0% of each run, Pallas kernels for 14% -> 14%
where the time goes in v2:
time: 29.9 us; the launch traced here: 29.8 us
  starting transfers between devices  11 us (37%)
  Pallas kernels  8.49 us (28%)
  waiting for transfers between devices  6.04 us (20%)
  local copies, waits for them, and re-layouts  2.27 us (8%)
  between operations  1.37 us (5%)
  other arithmetic  0.6 us (2%)
    ppermute x9, starting transfers between devices, exchange(): return lax.ppermute(value, axis, [(i, i ^ mask) for i in range(size)])  11 us
    pallas_call x2, Pallas kernels, score(): pl.pallas_call(functools.partial(score_kernel, taps, shifts, places, len(...  8.39 us
    ppermute x9, waiting for transfers between devices, exchange(): return lax.ppermute(value, axis, [(i, i ^ mask) for i in range(size)])  6.04 us
    unnamed x4, local copies, waits for them, and re-layouts  2.27 us
  transfers between devices with their start and end apart: 9, of which 4 were waited for; matrix products, arithmetic and copies ran while one was open for 0% of the time, Pallas kernels for 14%

profile of v2, /device:TPU:0, one launch (start us, length us, event | category | flops | bytes accessed | tf_op | source)
XLA Modules:
  0.0 29.8 jit_solution(8793334681823270501)
XLA Ops:
  1.3 0.0 copy-start.1
  1.3 0.8 %copy-done.1 = bf16[1,256,128]{2,1,0:T(8,128)(2,1)S(1)} copy-done((bf16[1,256,128]{2,1,0:T(8,128)(2,1)S(1)}, bf16[1,256,128]{2,1,0:T(8,128)(2,1)}, u32[]{:S(2)}) %copy-start.1) | copy-done | bytes 65560
  2.1 0.0 copy-start
  2.1 0.1 pack.1
  2.2 1.4 %copy-done = bf16[1,5000,191]{1,2,0:T(8,128)(2,1)S(1)} copy-done((bf16[1,5000,191]{1,2,0:T(8,128)(2,1)S(1)}, bf16[1,5000,191]{1,2,0:T(8,128)(2,1)}, u32[]{:S(2)}) %copy-start) | copy-done | bytes 1910024
  3.7 0.5 %collective-permute-start = (bf16[191,5000]{1,0:T(8,128)(2,1)S(1)}, bf16[191,5000]{1,0:T(8,128)(2,1)S(1)}, u32[]{:S(2)}, u32[]{:S(2)}) collective-permute-start(bf16[191,5000]{1,0:T(8,128)(2,1)S(1)} %bitcast.6), channel_id=1, source_target_pairs={{0,1},{1,0},{2,3},{3,2},{4,5},{5,4},{6,7},{7,6},{8,9},{9,8},{10,11... | collective-permute-start | bytes 5730008 | tf_op jit(solution)/shard_map/ppermute | solution.py:257
  4.1 3.6 %collective-permute-start.1 = (bf16[144,256]{1,0:T(8,128)(2,1)S(1)}, bf16[144,256]{1,0:T(8,128)(2,1)S(1)}, u32[]{:S(2)}, u32[]{:S(2)}) collective-permute-start(bf16[144,256]{1,0:T(8,128)(2,1)S(1)} %get-tuple-element.16), channel_id=1, source_target_pairs={{0,8},{2,10},{4,12},{6,14},{8,0},{10,2},{12,4},{14,6},{1,9},{3,11}... | collective-permute-start | bytes 221192 | tf_op jit(solution)/shard_map/ppermute | solution.py:257
  7.7 1.5 %collective-permute-start.2 = (bf16[144,256]{1,0:T(8,128)(2,1)S(1)}, bf16[144,256]{1,0:T(8,128)(2,1)S(1)}, u32[]{:S(2)}, u32[]{:S(2)}) collective-permute-start(bf16[144,256]{1,0:T(8,128)(2,1)S(1)} %get-tuple-element.16), channel_id=1, source_target_pairs={{0,2},{2,0},{4,6},{6,4},{8,10},{10,8},{12,14},{14,12},{1,3},{3,1},... | collective-permute-start | bytes 221192 | tf_op jit(solution)/shard_map/ppermute | solution.py:257
  9.2 1.6 %collective-permute-start.3 = (bf16[144,256]{1,0:T(8,128)(2,1)S(1)}, bf16[144,256]{1,0:T(8,128)(2,1)S(1)}, u32[]{:S(2)}, u32[]{:S(2)}) collective-permute-start(bf16[144,256]{1,0:T(8,128)(2,1)S(1)} %get-tuple-element.16), channel_id=1, source_target_pairs={{0,4},{2,6},{4,0},{6,2},{8,12},{10,14},{12,8},{14,10},{1,5},{3,7},... | collective-permute-start | bytes 221192 | tf_op jit(solution)/shard_map/ppermute | solution.py:257
  10.8 1.6 %collective-permute-done.1.refs_5_ = bf16[144,256]{1,0:T(8,128)(2,1)S(1)} collective-permute-done((bf16[144,256]{1,0:T(8,128)(2,1)S(1)}, bf16[144,256]{1,0:T(8,128)(2,1)S(1)}, u32[]{:S(2)}, u32[]{:S(2)}) %collective-permute-start.1) | collective-permute-done | bytes 73760 | tf_op jit(solution)/shard_map/ppermute | solution.py:257
  12.3 0.0 collective-permute-done.2.refs_3_
  12.3 1.3 %collective-permute-done.3.refs_4_ = bf16[144,256]{1,0:T(8,128)(2,1)S(1)} collective-permute-done((bf16[144,256]{1,0:T(8,128)(2,1)S(1)}, bf16[144,256]{1,0:T(8,128)(2,1)S(1)}, u32[]{:S(2)}, u32[]{:S(2)}) %collective-permute-start.3) | collective-permute-done | bytes 73760 | tf_op jit(solution)/shard_map/ppermute | solution.py:257
  13.7 1.5 %collective-permute-start.6 = (bf16[144,256]{1,0:T(8,128)(2,1)S(1)}, bf16[144,256]{1,0:T(8,128)(2,1)S(1)}, u32[]{:S(2)}, u32[]{:S(2)}) collective-permute-start(bf16[144,256]{1,0:T(8,128)(2,1)S(1)} %collective-permute-done.1.refs_5_), channel_id=1, source_target_pairs={{0,4},{2,6},{4,0},{6,2},{8,12},{10,14},{12,8},{14,10},{1,5},{3,7},... | collective-permute-start | bytes 221192 | tf_op jit(solution)/shard_map/ppermute | solution.py:257
  15.1 0.5 %collective-permute-start.5 = (bf16[144,256]{1,0:T(8,128)(2,1)S(1)}, bf16[144,256]{1,0:T(8,128)(2,1)S(1)}, u32[]{:S(2)}, u32[]{:S(2)}) collective-permute-start(bf16[144,256]{1,0:T(8,128)(2,1)S(1)} %collective-permute-done.1.refs_5_), channel_id=1, source_target_pairs={{0,2},{2,0},{4,6},{6,4},{8,10},{10,8},{12,14},{14,12},{1,3},{3,1},... | collective-permute-start | bytes 221192 | tf_op jit(solution)/shard_map/ppermute | solution.py:257
  15.7 0.8 %collective-permute-start.4 = (bf16[144,256]{1,0:T(8,128)(2,1)S(1)}, bf16[144,256]{1,0:T(8,128)(2,1)S(1)}, u32[]{:S(2)}, u32[]{:S(2)}) collective-permute-start(bf16[144,256]{1,0:T(8,128)(2,1)S(1)} %collective-permute-done.2.refs_3_), channel_id=1, source_target_pairs={{0,4},{2,6},{4,0},{6,2},{8,12},{10,14},{12,8},{14,10},{1,5},{3,7},... | collective-permute-start | bytes 221192 | tf_op jit(solution)/shard_map/ppermute | solution.py:257
  16.4 2.0 %collective-permute-done.6.refs_4_ = bf16[144,256]{1,0:T(8,128)(2,1)S(1)} collective-permute-done((bf16[144,256]{1,0:T(8,128)(2,1)S(1)}, bf16[144,256]{1,0:T(8,128)(2,1)S(1)}, u32[]{:S(2)}, u32[]{:S(2)}) %collective-permute-start.6) | collective-permute-done | bytes 73760 | tf_op jit(solution)/shard_map/ppermute | solution.py:257
  18.4 1.1 %collective-permute-start.7 = (bf16[144,256]{1,0:T(8,128)(2,1)S(1)}, bf16[144,256]{1,0:T(8,128)(2,1)S(1)}, u32[]{:S(2)}, u32[]{:S(2)}) collective-permute-start(bf16[144,256]{1,0:T(8,128)(2,1)S(1)} %collective-permute-done.6.refs_4_), channel_id=1, source_target_pairs={{0,2},{2,0},{4,6},{6,4},{8,10},{10,8},{12,14},{14,12},{1,3},{3,1},... | collective-permute-start | bytes 221192 | tf_op jit(solution)/shard_map/ppermute | solution.py:257
  19.5 0.0 collective-permute-done.refs_1_
  19.5 4.1 %score.2.refs_6_ = f32[8,64]{1,0:T(8,128)S(1)} custom-call(bf16[191,5000]{1,0:T(8,128)(2,1)S(1)} %bitcast.7, bf16[191,5000]{1,0:T(8,128)(2,1)S(1)} %collective-permute-done.refs_1_, bf16[144,256]{1,0:T(8,128)(2,1)S(1)} %get-tuple-element.19.refs_2_, bf16[144,256]{1,0:T(8,128)(2,1)S(1)} %collective-permute-done.2.refs_3_, ...), custom_call_target="tpu_custom_call" | custom-call | flops 16777216 | bytes 782336 | tf_op jit(solution)/shard_map/score/pallas_call | solution.py:231
  23.6 0.0 collective-permute-done.5.refs_3_
  23.6 0.0 collective-permute-done.4.refs_2_
  23.7 0.0 collective-permute-done.7.refs_5_
  23.7 4.3 %score.3 = (f32[8,32]{1,0:T(8,128)S(1)}, f32[8,32]{1,0:T(8,128)S(1)}) custom-call(bf16[191,5000]{1,0:T(8,128)(2,1)S(1)} %bitcast.8, bf16[191,5000]{1,0:T(8,128)(2,1)S(1)} %collective-permute-done.refs_1_, bf16[144,256]{1,0:T(8,128)(2,1)S(1)} %collective-permute-done.4.refs_2_, bf16[144,256]{1,0:T(8,128)(2,1)S(1)} %collective-permute-done.5.refs_3_, ...), custom_call_target="tpu_custom_call" | custom-call | flops 16777216 | bytes 782336 | tf_op jit(solution)/shard_map/score/pallas_call | solution.py:231
  28.0 0.1 collective-permute-start.8
  28.0 1.2 %collective-permute-done.8 = f32[8,32]{1,0:T(8,128)S(1)} collective-permute-done((f32[8,32]{1,0:T(8,128)S(1)}, f32[8,32]{1,0:T(8,128)S(1)}, u32[]{:S(2)}, u32[]{:S(2)}) %collective-permute-start.8) | collective-permute-done | bytes 1056 | tf_op jit(solution)/shard_map/ppermute | solution.py:257
  29.2 0.6 %add_bitcast_fusion = f32[1,8,32]{2,1,0:T(8,128)} fusion(f32[8,32]{1,0:T(8,128)S(1)} %get-tuple-element.21, f32[8,32]{1,0:T(8,128)S(1)} %collective-permute-done.8), kind=kLoop, calls=%fused_computation | loop fusion | flops 256 | bytes 3072 | tf_op jit(solution)/shard_map/broadcast_in_dim | solution.py:298
Async XLA Ops:
  1.3 0.8 %copy-start.1 = (bf16[1,256,128]{2,1,0:T(8,128)(2,1)S(1)}, bf16[1,256,128]{2,1,0:T(8,128)(2,1)}, u32[]{:S(2)}) copy-start(bf16[1,256,128]{2,1,0:T(8,128)(2,1)} %param.5) | copy-start | bytes 196612
  2.1 1.5 %copy-start = (bf16[1,5000,191]{1,2,0:T(8,128)(2,1)S(1)}, bf16[1,5000,191]{1,2,0:T(8,128)(2,1)}, u32[]{:S(2)}) copy-start(bf16[1,5000,191]{1,2,0:T(8,128)(2,1)} %param.4) | copy-start | bytes 5730004
  3.7 15.8 %collective-permute-start = (bf16[191,5000]{1,0:T(8,128)(2,1)S(1)}, bf16[191,5000]{1,0:T(8,128)(2,1)S(1)}, u32[]{:S(2)}, u32[]{:S(2)}) collective-permute-start(bf16[191,5000]{1,0:T(8,128)(2,1)S(1)} %bitcast.6), channel_id=1, source_target_pairs={{0,1},{1,0},{2,3},{3,2},{4,5},{5,4},{6,7},{7,6},{8,9},{9,8},{10,11... | collective-permute-start | bytes 5730008 | tf_op jit(solution)/shard_map/ppermute | solution.py:257
  4.1 8.2 %collective-permute-start.1 = (bf16[144,256]{1,0:T(8,128)(2,1)S(1)}, bf16[144,256]{1,0:T(8,128)(2,1)S(1)}, u32[]{:S(2)}, u32[]{:S(2)}) collective-permute-start(bf16[144,256]{1,0:T(8,128)(2,1)S(1)} %get-tuple-element.16), channel_id=1, source_target_pairs={{0,8},{2,10},{4,12},{6,14},{8,0},{10,2},{12,4},{14,6},{1,9},{3,11}... | collective-permute-start | bytes 221192 | tf_op jit(solution)/shard_map/ppermute | solution.py:257
  7.7 4.6 %collective-permute-start.2 = (bf16[144,256]{1,0:T(8,128)(2,1)S(1)}, bf16[144,256]{1,0:T(8,128)(2,1)S(1)}, u32[]{:S(2)}, u32[]{:S(2)}) collective-permute-start(bf16[144,256]{1,0:T(8,128)(2,1)S(1)} %get-tuple-element.16), channel_id=1, source_target_pairs={{0,2},{2,0},{4,6},{6,4},{8,10},{10,8},{12,14},{14,12},{1,3},{3,1},... | collective-permute-start | bytes 221192 | tf_op jit(solution)/shard_map/ppermute | solution.py:257
  9.2 4.5 %collective-permute-start.3 = (bf16[144,256]{1,0:T(8,128)(2,1)S(1)}, bf16[144,256]{1,0:T(8,128)(2,1)S(1)}, u32[]{:S(2)}, u32[]{:S(2)}) collective-permute-start(bf16[144,256]{1,0:T(8,128)(2,1)S(1)} %get-tuple-element.16), channel_id=1, source_target_pairs={{0,4},{2,6},{4,0},{6,2},{8,12},{10,14},{12,8},{14,10},{1,5},{3,7},... | collective-permute-start | bytes 221192 | tf_op jit(solution)/shard_map/ppermute | solution.py:257
  13.7 4.7 %collective-permute-start.6 = (bf16[144,256]{1,0:T(8,128)(2,1)S(1)}, bf16[144,256]{1,0:T(8,128)(2,1)S(1)}, u32[]{:S(2)}, u32[]{:S(2)}) collective-permute-start(bf16[144,256]{1,0:T(8,128)(2,1)S(1)} %collective-permute-done.1.refs_5_), channel_id=1, source_target_pairs={{0,4},{2,6},{4,0},{6,2},{8,12},{10,14},{12,8},{14,10},{1,5},{3,7},... | collective-permute-start | bytes 221192 | tf_op jit(solution)/shard_map/ppermute | solution.py:257
  15.1 8.5 %collective-permute-start.5 = (bf16[144,256]{1,0:T(8,128)(2,1)S(1)}, bf16[144,256]{1,0:T(8,128)(2,1)S(1)}, u32[]{:S(2)}, u32[]{:S(2)}) collective-permute-start(bf16[144,256]{1,0:T(8,128)(2,1)S(1)} %collective-permute-done.1.refs_5_), channel_id=1, source_target_pairs={{0,2},{2,0},{4,6},{6,4},{8,10},{10,8},{12,14},{14,12},{1,3},{3,1},... | collective-permute-start | bytes 221192 | tf_op jit(solution)/shard_map/ppermute | solution.py:257
  15.7 8.0 %collective-permute-start.4 = (bf16[144,256]{1,0:T(8,128)(2,1)S(1)}, bf16[144,256]{1,0:T(8,128)(2,1)S(1)}, u32[]{:S(2)}, u32[]{:S(2)}) collective-permute-start(bf16[144,256]{1,0:T(8,128)(2,1)S(1)} %collective-permute-done.2.refs_3_), channel_id=1, source_target_pairs={{0,4},{2,6},{4,0},{6,2},{8,12},{10,14},{12,8},{14,10},{1,5},{3,7},... | collective-permute-start | bytes 221192 | tf_op jit(solution)/shard_map/ppermute | solution.py:257
  18.4 5.2 %collective-permute-start.7 = (bf16[144,256]{1,0:T(8,128)(2,1)S(1)}, bf16[144,256]{1,0:T(8,128)(2,1)S(1)}, u32[]{:S(2)}, u32[]{:S(2)}) collective-permute-start(bf16[144,256]{1,0:T(8,128)(2,1)S(1)} %collective-permute-done.6.refs_4_), channel_id=1, source_target_pairs={{0,2},{2,0},{4,6},{6,4},{8,10},{10,8},{12,14},{14,12},{1,3},{3,1},... | collective-permute-start | bytes 221192 | tf_op jit(solution)/shard_map/ppermute | solution.py:257
  28.0 1.2 %collective-permute-start.8 = (f32[8,32]{1,0:T(8,128)S(1)}, f32[8,32]{1,0:T(8,128)S(1)}, u32[]{:S(2)}, u32[]{:S(2)}) collective-permute-start(f32[8,32]{1,0:T(8,128)S(1)} %get-tuple-element.22), channel_id=1, source_target_pairs={{0,1},{1,0},{2,3},{3,2},{4,5},{5,4},{6,7},{7,6},{8,9},{9,8},{10,11... | collective-permute-start | bytes 3080 | tf_op jit(solution)/shard_map/ppermute | solution.py:257

commit v3 on v2

--- a/solution.py
+++ b/solution.py
@@ -2,6 +2,7 @@
 
 import jax
 import jax.numpy as jnp
+import numpy as np
 from jax import lax
 from jax.experimental import pallas as pl
 from jax.experimental.pallas import tpu as pltpu
@@ -45,13 +46,32 @@
     )(offsets, counts, templates)
 
 
+def three_terms(value):
+    terms = []
+    for _ in range(3):
+        terms.append(value.astype(jnp.bfloat16))
+        value = value - terms[-1].astype(jnp.float32)
+    return terms
+
+
+def fourier_tables(period, shifts):
+    bins = -(-(period // 2 + 1) // 8) * 8
+    k = np.arange(bins)[:, None]
+    used = k <= period // 2
+    angle = 2 * np.pi * k * np.arange(period)[None, :] / period
+    forward = np.concatenate([np.cos(angle) * used, np.sin(angle) * used], axis=0)
+    weight = np.where((k == 0) | (k == period // 2), 1.0, 2.0) / period
+    inverse = np.concatenate([forward[:bins] * weight, -forward[bins:] * weight], axis=0)
+    return forward.astype(np.float32), inverse[:, :shifts].T.astype(np.float32)
+
+
 def score_kernel(taps, shifts, places, more, last, *refs):
     n = len(places)
-    mine, theirs = refs[:2]
-    packed = refs[2 : 2 + n]
-    at = 2 + n + more
-    prev_ref, outs = refs[2 + n : at], refs[at : at + 1 + last]
-    tmpl, gains, ints_v, ints, tails, rows_f, pitched, sums, total, sem = refs[at + 1 + last :]
+    mine, theirs, forward, inverse = refs[:4]
+    packed = refs[4 : 4 + n]
+    at = 4 + n + more
+    prev_ref, outs = refs[4 + n : at], refs[at : at + 1 + last]
+    gains, ints_v, ints, tails, rows_f, rows_b, sums, scales, sem = refs[at + 1 + last :]
     samples, channels = mine.shape
     width = packed[0].shape[1]
     groups = width // LANES
@@ -70,7 +90,6 @@
     for i in range(n):
         for g in range(groups):
             block = packed[i][:taps, g * LANES : (g + 1) * LANES].astype(jnp.float32)
-            tmpl[i * groups + g, :taps, :] = block
             tiles = [block[8 * a : 8 * a + 8] for a in range(steps)]
             energy = jnp.zeros((8, LANES), jnp.float32)
             for a in range(0, steps, 2):
@@ -135,73 +154,67 @@
                 sides.append(turned(found[0], found[1], turn))
             rows_f[:samples, :] = jnp.where(wide < split, sides[0], sides[1])
 
+        rows_b[i, :, pl.ds(pl.multiple_of(g * LANES, LANES), LANES)] = rows_f[...].astype(jnp.bfloat16)
+
         origin = index >> 16
-        held = [rows_f[8 * m : 8 * m + 8, :] for m in range(steps + blocks)]
-        for m in range(steps + blocks):
-            pitched[pl.ds(origin + PITCH * m, 8), :] = held[m]
-
-        level = [v * v for v in held]
+        level = [rows_f[8 * m : 8 * m + 8, :] for m in range(steps + blocks)]
+        level = [v * v for v in level]
         span = 1
         while span < steps:
             level = [level[m] + level[m + span] for m in range(len(level) - span)]
             span *= 2
         for m in range(blocks + 1):
             sums[pl.ds(origin + PITCH * m, 8), :] = level[m]
-
-        def spread(ref, m):
-            return ref[pl.ds(m + m // 8, 8, stride=PITCH), :]
-
-        near = [spread(sums, m) for m in range(15)]
+        near = [sums[pl.ds(m + m // 8, 8, stride=PITCH), :] for m in range(15)]
         before, after = [near[7]], [near[8]]
         for m in range(1, 8):
             before.append(before[-1] + near[7 - m])
         for m in range(1, 7):
             after.append(after[-1] + near[8 + m])
         window = [before[7]] + [before[7 - b] + after[b - 1] for b in range(1, 8)]
-
-        zero = jnp.zeros((8, LANES), jnp.float32)
-        one, two, three = ([zero] * 4 for _ in range(3))
-        data = [spread(pitched, m) for m in range(7)]
-        even = [data[2 * m] - data[2 * m + 1] for m in range(3)]
-        odd = [data[2 * m + 1] for m in range(3)]
-        next_even = [data[2 * m + 1] - data[2 * m + 2] for m in range(3)]
-        current = data[6]
-        for a in range(taps // 2):
-            middle, following = spread(pitched, 2 * a + 7), spread(pitched, 2 * a + 8)
-            even.append(current - middle)
-            odd.append(middle)
-            next_even.append(middle - following)
-            current = following
-            t0 = tmpl[index, pl.ds(2 * a, 8, stride=0), :]
-            t1 = tmpl[index, pl.ds(2 * a + 1, 8, stride=0), :]
-            both = t0 + t1
-            for b in range(4):
-                one[b] = one[b] + t0 * even[a + b]
-                two[b] = two[b] + both * odd[a + b]
-                three[b] = three[b] + t1 * next_even[a + b]
         gain = gains[pl.ds(index, 8, stride=0), :]
         for b in range(8):
-            product = one[b // 2] + two[b // 2] if b % 2 == 0 else two[b // 2] - three[b // 2]
-            value = product * lax.rsqrt(window[b] / taps + 1e-06) * gain
-            total[pl.ds((i * groups + g) * shifts + b, 8, stride=8), :] = value
+            scale = lax.rsqrt(window[b] / taps + 1e-06) * gain
+            scales[pl.ds(index * shifts + b, 8, stride=8), :] = scale
         return 0
 
     lax.fori_loop(0, n * groups, item, 0)
-    rest_f = jnp.concatenate(
-        [
-            sum(total[(i * groups + g) * shifts : (i * groups + g + 1) * shifts, :] for g in range(groups))
-            for i in range(n)
-        ],
-        axis=0,
+    def dot(left, right):
+        return jnp.dot(left, right, preferred_element_type=jnp.float32)
+
+    bins = forward.shape[0] // 2
+    forward_terms = three_terms(forward[...])
+    inverse_terms = jnp.concatenate(three_terms(inverse[...]), axis=0)
+    totals = []
+    for i in range(n):
+        spectra = []
+        for value, depth in ((rows_b[i], rows_b.shape[1]), (packed[i][:taps, :], taps)):
+            terms = [dot(term[:, :depth], value) for term in forward_terms]
+            spectra.append(terms[2] + terms[1] + terms[0])
+        rec, tmpl = spectra
+        rec_c, rec_s, tmpl_c, tmpl_s = rec[:bins], rec[bins:], tmpl[:bins], tmpl[bins:]
+        spectrum = jnp.concatenate(
+            [rec_c * tmpl_c + rec_s * tmpl_s, rec_c * tmpl_s - rec_s * tmpl_c], axis=0
+        )
+        products = [
+            dot(inverse_terms[: (3 - m) * shifts, :], term)
+            for m, term in enumerate(three_terms(spectrum))
+        ]
+        small = products[0][2 * shifts :] + products[1][shifts:] + products[2]
+        lag = small + (products[0][shifts : 2 * shifts] + products[1][:shifts]) + products[0][:shifts]
+        totals.append(
+            sum(
+                lag[:, g * LANES : (g + 1) * LANES]
+                * scales[(i * groups + g) * shifts : (i * groups + g + 1) * shifts, :]
+                for g in range(groups)
+            )
+        )
+
+    ones = jnp.ones((8, LANES), jnp.bfloat16)
+    stacked = sum(
+        lax.dot_general(ones, term, (((1,), (1,)), ((), ())), preferred_element_type=jnp.float32)
+        for term in three_terms(jnp.concatenate(totals, axis=0))
     )
-    stacked = jnp.zeros((8, n * shifts), jnp.float32)
-    for _ in range(3):
-        term = rest_f.astype(jnp.bfloat16)
-        rest_f = rest_f - term.astype(jnp.float32)
-        stacked = stacked + lax.dot_general(
-            jnp.ones((8, LANES), jnp.bfloat16), term, (((1,), (1,)), ((), ())),
-            preferred_element_type=jnp.float32,
-        )
     result = prev_ref[0][...] if more else jnp.zeros(outs[0].shape[:1] + (shifts,), jnp.float32)
     sub = lax.broadcasted_iota(jnp.int32, result.shape, 0)
     blk = lax.axis_index("blk")
@@ -216,13 +229,13 @@
     outs[1][...] = jnp.where(chan == 0, right, left)
 
 
-def score(records, packed, places, templates, taps, shifts, prev=(), last=True):
+def score(records, tables, packed, places, templates, taps, shifts, prev=(), last=True):
     n = len(packed)
     samples, channels = records[0].shape
     width = packed[0].shape[1]
     groups = width // LANES
     items = n * groups
-    padded = -(-samples // 8) * 8
+    padded = tables[0].shape[1]
     vmem = pl.BlockSpec(memory_space=pltpu.VMEM)
     if last:
         out_shape = (jax.ShapeDtypeStruct((templates, shifts // 2), jnp.float32),) * 2
@@ -231,16 +244,15 @@
     return pl.pallas_call(
         functools.partial(score_kernel, taps, shifts, places, len(prev), int(last)),
         out_shape=out_shape,
-        in_specs=[vmem] * (2 + n + len(prev)),
+        in_specs=[vmem] * (4 + n + len(prev)),
         out_specs=(vmem,) * len(out_shape),
         scratch_shapes=[
-            pltpu.VMEM((items, taps + 8, LANES), jnp.float32),
             pltpu.VMEM((-(-items // 8) * 8 + 8, LANES), jnp.float32),
             pltpu.VMEM((n, LANES), jnp.int32),
             pltpu.SMEM((n, LANES), jnp.int32),
             pltpu.VMEM((2, samples, LANES), records[0].dtype),
             pltpu.VMEM((padded, LANES), jnp.float32),
-            pltpu.VMEM((padded // 8 * PITCH + 8, LANES), jnp.float32),
+            pltpu.VMEM((n, padded, width), jnp.bfloat16),
             pltpu.VMEM(((shifts // 8 + 2) * PITCH, LANES), jnp.float32),
             pltpu.VMEM((items * shifts + 8, LANES), jnp.float32),
             pltpu.SemaphoreType.DMA,
@@ -250,7 +262,7 @@
             flops=2 * n * width * taps * shifts, bytes_accessed=n * width * samples * 4, transcendentals=0
         ),
         name="score",
-    )(*records, *packed, *prev)
+    )(*records, *tables, *packed, *prev)
 
 
 def exchange(value, axis, size, mask):
@@ -263,7 +275,8 @@
     shifts = record.shape[2] - taps + 1
     packed, own = pack(templates[0], offsets, counts)
     mine = jnp.transpose(record[0])
-    packed, mine = lax.optimization_barrier((packed, mine))
+    period = -(-record.shape[2] // 64) * 64
+    tables = tuple(jnp.asarray(table) for table in fourier_tables(period, shifts))
     if blk == CHUNK:
         held = {0: own}
         for mask in (4, 1, 2):
@@ -278,7 +291,7 @@
         rows = ()
         for masks, last in (((0, 1, 2, 4), False), ((3, 5, 6, 7), True)):
             rows = score(
-                (mine, theirs), [held[m] for m in masks], [(m, False) for m in masks],
+                (mine, theirs), tables, [held[m] for m in masks], [(m, False) for m in masks],
                 blk, taps, shifts, rows, last,
             )
         keep, send = rows
@@ -289,7 +302,7 @@
         for at in range(0, blk, CHUNK):
             size = min(CHUNK, blk - at)
             keep, send = score(
-                (mine, theirs), [every[at + i] for i in range(size)],
+                (mine, theirs), tables, [every[at + i] for i in range(size)],
                 [(i, True) for i in range(size)], size, taps, shifts,
             )
             keeps.append(keep)

time: 29.9 us -> 28.5 us (0.953)
  local copies, waits for them, and re-layouts: 2.27 us -> 0.84 us
    unnamed x4 -> x8, local copies, waits for them, and re-layouts: 2.27 us -> 0.84 us
  transfers between devices with their start and end apart: 9 -> 9, of which waited for: 4 -> 4; matrix products, arithmetic and copies ran while one was open for 0% -> 0% of each run, Pallas kernels for 14% -> 15%
where the time goes in v3:
time: 28.5 us; the launch traced here: 28.3 us
  starting transfers between devices  11.1 us (39%)
  Pallas kernels  8.4 us (29%)
  waiting for transfers between devices  6.05 us (21%)
  between operations  1.38 us (5%)
  local copies, waits for them, and re-layouts  0.84 us (3%)
  other arithmetic  0.6 us (2%)
    ppermute x9, starting transfers between devices, exchange(): return lax.ppermute(value, axis, [(i, i ^ mask) for i in range(size)])  11.1 us
    pallas_call x2, Pallas kernels, score(): pl.pallas_call(functools.partial(score_kernel, taps, shifts, places, len(...  8.3 us
    ppermute x9, waiting for transfers between devices, exchange(): return lax.ppermute(value, axis, [(i, i ^ mask) for i in range(size)])  6.05 us
    unnamed x8, local copies, waits for them, and re-layouts  0.84 us
    broadcast_in_dim x1, other arithmetic, on_device(): return (keep + exchange(send, 'chan', 2, 1))[None]  0.6 us
  transfers between devices with their start and end apart: 9, of which 4 were waited for; matrix products, arithmetic and copies ran while one was open for 0% of the time, Pallas kernels for 15%

profile of v3, /device:TPU:0, one launch (start us, length us, event | category | flops | bytes accessed | tf_op | source)
XLA Modules:
  0.0 28.3 jit_solution(1365424787254366782)
XLA Ops:
  0.0 0.5 %collective-permute-start = (bf16[191,5000]{1,0:T(8,128)(2,1)}, bf16[191,5000]{1,0:T(8,128)(2,1)S(1)}, u32[]{:S(2)}, u32[]{:S(2)}) collective-permute-start(bf16[191,5000]{1,0:T(8,128)(2,1)} %bitcast.6), channel_id=1, source_target_pairs={{0,1},{1,0},{2,3},{3,2},{4,5},{5,4},{6,7},{7,6},{8,9},{9,8},{10,11... | collective-permute-start | bytes 5730008 | tf_op jit(solution)/shard_map/ppermute | solution.py:269
  1.7 0.0 copy-start.3
  1.8 0.8 %copy-done.3 = bf16[1,256,128]{2,1,0:T(8,128)(2,1)S(1)} copy-done((bf16[1,256,128]{2,1,0:T(8,128)(2,1)S(1)}, bf16[1,256,128]{2,1,0:T(8,128)(2,1)}, u32[]{:S(2)}) %copy-start.3) | copy-done | bytes 65560
  2.6 0.0 copy-start
  2.6 0.0 copy-start.1
  2.6 0.0 copy-start.2
  2.6 0.1 pack.1
  2.7 3.7 %collective-permute-start.1 = (bf16[144,256]{1,0:T(8,128)(2,1)S(1)}, bf16[144,256]{1,0:T(8,128)(2,1)S(1)}, u32[]{:S(2)}, u32[]{:S(2)}) collective-permute-start(bf16[144,256]{1,0:T(8,128)(2,1)S(1)} %get-tuple-element.12), channel_id=1, source_target_pairs={{0,8},{2,10},{4,12},{6,14},{8,0},{10,2},{12,4},{14,6},{1,9},{3,11}... | collective-permute-start | bytes 221192 | tf_op jit(solution)/shard_map/ppermute | solution.py:269
  6.4 1.5 %collective-permute-start.2 = (bf16[144,256]{1,0:T(8,128)(2,1)S(1)}, bf16[144,256]{1,0:T(8,128)(2,1)S(1)}, u32[]{:S(2)}, u32[]{:S(2)}) collective-permute-start(bf16[144,256]{1,0:T(8,128)(2,1)S(1)} %get-tuple-element.12), channel_id=1, source_target_pairs={{0,2},{2,0},{4,6},{6,4},{8,10},{10,8},{12,14},{14,12},{1,3},{3,1},... | collective-permute-start | bytes 221192 | tf_op jit(solution)/shard_map/ppermute | solution.py:269
  7.8 1.6 %collective-permute-start.3 = (bf16[144,256]{1,0:T(8,128)(2,1)S(1)}, bf16[144,256]{1,0:T(8,128)(2,1)S(1)}, u32[]{:S(2)}, u32[]{:S(2)}) collective-permute-start(bf16[144,256]{1,0:T(8,128)(2,1)S(1)} %get-tuple-element.12), channel_id=1, source_target_pairs={{0,4},{2,6},{4,0},{6,2},{8,12},{10,14},{12,8},{14,10},{1,5},{3,7},... | collective-permute-start | bytes 221192 | tf_op jit(solution)/shard_map/ppermute | solution.py:269
  9.4 1.6 %collective-permute-done.1.refs_7_ = bf16[144,256]{1,0:T(8,128)(2,1)S(1)} collective-permute-done((bf16[144,256]{1,0:T(8,128)(2,1)S(1)}, bf16[144,256]{1,0:T(8,128)(2,1)S(1)}, u32[]{:S(2)}, u32[]{:S(2)}) %collective-permute-start.1) | collective-permute-done | bytes 73760 | tf_op jit(solution)/shard_map/ppermute | solution.py:269
  11.0 0.0 collective-permute-done.2.refs_5_
  11.0 1.3 %collective-permute-done.3.refs_6_ = bf16[144,256]{1,0:T(8,128)(2,1)S(1)} collective-permute-done((bf16[144,256]{1,0:T(8,128)(2,1)S(1)}, bf16[144,256]{1,0:T(8,128)(2,1)S(1)}, u32[]{:S(2)}, u32[]{:S(2)}) %collective-permute-start.3) | collective-permute-done | bytes 73760 | tf_op jit(solution)/shard_map/ppermute | solution.py:269
  12.3 1.4 %collective-permute-start.6 = (bf16[144,256]{1,0:T(8,128)(2,1)S(1)}, bf16[144,256]{1,0:T(8,128)(2,1)S(1)}, u32[]{:S(2)}, u32[]{:S(2)}) collective-permute-start(bf16[144,256]{1,0:T(8,128)(2,1)S(1)} %collective-permute-done.1.refs_7_), channel_id=1, source_target_pairs={{0,4},{2,6},{4,0},{6,2},{8,12},{10,14},{12,8},{14,10},{1,5},{3,7},... | collective-permute-start | bytes 221192 | tf_op jit(solution)/shard_map/ppermute | solution.py:269
  13.8 0.5 %collective-permute-start.5 = (bf16[144,256]{1,0:T(8,128)(2,1)S(1)}, bf16[144,256]{1,0:T(8,128)(2,1)S(1)}, u32[]{:S(2)}, u32[]{:S(2)}) collective-permute-start(bf16[144,256]{1,0:T(8,128)(2,1)S(1)} %collective-permute-done.1.refs_7_), channel_id=1, source_target_pairs={{0,2},{2,0},{4,6},{6,4},{8,10},{10,8},{12,14},{14,12},{1,3},{3,1},... | collective-permute-start | bytes 221192 | tf_op jit(solution)/shard_map/ppermute | solution.py:269
  14.3 0.8 %collective-permute-start.4 = (bf16[144,256]{1,0:T(8,128)(2,1)S(1)}, bf16[144,256]{1,0:T(8,128)(2,1)S(1)}, u32[]{:S(2)}, u32[]{:S(2)}) collective-permute-start(bf16[144,256]{1,0:T(8,128)(2,1)S(1)} %collective-permute-done.2.refs_5_), channel_id=1, source_target_pairs={{0,4},{2,6},{4,0},{6,2},{8,12},{10,14},{12,8},{14,10},{1,5},{3,7},... | collective-permute-start | bytes 221192 | tf_op jit(solution)/shard_map/ppermute | solution.py:269
  15.1 2.0 %collective-permute-done.6.refs_6_ = bf16[144,256]{1,0:T(8,128)(2,1)S(1)} collective-permute-done((bf16[144,256]{1,0:T(8,128)(2,1)S(1)}, bf16[144,256]{1,0:T(8,128)(2,1)S(1)}, u32[]{:S(2)}, u32[]{:S(2)}) %collective-permute-start.6) | collective-permute-done | bytes 73760 | tf_op jit(solution)/shard_map/ppermute | solution.py:269
  17.0 1.1 %collective-permute-start.7 = (bf16[144,256]{1,0:T(8,128)(2,1)S(1)}, bf16[144,256]{1,0:T(8,128)(2,1)S(1)}, u32[]{:S(2)}, u32[]{:S(2)}) collective-permute-start(bf16[144,256]{1,0:T(8,128)(2,1)S(1)} %collective-permute-done.6.refs_6_), channel_id=1, source_target_pairs={{0,2},{2,0},{4,6},{6,4},{8,10},{10,8},{12,14},{14,12},{1,3},{3,1},... | collective-permute-start | bytes 221192 | tf_op jit(solution)/shard_map/ppermute | solution.py:269
  18.1 0.0 collective-permute-done.refs_1_
  18.1 0.0 copy-done
  18.1 0.0 copy-done.1
  18.2 0.0 copy-done.2
  18.2 4.1 %score.2.refs_8_ = f32[8,64]{1,0:T(8,128)S(1)} custom-call(bf16[191,5000]{1,0:T(8,128)(2,1)S(1)} %bitcast.7, bf16[191,5000]{1,0:T(8,128)(2,1)S(1)} %collective-permute-done.refs_1_, f32[208,192]{1,0:T(8,128)S(1)} %copy-done.1, f32[64,208]{1,0:T(8,128)S(1)} %copy-done.2, bf16[144,256]{1,0:T(8,128)(2,1)S(1)} %get-tuple-element.15.refs_4_, ...), custom_call_target="tpu_custom_call" | custom-call | flops 16777216 | bytes 782336 | tf_op jit(solution)/shard_map/score/pallas_call | solution.py:244
  22.3 0.0 collective-permute-done.5.refs_5_
  22.3 0.0 collective-permute-done.4.refs_4_
  22.3 0.0 collective-permute-done.7.refs_7_
  22.3 4.2 %score.3 = (f32[8,32]{1,0:T(8,128)S(1)}, f32[8,32]{1,0:T(8,128)S(1)}) custom-call(bf16[191,5000]{1,0:T(8,128)(2,1)S(1)} %bitcast.8, bf16[191,5000]{1,0:T(8,128)(2,1)S(1)} %collective-permute-done.refs_1_, f32[208,192]{1,0:T(8,128)S(1)} %copy-done.1, f32[64,208]{1,0:T(8,128)S(1)} %copy-done.2, bf16[144,256]{1,0:T(8,128)(2,1)S(1)} %collective-permute-done.4.refs_4_, ...), custom_call_target="tpu_custom_call" | custom-call | flops 16777216 | bytes 782336 | tf_op jit(solution)/shard_map/score/pallas_call | solution.py:244
  26.5 0.1 collective-permute-start.8
  26.6 1.2 %collective-permute-done.8 = f32[8,32]{1,0:T(8,128)S(1)} collective-permute-done((f32[8,32]{1,0:T(8,128)S(1)}, f32[8,32]{1,0:T(8,128)S(1)}, u32[]{:S(2)}, u32[]{:S(2)}) %collective-permute-start.8) | collective-permute-done | bytes 1056 | tf_op jit(solution)/shard_map/ppermute | solution.py:269
  27.7 0.6 %add_bitcast_fusion = f32[1,8,32]{2,1,0:T(8,128)} fusion(f32[8,32]{1,0:T(8,128)S(1)} %get-tuple-element.17, f32[8,32]{1,0:T(8,128)S(1)} %collective-permute-done.8), kind=kLoop, calls=%fused_computation | loop fusion | flops 256 | bytes 3072 | tf_op jit(solution)/shard_map/broadcast_in_dim | solution.py:311
Async XLA Ops:
  0.0 18.1 %collective-permute-start = (bf16[191,5000]{1,0:T(8,128)(2,1)}, bf16[191,5000]{1,0:T(8,128)(2,1)S(1)}, u32[]{:S(2)}, u32[]{:S(2)}) collective-permute-start(bf16[191,5000]{1,0:T(8,128)(2,1)} %bitcast.6), channel_id=1, source_target_pairs={{0,1},{1,0},{2,3},{3,2},{4,5},{5,4},{6,7},{7,6},{8,9},{9,8},{10,11... | collective-permute-start | bytes 5730008 | tf_op jit(solution)/shard_map/ppermute | solution.py:269
  1.7 0.8 %copy-start.3 = (bf16[1,256,128]{2,1,0:T(8,128)(2,1)S(1)}, bf16[1,256,128]{2,1,0:T(8,128)(2,1)}, u32[]{:S(2)}) copy-start(bf16[1,256,128]{2,1,0:T(8,128)(2,1)} %param.7) | copy-start | bytes 196612
  2.6 15.6 %copy-start = (bf16[1,5000,191]{1,2,0:T(8,128)(2,1)S(1)}, bf16[1,5000,191]{1,2,0:T(8,128)(2,1)}, u32[]{:S(2)}) copy-start(bf16[1,5000,191]{1,2,0:T(8,128)(2,1)} %param.6) | copy-start | bytes 5730004
  2.6 15.6 %copy-start.1 = (f32[208,192]{1,0:T(8,128)S(1)}, f32[208,192]{1,0:T(8,128)}, u32[]{:S(2)}) copy-start(f32[208,192]{1,0:T(8,128)} %constant.4.clone.refs_2_) | copy-start | bytes 479236
  2.6 15.6 %copy-start.2 = (f32[64,208]{1,0:T(8,128)S(1)}, f32[64,208]{1,0:T(8,128)}, u32[]{:S(2)}) copy-start(f32[64,208]{1,0:T(8,128)} %constant.5.clone.refs_3_) | copy-start | bytes 159748
  2.7 8.3 %collective-permute-start.1 = (bf16[144,256]{1,0:T(8,128)(2,1)S(1)}, bf16[144,256]{1,0:T(8,128)(2,1)S(1)}, u32[]{:S(2)}, u32[]{:S(2)}) collective-permute-start(bf16[144,256]{1,0:T(8,128)(2,1)S(1)} %get-tuple-element.12), channel_id=1, source_target_pairs={{0,8},{2,10},{4,12},{6,14},{8,0},{10,2},{12,4},{14,6},{1,9},{3,11}... | collective-permute-start | bytes 221192 | tf_op jit(solution)/shard_map/ppermute | solution.py:269
  6.4 4.6 %collective-permute-start.2 = (bf16[144,256]{1,0:T(8,128)(2,1)S(1)}, bf16[144,256]{1,0:T(8,128)(2,1)S(1)}, u32[]{:S(2)}, u32[]{:S(2)}) collective-permute-start(bf16[144,256]{1,0:T(8,128)(2,1)S(1)} %get-tuple-element.12), channel_id=1, source_target_pairs={{0,2},{2,0},{4,6},{6,4},{8,10},{10,8},{12,14},{14,12},{1,3},{3,1},... | collective-permute-start | bytes 221192 | tf_op jit(solution)/shard_map/ppermute | solution.py:269
  7.8 4.5 %collective-permute-start.3 = (bf16[144,256]{1,0:T(8,128)(2,1)S(1)}, bf16[144,256]{1,0:T(8,128)(2,1)S(1)}, u32[]{:S(2)}, u32[]{:S(2)}) collective-permute-start(bf16[144,256]{1,0:T(8,128)(2,1)S(1)} %get-tuple-element.12), channel_id=1, source_target_pairs={{0,4},{2,6},{4,0},{6,2},{8,12},{10,14},{12,8},{14,10},{1,5},{3,7},... | collective-permute-start | bytes 221192 | tf_op jit(solution)/shard_map/ppermute | solution.py:269
  12.3 4.7 %collective-permute-start.6 = (bf16[144,256]{1,0:T(8,128)(2,1)S(1)}, bf16[144,256]{1,0:T(8,128)(2,1)S(1)}, u32[]{:S(2)}, u32[]{:S(2)}) collective-permute-start(bf16[144,256]{1,0:T(8,128)(2,1)S(1)} %collective-permute-done.1.refs_7_), channel_id=1, source_target_pairs={{0,4},{2,6},{4,0},{6,2},{8,12},{10,14},{12,8},{14,10},{1,5},{3,7},... | collective-permute-start | bytes 221192 | tf_op jit(solution)/shard_map/ppermute | solution.py:269
  13.8 8.5 %collective-permute-start.5 = (bf16[144,256]{1,0:T(8,128)(2,1)S(1)}, bf16[144,256]{1,0:T(8,128)(2,1)S(1)}, u32[]{:S(2)}, u32[]{:S(2)}) collective-permute-start(bf16[144,256]{1,0:T(8,128)(2,1)S(1)} %collective-permute-done.1.refs_7_), channel_id=1, source_target_pairs={{0,2},{2,0},{4,6},{6,4},{8,10},{10,8},{12,14},{14,12},{1,3},{3,1},... | collective-permute-start | bytes 221192 | tf_op jit(solution)/shard_map/ppermute | solution.py:269
  14.3 8.0 %collective-permute-start.4 = (bf16[144,256]{1,0:T(8,128)(2,1)S(1)}, bf16[144,256]{1,0:T(8,128)(2,1)S(1)}, u32[]{:S(2)}, u32[]{:S(2)}) collective-permute-start(bf16[144,256]{1,0:T(8,128)(2,1)S(1)} %collective-permute-done.2.refs_5_), channel_id=1, source_target_pairs={{0,4},{2,6},{4,0},{6,2},{8,12},{10,14},{12,8},{14,10},{1,5},{3,7},... | collective-permute-start | bytes 221192 | tf_op jit(solution)/shard_map/ppermute | solution.py:269
  17.0 5.3 %collective-permute-start.7 = (bf16[144,256]{1,0:T(8,128)(2,1)S(1)}, bf16[144,256]{1,0:T(8,128)(2,1)S(1)}, u32[]{:S(2)}, u32[]{:S(2)}) collective-permute-start(bf16[144,256]{1,0:T(8,128)(2,1)S(1)} %collective-permute-done.6.refs_6_), channel_id=1, source_target_pairs={{0,2},{2,0},{4,6},{6,4},{8,10},{10,8},{12,14},{14,12},{1,3},{3,1},... | collective-permute-start | bytes 221192 | tf_op jit(solution)/shard_map/ppermute | solution.py:269
  26.5 1.2 %collective-permute-start.8 = (f32[8,32]{1,0:T(8,128)S(1)}, f32[8,32]{1,0:T(8,128)S(1)}, u32[]{:S(2)}, u32[]{:S(2)}) collective-permute-start(f32[8,32]{1,0:T(8,128)S(1)} %get-tuple-element.18), channel_id=1, source_target_pairs={{0,1},{1,0},{2,3},{3,2},{4,5},{5,4},{6,7},{7,6},{8,9},{9,8},{10,11... | collective-permute-start | bytes 3080 | tf_op jit(solution)/shard_map/ppermute | solution.py:269

commit v4 on v3

--- a/solution.py
+++ b/solution.py
@@ -14,13 +14,21 @@
 PITCH = 9
 
 
-def pack_kernel(off_ref, cnt_ref, tmpl_ref, out_ref, own_ref):
+def pack_kernel(off_ref, cnt_ref, tmpl_ref, out_ref, own_ref, off_s, cnt_s, tmpl_v, sems):
     rows, taps = tmpl_ref.shape
-    turned = jnp.transpose(tmpl_ref[...].astype(jnp.float32)).astype(out_ref.dtype)
+    copies = [
+        pltpu.make_async_copy(source, target, sems.at[at])
+        for at, (source, target) in enumerate(((off_ref, off_s), (cnt_ref, cnt_s), (tmpl_ref, tmpl_v)))
+    ]
+    for copy in copies:
+        copy.start()
+    for copy in copies:
+        copy.wait()
+    turned = jnp.transpose(tmpl_v[...].astype(jnp.float32)).astype(out_ref.dtype)
     out_ref[:taps, :] = turned
     own_ref[:taps, :] = turned
     lane = lax.broadcasted_iota(jnp.int32, (META, rows), 1)
-    off, cnt = off_ref[0], cnt_ref[0]
+    off, cnt = off_s[0], cnt_s[0]
     level = lax.broadcasted_iota(jnp.int32, (META, rows), 0)
     value = jnp.where(lane == 0, off, cnt)
     meta = jnp.where(level == 0, value >> 8, value & 255)
@@ -34,10 +42,12 @@
     return pl.pallas_call(
         pack_kernel,
         out_shape=(jax.ShapeDtypeStruct((taps + META, rows), templates.dtype),) * 2,
-        in_specs=[
-            pl.BlockSpec(memory_space=pltpu.SMEM),
-            pl.BlockSpec(memory_space=pltpu.SMEM),
-            pl.BlockSpec(memory_space=pltpu.VMEM),
+        in_specs=[pl.BlockSpec(memory_space=pl.ANY)] * 3,
+        scratch_shapes=[
+            pltpu.SMEM((1,), jnp.int32),
+            pltpu.SMEM((1,), jnp.int32),
+            pltpu.VMEM((rows, taps), templates.dtype),
+            pltpu.SemaphoreType.DMA((3,)),
         ],
         out_specs=(pl.BlockSpec(memory_space=pltpu.VMEM),) * 2,
         cost_estimate=pl.CostEstimate(flops=4 * 10**9, bytes_accessed=10**7, transcendentals=0),
@@ -282,18 +292,24 @@
         for mask in (4, 1, 2):
             held[mask] = exchange(packed, "blk", blk, mask)
         theirs = exchange(mine, "chan", 2, 1)
-        near = lax.optimization_barrier((held[4], held[1], held[2]))
-        held[4], held[1], held[2] = near
-        held[3] = exchange(held[1], "blk", blk, 2)
-        held[6] = exchange(held[4], "blk", blk, 2)
-        held[5] = exchange(held[4], "blk", blk, 1)
-        held[7] = exchange(held[6], "blk", blk, 1)
-        rows = ()
-        for masks, last in (((0, 1, 2, 4), False), ((3, 5, 6, 7), True)):
-            rows = score(
+
+        def step(masks, rows, last=False):
+            return score(
                 (mine, theirs), tables, [held[m] for m in masks], [(m, False) for m in masks],
                 blk, taps, shifts, rows, last,
             )
+
+        rows = step((0,), ())
+        rows, *near = lax.optimization_barrier((rows, held[4], held[1], held[2]))
+        held[4], held[1], held[2] = near
+        held[6] = exchange(held[4], "blk", blk, 2)
+        held[5] = exchange(held[4], "blk", blk, 1)
+        held[3] = exchange(held[1], "blk", blk, 2)
+        rows = step((1, 2, 4), rows)
+        rows, held[6] = lax.optimization_barrier((rows, held[6]))
+        held[7] = exchange(held[6], "blk", blk, 1)
+        rows = step((3, 5, 6), rows)
+        rows = step((7,), rows, True)
         keep, send = rows
     else:
         theirs = exchange(mine, "chan", 2, 1)

time: 28.5 us -> 28.5 us (level)
  waiting for transfers between devices: 6.05 us -> 3.43 us
  Pallas kernels: 8.4 us -> 10.7 us
    ppermute x9, waiting for transfers between devices: 6.05 us -> 3.43 us  [exchange(): return lax.ppermute(value, axis, [(i, i ^ mask) for i in range(size)])]
    pallas_call x2 -> x4, Pallas kernels: 8.3 us -> 9.99 us  [score(): pl.pallas_call(functools.partial(score_kernel, taps, shifts, places, len(...]
    pallas_call x1, Pallas kernels: 0.1 us -> 0.68 us  [pack(): pl.pallas_call(pack_kernel, out_shape=(jax.ShapeDtypeStruct((taps + META,...]
  transfers between devices with their start and end apart: 9 -> 9, of which waited for: 4 -> 2; matrix products, arithmetic and copies ran while one was open for 0% -> 0% of each run, Pallas kernels for 15% -> 31%
where the time goes in v4:
time: 28.5 us; the launch traced here: 28.3 us
  starting transfers between devices  11.3 us (40%)
  Pallas kernels  10.7 us (38%)
  waiting for transfers between devices  3.43 us (12%)
  between operations  1.4 us (5%)
  local copies, waits for them, and re-layouts  0.84 us (3%)
  other arithmetic  0.6 us (2%)
    ppermute x9, starting transfers between devices, exchange(): return lax.ppermute(value, axis, [(i, i ^ mask) for i in range(size)])  11.3 us
    pallas_call x4, Pallas kernels, score(): pl.pallas_call(functools.partial(score_kernel, taps, shifts, places, len(...  9.99 us
    ppermute x9, waiting for transfers between devices, exchange(): return lax.ppermute(value, axis, [(i, i ^ mask) for i in range(size)])  3.43 us
    unnamed x8, local copies, waits for them, and re-layouts  0.84 us
    pallas_call x1, Pallas kernels, pack(): pl.pallas_call(pack_kernel, out_shape=(jax.ShapeDtypeStruct((taps + META,...  0.68 us
    broadcast_in_dim x1, other arithmetic, on_device(): return (keep + exchange(send, 'chan', 2, 1))[None]  0.6 us
  transfers between devices with their start and end apart: 9, of which 2 were waited for; matrix products, arithmetic and copies ran while one was open for 0% of the time, Pallas kernels for 31%

profile of v4, /device:TPU:0, one launch (start us, length us, event | category | flops | bytes accessed | tf_op | source)
XLA Modules:
  0.0 28.3 jit_solution(15713610521314039413)
XLA Ops:
  0.0 0.5 %collective-permute-start = (bf16[191,5000]{1,0:T(8,128)(2,1)}, bf16[191,5000]{1,0:T(8,128)(2,1)S(1)}, u32[]{:S(2)}, u32[]{:S(2)}) collective-permute-start(bf16[191,5000]{1,0:T(8,128)(2,1)} %bitcast.6), channel_id=1, source_target_pairs={{0,1},{1,0},{2,3},{3,2},{4,5},{5,4},{6,7},{7,6},{8,9},{9,8},{10,11... | collective-permute-start | bytes 5730008 | tf_op jit(solution)/shard_map/ppermute | solution.py:279
  1.7 0.0 copy-start.3
  1.8 0.8 %copy-done.3 = bf16[1,256,128]{2,1,0:T(8,128)(2,1)S(1)} copy-done((bf16[1,256,128]{2,1,0:T(8,128)(2,1)S(1)}, bf16[1,256,128]{2,1,0:T(8,128)(2,1)}, u32[]{:S(2)}) %copy-start.3) | copy-done | bytes 65560
  2.6 0.0 copy-start
  2.6 0.0 copy-start.1
  2.6 0.0 copy-start.2
  2.6 0.7 %pack.1 = (bf16[144,256]{1,0:T(8,128)(2,1)S(1)}, bf16[144,256]{1,0:T(8,128)(2,1)S(1)}) custom-call(s32[1]{0:T(128)S(6)} %copy.7.off_ref, s32[1]{0:T(128)S(6)} %copy.8.cnt_ref, bf16[256,128]{1,0:T(8,128)(2,1)S(1)} %bitcast.11), custom_call_target="tpu_custom_call" | custom-call | flops 4000000000 | bytes 10000000 | tf_op jit(solution)/shard_map/pack/pallas_call | solution.py:42
  3.3 2.6 %collective-permute-start.3 = (bf16[144,256]{1,0:T(8,128)(2,1)S(1)}, bf16[144,256]{1,0:T(8,128)(2,1)S(1)}, u32[]{:S(2)}, u32[]{:S(2)}) collective-permute-start(bf16[144,256]{1,0:T(8,128)(2,1)S(1)} %get-tuple-element.16), channel_id=1, source_target_pairs={{0,4},{2,6},{4,0},{6,2},{8,12},{10,14},{12,8},{14,10},{1,5},{3,7},... | collective-permute-start | bytes 221192 | tf_op jit(solution)/shard_map/ppermute | solution.py:279
  5.9 1.5 %collective-permute-start.2 = (bf16[144,256]{1,0:T(8,128)(2,1)S(1)}, bf16[144,256]{1,0:T(8,128)(2,1)S(1)}, u32[]{:S(2)}, u32[]{:S(2)}) collective-permute-start(bf16[144,256]{1,0:T(8,128)(2,1)S(1)} %get-tuple-element.16), channel_id=1, source_target_pairs={{0,2},{2,0},{4,6},{6,4},{8,10},{10,8},{12,14},{14,12},{1,3},{3,1},... | collective-permute-start | bytes 221192 | tf_op jit(solution)/shard_map/ppermute | solution.py:279
  7.4 2.6 %collective-permute-start.1 = (bf16[144,256]{1,0:T(8,128)(2,1)S(1)}, bf16[144,256]{1,0:T(8,128)(2,1)S(1)}, u32[]{:S(2)}, u32[]{:S(2)}) collective-permute-start(bf16[144,256]{1,0:T(8,128)(2,1)S(1)} %get-tuple-element.16), channel_id=1, source_target_pairs={{0,8},{2,10},{4,12},{6,14},{8,0},{10,2},{12,4},{14,6},{1,9},{3,11}... | collective-permute-start | bytes 221192 | tf_op jit(solution)/shard_map/ppermute | solution.py:279
  10.0 0.0 collective-permute-done.refs_1_
  10.0 0.0 copy-done
  10.0 0.0 copy-done.1
  10.0 0.0 copy-done.2
  10.0 1.6 %score.4.refs_7_ = f32[8,64]{1,0:T(8,128)S(1)} custom-call(bf16[191,5000]{1,0:T(8,128)(2,1)S(1)} %bitcast.7, bf16[191,5000]{1,0:T(8,128)(2,1)S(1)} %collective-permute-done.refs_1_, f32[208,192]{1,0:T(8,128)S(1)} %copy-done.1, f32[64,208]{1,0:T(8,128)S(1)} %copy-done.2, bf16[144,256]{1,0:T(8,128)(2,1)S(1)} %get-tuple-element.15.refs_4_), custom_call_target="tpu_custom_call" | custom-call | flops 4194304 | bytes 195584 | tf_op jit(solution)/shard_map/score/pallas_call | solution.py:254
  11.7 0.0 collective-permute-done.3.refs_5_
  11.7 0.0 collective-permute-done.2.refs_4_
  11.7 2.3 %collective-permute-done.1.refs_6_ = bf16[144,256]{1,0:T(8,128)(2,1)S(1)} collective-permute-done((bf16[144,256]{1,0:T(8,128)(2,1)S(1)}, bf16[144,256]{1,0:T(8,128)(2,1)S(1)}, u32[]{:S(2)}, u32[]{:S(2)}) %collective-permute-start.1) | collective-permute-done | bytes 73760 | tf_op jit(solution)/shard_map/ppermute | solution.py:279
  13.9 0.0 collective-permute-start.4
  13.9 0.8 %collective-permute-start.7 = (bf16[144,256]{1,0:T(8,128)(2,1)S(1)}, bf16[144,256]{1,0:T(8,128)(2,1)S(1)}, u32[]{:S(2)}, u32[]{:S(2)}) collective-permute-start(bf16[144,256]{1,0:T(8,128)(2,1)S(1)} %collective-permute-done.1.refs_6_), channel_id=1, source_target_pairs={{0,2},{2,0},{4,6},{6,4},{8,10},{10,8},{12,14},{14,12},{1,3},{3,1},... | collective-permute-start | bytes 221192 | tf_op jit(solution)/shard_map/ppermute | solution.py:279
  14.8 1.9 %collective-permute-start.6 = (bf16[144,256]{1,0:T(8,128)(2,1)S(1)}, bf16[144,256]{1,0:T(8,128)(2,1)S(1)}, u32[]{:S(2)}, u32[]{:S(2)}) collective-permute-start(bf16[144,256]{1,0:T(8,128)(2,1)S(1)} %collective-permute-done.2.refs_4_), channel_id=1, source_target_pairs={{0,4},{2,6},{4,0},{6,2},{8,12},{10,14},{12,8},{14,10},{1,5},{3,7},... | collective-permute-start | bytes 221192 | tf_op jit(solution)/shard_map/ppermute | solution.py:279
  16.7 3.3 %score.5.refs_7_ = f32[8,64]{1,0:T(8,128)S(1)} custom-call(bf16[191,5000]{1,0:T(8,128)(2,1)S(1)} %bitcast.8, bf16[191,5000]{1,0:T(8,128)(2,1)S(1)} %collective-permute-done.refs_1_, f32[208,192]{1,0:T(8,128)S(1)} %copy-done.1, f32[64,208]{1,0:T(8,128)S(1)} %copy-done.2, bf16[144,256]{1,0:T(8,128)(2,1)S(1)} %collective-permute-done.2.refs_4_, ...), custom_call_target="tpu_custom_call" | custom-call | flops 12582912 | bytes 586752 | tf_op jit(solution)/shard_map/score/pallas_call | solution.py:254
  20.0 0.0 collective-permute-done.4.refs_6_
  20.0 1.4 %collective-permute-start.5 = (bf16[144,256]{1,0:T(8,128)(2,1)S(1)}, bf16[144,256]{1,0:T(8,128)(2,1)S(1)}, u32[]{:S(2)}, u32[]{:S(2)}) collective-permute-start(bf16[144,256]{1,0:T(8,128)(2,1)S(1)} %collective-permute-done.4.refs_6_), channel_id=1, source_target_pairs={{0,2},{2,0},{4,6},{6,4},{8,10},{10,8},{12,14},{14,12},{1,3},{3,1},... | collective-permute-start | bytes 221192 | tf_op jit(solution)/shard_map/ppermute | solution.py:279
  21.4 0.0 collective-permute-done.6.refs_4_
  21.4 0.0 collective-permute-done.7.refs_5_
  21.4 3.3 %score.6.refs_5_ = f32[8,64]{1,0:T(8,128)S(1)} custom-call(bf16[191,5000]{1,0:T(8,128)(2,1)S(1)} %bitcast.9, bf16[191,5000]{1,0:T(8,128)(2,1)S(1)} %collective-permute-done.refs_1_, f32[208,192]{1,0:T(8,128)S(1)} %copy-done.1, f32[64,208]{1,0:T(8,128)S(1)} %copy-done.2, bf16[144,256]{1,0:T(8,128)(2,1)S(1)} %collective-permute-done.6.refs_4_, ...), custom_call_target="tpu_custom_call" | custom-call | flops 12582912 | bytes 586752 | tf_op jit(solution)/shard_map/score/pallas_call | solution.py:254
  24.7 0.0 collective-permute-done.5.refs_4_
  24.7 1.8 %score.7 = (f32[8,32]{1,0:T(8,128)S(1)}, f32[8,32]{1,0:T(8,128)S(1)}) custom-call(bf16[191,5000]{1,0:T(8,128)(2,1)S(1)} %bitcast.10, bf16[191,5000]{1,0:T(8,128)(2,1)S(1)} %collective-permute-done.refs_1_, f32[208,192]{1,0:T(8,128)S(1)} %copy-done.1, f32[64,208]{1,0:T(8,128)S(1)} %copy-done.2, bf16[144,256]{1,0:T(8,128)(2,1)S(1)} %collective-permute-done.5.refs_4_, ...), custom_call_target="tpu_custom_call" | custom-call | flops 4194304 | bytes 195584 | tf_op jit(solution)/shard_map/score/pallas_call | solution.py:254
  26.5 0.1 collective-permute-start.8
  26.5 1.2 %collective-permute-done.8 = f32[8,32]{1,0:T(8,128)S(1)} collective-permute-done((f32[8,32]{1,0:T(8,128)S(1)}, f32[8,32]{1,0:T(8,128)S(1)}, u32[]{:S(2)}, u32[]{:S(2)}) %collective-permute-start.8) | collective-permute-done | bytes 1056 | tf_op jit(solution)/shard_map/ppermute | solution.py:279
  27.7 0.6 %add_bitcast_fusion = f32[1,8,32]{2,1,0:T(8,128)} fusion(f32[8,32]{1,0:T(8,128)S(1)} %get-tuple-element.23, f32[8,32]{1,0:T(8,128)S(1)} %collective-permute-done.8), kind=kLoop, calls=%fused_computation | loop fusion | flops 256 | bytes 3072 | tf_op jit(solution)/shard_map/broadcast_in_dim | solution.py:327
Async XLA Ops:
  0.0 10.0 %collective-permute-start = (bf16[191,5000]{1,0:T(8,128)(2,1)}, bf16[191,5000]{1,0:T(8,128)(2,1)S(1)}, u32[]{:S(2)}, u32[]{:S(2)}) collective-permute-start(bf16[191,5000]{1,0:T(8,128)(2,1)} %bitcast.6), channel_id=1, source_target_pairs={{0,1},{1,0},{2,3},{3,2},{4,5},{5,4},{6,7},{7,6},{8,9},{9,8},{10,11... | collective-permute-start | bytes 5730008 | tf_op jit(solution)/shard_map/ppermute | solution.py:279
  1.7 0.8 %copy-start.3 = (bf16[1,256,128]{2,1,0:T(8,128)(2,1)S(1)}, bf16[1,256,128]{2,1,0:T(8,128)(2,1)}, u32[]{:S(2)}) copy-start(bf16[1,256,128]{2,1,0:T(8,128)(2,1)} %param.7) | copy-start | bytes 196612
  2.6 7.4 %copy-start = (bf16[1,5000,191]{1,2,0:T(8,128)(2,1)S(1)}, bf16[1,5000,191]{1,2,0:T(8,128)(2,1)}, u32[]{:S(2)}) copy-start(bf16[1,5000,191]{1,2,0:T(8,128)(2,1)} %param.6) | copy-start | bytes 5730004
  2.6 7.4 %copy-start.1 = (f32[208,192]{1,0:T(8,128)S(1)}, f32[208,192]{1,0:T(8,128)}, u32[]{:S(2)}) copy-start(f32[208,192]{1,0:T(8,128)} %constant.4.clone.refs_2_) | copy-start | bytes 479236
  2.6 7.4 %copy-start.2 = (f32[64,208]{1,0:T(8,128)S(1)}, f32[64,208]{1,0:T(8,128)}, u32[]{:S(2)}) copy-start(f32[64,208]{1,0:T(8,128)} %constant.5.clone.refs_3_) | copy-start | bytes 159748
  3.3 8.4 %collective-permute-start.3 = (bf16[144,256]{1,0:T(8,128)(2,1)S(1)}, bf16[144,256]{1,0:T(8,128)(2,1)S(1)}, u32[]{:S(2)}, u32[]{:S(2)}) collective-permute-start(bf16[144,256]{1,0:T(8,128)(2,1)S(1)} %get-tuple-element.16), channel_id=1, source_target_pairs={{0,4},{2,6},{4,0},{6,2},{8,12},{10,14},{12,8},{14,10},{1,5},{3,7},... | collective-permute-start | bytes 221192 | tf_op jit(solution)/shard_map/ppermute | solution.py:279
  5.9 5.8 %collective-permute-start.2 = (bf16[144,256]{1,0:T(8,128)(2,1)S(1)}, bf16[144,256]{1,0:T(8,128)(2,1)S(1)}, u32[]{:S(2)}, u32[]{:S(2)}) collective-permute-start(bf16[144,256]{1,0:T(8,128)(2,1)S(1)} %get-tuple-element.16), channel_id=1, source_target_pairs={{0,2},{2,0},{4,6},{6,4},{8,10},{10,8},{12,14},{14,12},{1,3},{3,1},... | collective-permute-start | bytes 221192 | tf_op jit(solution)/shard_map/ppermute | solution.py:279
  7.4 6.5 %collective-permute-start.1 = (bf16[144,256]{1,0:T(8,128)(2,1)S(1)}, bf16[144,256]{1,0:T(8,128)(2,1)S(1)}, u32[]{:S(2)}, u32[]{:S(2)}) collective-permute-start(bf16[144,256]{1,0:T(8,128)(2,1)S(1)} %get-tuple-element.16), channel_id=1, source_target_pairs={{0,8},{2,10},{4,12},{6,14},{8,0},{10,2},{12,4},{14,6},{1,9},{3,11}... | collective-permute-start | bytes 221192 | tf_op jit(solution)/shard_map/ppermute | solution.py:279
  13.9 6.1 %collective-permute-start.4 = (bf16[144,256]{1,0:T(8,128)(2,1)S(1)}, bf16[144,256]{1,0:T(8,128)(2,1)S(1)}, u32[]{:S(2)}, u32[]{:S(2)}) collective-permute-start(bf16[144,256]{1,0:T(8,128)(2,1)S(1)} %collective-permute-done.1.refs_6_), channel_id=1, source_target_pairs={{0,4},{2,6},{4,0},{6,2},{8,12},{10,14},{12,8},{14,10},{1,5},{3,7},... | collective-permute-start | bytes 221192 | tf_op jit(solution)/shard_map/ppermute | solution.py:279
  13.9 7.4 %collective-permute-start.7 = (bf16[144,256]{1,0:T(8,128)(2,1)S(1)}, bf16[144,256]{1,0:T(8,128)(2,1)S(1)}, u32[]{:S(2)}, u32[]{:S(2)}) collective-permute-start(bf16[144,256]{1,0:T(8,128)(2,1)S(1)} %collective-permute-done.1.refs_6_), channel_id=1, source_target_pairs={{0,2},{2,0},{4,6},{6,4},{8,10},{10,8},{12,14},{14,12},{1,3},{3,1},... | collective-permute-start | bytes 221192 | tf_op jit(solution)/shard_map/ppermute | solution.py:279
  14.8 6.6 %collective-permute-start.6 = (bf16[144,256]{1,0:T(8,128)(2,1)S(1)}, bf16[144,256]{1,0:T(8,128)(2,1)S(1)}, u32[]{:S(2)}, u32[]{:S(2)}) collective-permute-start(bf16[144,256]{1,0:T(8,128)(2,1)S(1)} %collective-permute-done.2.refs_4_), channel_id=1, source_target_pairs={{0,4},{2,6},{4,0},{6,2},{8,12},{10,14},{12,8},{14,10},{1,5},{3,7},... | collective-permute-start | bytes 221192 | tf_op jit(solution)/shard_map/ppermute | solution.py:279
  20.0 4.7 %collective-permute-start.5 = (bf16[144,256]{1,0:T(8,128)(2,1)S(1)}, bf16[144,256]{1,0:T(8,128)(2,1)S(1)}, u32[]{:S(2)}, u32[]{:S(2)}) collective-permute-start(bf16[144,256]{1,0:T(8,128)(2,1)S(1)} %collective-permute-done.4.refs_6_), channel_id=1, source_target_pairs={{0,2},{2,0},{4,6},{6,4},{8,10},{10,8},{12,14},{14,12},{1,3},{3,1},... | collective-permute-start | bytes 221192 | tf_op jit(solution)/shard_map/ppermute | solution.py:279
  26.5 1.2 %collective-permute-start.8 = (f32[8,32]{1,0:T(8,128)S(1)}, f32[8,32]{1,0:T(8,128)S(1)}, u32[]{:S(2)}, u32[]{:S(2)}) collective-permute-start(f32[8,32]{1,0:T(8,128)S(1)} %get-tuple-element.24), channel_id=1, source_target_pairs={{0,1},{1,0},{2,3},{3,2},{4,5},{5,4},{6,7},{7,6},{8,9},{9,8},{10,11... | collective-permute-start | bytes 3080 | tf_op jit(solution)/shard_map/ppermute | solution.py:279

commit v5 on v4

--- a/solution.py
+++ b/solution.py
@@ -9,47 +9,32 @@
 from jax.sharding import PartitionSpec as P
 
 LANES = 128
-META = 16
+META = 8
 CHUNK = 8
 PITCH = 9
 
 
-def pack_kernel(off_ref, cnt_ref, tmpl_ref, out_ref, own_ref, off_s, cnt_s, tmpl_v, sems):
+def pack_kernel(off_ref, cnt_ref, tmpl_ref, out_ref, own_ref):
     rows, taps = tmpl_ref.shape
-    copies = [
-        pltpu.make_async_copy(source, target, sems.at[at])
-        for at, (source, target) in enumerate(((off_ref, off_s), (cnt_ref, cnt_s), (tmpl_ref, tmpl_v)))
-    ]
-    for copy in copies:
-        copy.start()
-    for copy in copies:
-        copy.wait()
-    turned = jnp.transpose(tmpl_v[...].astype(jnp.float32)).astype(out_ref.dtype)
-    out_ref[:taps, :] = turned
-    own_ref[:taps, :] = turned
     lane = lax.broadcasted_iota(jnp.int32, (META, rows), 1)
-    off, cnt = off_s[0], cnt_s[0]
     level = lax.broadcasted_iota(jnp.int32, (META, rows), 0)
-    value = jnp.where(lane == 0, off, cnt)
-    meta = jnp.where(level == 0, value >> 8, value & 255)
-    meta = meta.astype(jnp.float32).astype(out_ref.dtype)
-    out_ref[taps:, :] = meta
-    own_ref[taps:, :] = meta
+    value = jnp.where(lane == 0, off_ref[0], cnt_ref[0])
+    meta = jnp.where(level == 0, value >> 8, value & 255).astype(jnp.float32).astype(out_ref.dtype)
+    turned = jnp.transpose(tmpl_ref[...].astype(jnp.float32)).astype(out_ref.dtype)
+    for ref in (out_ref, own_ref):
+        ref[:taps, :] = turned
+        ref[taps:, :] = meta
 
 
 def pack(templates, offsets, counts):
     rows, taps = templates.shape
+    smem = pl.BlockSpec(memory_space=pltpu.SMEM)
+    vmem = pl.BlockSpec(memory_space=pltpu.VMEM)
     return pl.pallas_call(
         pack_kernel,
         out_shape=(jax.ShapeDtypeStruct((taps + META, rows), templates.dtype),) * 2,
-        in_specs=[pl.BlockSpec(memory_space=pl.ANY)] * 3,
-        scratch_shapes=[
-            pltpu.SMEM((1,), jnp.int32),
-            pltpu.SMEM((1,), jnp.int32),
-            pltpu.VMEM((rows, taps), templates.dtype),
-            pltpu.SemaphoreType.DMA((3,)),
-        ],
-        out_specs=(pl.BlockSpec(memory_space=pltpu.VMEM),) * 2,
+        in_specs=[smem, smem, vmem],
+        out_specs=(vmem, vmem),
         cost_estimate=pl.CostEstimate(flops=4 * 10**9, bytes_accessed=10**7, transcendentals=0),
         compiler_params=pltpu.CompilerParams(vmem_limit_bytes=4 * 2**20),
         name="pack",
@@ -75,13 +60,13 @@
     return forward.astype(np.float32), inverse[:, :shifts].T.astype(np.float32)
 
 
-def score_kernel(taps, shifts, places, more, last, *refs):
+def score_kernel(taps, shifts, places, more, last, split, *refs):
     n = len(places)
     mine, theirs, forward, inverse = refs[:4]
     packed = refs[4 : 4 + n]
     at = 4 + n + more
-    prev_ref, outs = refs[4 + n : at], refs[at : at + 1 + last]
-    gains, ints_v, ints, tails, rows_f, rows_b, sums, scales, sem = refs[at + 1 + last :]
+    prev_ref, outs = refs[4 + n : at], refs[at : at + 1 + last + 2 * split]
+    gains, ints, tails, rows_f, rows_b, sums, scales = refs[at + len(outs) :]
     samples, channels = mine.shape
     width = packed[0].shape[1]
     groups = width // LANES
@@ -94,9 +79,9 @@
 
     for i in range(n):
         meta = packed[i][taps:, :LANES].astype(jnp.float32)
-        ints_v[i : i + 1, :] = (meta[:1] * 256.0 + meta[1:2]).astype(jnp.int32)
-    to_scalars = pltpu.make_async_copy(ints_v, ints, sem)
-    to_scalars.start()
+        numbers = (meta[:1] * 256.0 + meta[1:2]).astype(jnp.int32)
+        ints[i, 0] = numbers[0, 0]
+        ints[i, 1] = numbers[0, 1]
     for i in range(n):
         for g in range(groups):
             block = packed[i][:taps, g * LANES : (g + 1) * LANES].astype(jnp.float32)
@@ -109,7 +94,6 @@
         tails[0, :, :rest] = mine[:, whole_tiles * LANES :]
         tails[1, :, :rest] = theirs[:, whole_tiles * LANES :]
     rows_f[(samples // 8) * 8 :, :] = jnp.zeros_like(rows_f[(samples // 8) * 8 :, :])
-    to_scalars.wait()
     for i in range(n):
         count = jnp.full((1, LANES), ints[i, 1], jnp.int32)
         ratio = jnp.sqrt(taps / count.astype(jnp.float32)) * (1.0 / taps)
@@ -192,14 +176,17 @@
     def dot(left, right):
         return jnp.dot(left, right, preferred_element_type=jnp.float32)
 
-    bins = forward.shape[0] // 2
-    forward_terms = three_terms(forward[...])
-    inverse_terms = jnp.concatenate(three_terms(inverse[...]), axis=0)
+    if split:
+        for table, ref in zip((forward, inverse), outs[-2:]):
+            ref[...] = jnp.concatenate(three_terms(table[...]), axis=0)
+        forward, inverse = outs[-2:]
+    tall = forward.shape[0] // 3
+    bins = tall // 2
     totals = []
     for i in range(n):
         spectra = []
         for value, depth in ((rows_b[i], rows_b.shape[1]), (packed[i][:taps, :], taps)):
-            terms = [dot(term[:, :depth], value) for term in forward_terms]
+            terms = [dot(forward[m * tall : (m + 1) * tall, :depth], value) for m in range(3)]
             spectra.append(terms[2] + terms[1] + terms[0])
         rec, tmpl = spectra
         rec_c, rec_s, tmpl_c, tmpl_s = rec[:bins], rec[bins:], tmpl[:bins], tmpl[bins:]
@@ -207,7 +194,7 @@
             [rec_c * tmpl_c + rec_s * tmpl_s, rec_c * tmpl_s - rec_s * tmpl_c], axis=0
         )
         products = [
-            dot(inverse_terms[: (3 - m) * shifts, :], term)
+            dot(inverse[: (3 - m) * shifts, :], term)
             for m, term in enumerate(three_terms(spectrum))
         ]
         small = products[0][2 * shifts :] + products[1][shifts:] + products[2]
@@ -239,7 +226,7 @@
     outs[1][...] = jnp.where(chan == 0, right, left)
 
 
-def score(records, tables, packed, places, templates, taps, shifts, prev=(), last=True):
+def score(records, tables, packed, places, templates, taps, shifts, prev=(), last=True, split=True):
     n = len(packed)
     samples, channels = records[0].shape
     width = packed[0].shape[1]
@@ -251,21 +238,23 @@
         out_shape = (jax.ShapeDtypeStruct((templates, shifts // 2), jnp.float32),) * 2
     else:
         out_shape = (jax.ShapeDtypeStruct((templates, shifts), jnp.float32),)
+    if split:
+        out_shape += tuple(
+            jax.ShapeDtypeStruct((3 * table.shape[0], table.shape[1]), jnp.bfloat16) for table in tables
+        )
     return pl.pallas_call(
-        functools.partial(score_kernel, taps, shifts, places, len(prev), int(last)),
+        functools.partial(score_kernel, taps, shifts, places, len(prev), int(last), int(split)),
         out_shape=out_shape,
         in_specs=[vmem] * (4 + n + len(prev)),
         out_specs=(vmem,) * len(out_shape),
         scratch_shapes=[
             pltpu.VMEM((-(-items // 8) * 8 + 8, LANES), jnp.float32),
-            pltpu.VMEM((n, LANES), jnp.int32),
-            pltpu.SMEM((n, LANES), jnp.int32),
+            pltpu.SMEM((n, 2), jnp.int32),
             pltpu.VMEM((2, samples, LANES), records[0].dtype),
             pltpu.VMEM((padded, LANES), jnp.float32),
             pltpu.VMEM((n, padded, width), jnp.bfloat16),
             pltpu.VMEM(((shifts // 8 + 2) * PITCH, LANES), jnp.float32),
             pltpu.VMEM((items * shifts + 8, LANES), jnp.float32),
-            pltpu.SemaphoreType.DMA,
         ],
         compiler_params=pltpu.CompilerParams(vmem_limit_bytes=32 * 2**20),
         cost_estimate=pl.CostEstimate(
@@ -293,15 +282,16 @@
             held[mask] = exchange(packed, "blk", blk, mask)
         theirs = exchange(mine, "chan", 2, 1)
 
-        def step(masks, rows, last=False):
+        def step(masks, rows, last=False, split=False):
             return score(
                 (mine, theirs), tables, [held[m] for m in masks], [(m, False) for m in masks],
-                blk, taps, shifts, rows, last,
+                blk, taps, shifts, rows, last, split,
             )
 
-        rows = step((0,), ())
-        rows, *near = lax.optimization_barrier((rows, held[4], held[1], held[2]))
-        held[4], held[1], held[2] = near
+        rows, *tables = step((0,), (), split=True)
+        near = lax.optimization_barrier((rows, *(held[m] for m in (2, 1, 4))))
+        rows = near[:1]
+        held.update(zip((2, 1, 4), near[1:]))
         held[6] = exchange(held[4], "blk", blk, 2)
         held[5] = exchange(held[4], "blk", blk, 1)
         held[3] = exchange(held[1], "blk", blk, 2)
@@ -317,7 +307,7 @@
         keeps, sends = [], []
         for at in range(0, blk, CHUNK):
             size = min(CHUNK, blk - at)
-            keep, send = score(
+            keep, send, *_ = score(
                 (mine, theirs), tables, [every[at + i] for i in range(size)],
                 [(i, True) for i in range(size)], size, taps, shifts,
             )

time: 28.5 us -> 25.3 us (0.89)
  Pallas kernels: 10.7 us -> 8.18 us
  waiting for transfers between devices: 3.43 us -> 2.94 us
    pallas_call x4, Pallas kernels: 9.99 us -> 8.08 us  [score(): pl.pallas_call(functools.partial(score_kernel, taps, shifts, places, len(...]
    pallas_call x1, Pallas kernels: 0.68 us -> 0.1 us  [pack(): pl.pallas_call(pack_kernel, out_shape=(jax.ShapeDtypeStruct((taps + META,...]
    ppermute x9, waiting for transfers between devices: 3.43 us -> 2.94 us  [exchange(): return lax.ppermute(value, axis, [(i, i ^ mask) for i in range(size)])]
  transfers between devices with their start and end apart: 9 -> 9, of which waited for: 2 -> 4; matrix products, arithmetic and copies ran while one was open for 0% -> 0% of each run, Pallas kernels for 31% -> 27%
where the time goes in v5:
time: 25.3 us; the launch traced here: 25.1 us
  starting transfers between devices  11.2 us (44%)
  Pallas kernels  8.18 us (32%)
  waiting for transfers between devices  2.94 us (12%)
  between operations  1.34 us (5%)
  local copies, waits for them, and re-layouts  0.84 us (3%)
  other arithmetic  0.6 us (2%)
    ppermute x9, starting transfers between devices, exchange(): return lax.ppermute(value, axis, [(i, i ^ mask) for i in range(size)])  11.2 us
    pallas_call x4, Pallas kernels, score(): pl.pallas_call(functools.partial(score_kernel, taps, shifts, places, len(...  8.08 us
    ppermute x9, waiting for transfers between devices, exchange(): return lax.ppermute(value, axis, [(i, i ^ mask) for i in range(size)])  2.94 us
    unnamed x8, local copies, waits for them, and re-layouts  0.84 us
    broadcast_in_dim x1, other arithmetic, on_device(): return (keep + exchange(send, 'chan', 2, 1))[None]  0.6 us
  transfers between devices with their start and end apart: 9, of which 4 were waited for; matrix products, arithmetic and copies ran while one was open for 0% of the time, Pallas kernels for 27%

profile of v5, /device:TPU:0, one launch (start us, length us, event | category | flops | bytes accessed | tf_op | source)
XLA Modules:
  0.0 25.1 jit_solution(12940439981346997352)
XLA Ops:
  0.0 0.5 %collective-permute-start = (bf16[191,5000]{1,0:T(8,128)(2,1)}, bf16[191,5000]{1,0:T(8,128)(2,1)S(1)}, u32[]{:S(2)}, u32[]{:S(2)}) collective-permute-start(bf16[191,5000]{1,0:T(8,128)(2,1)} %bitcast.6), channel_id=1, source_target_pairs={{0,1},{1,0},{2,3},{3,2},{4,5},{5,4},{6,7},{7,6},{8,9},{9,8},{10,11... | collective-permute-start | bytes 5730008 | tf_op jit(solution)/shard_map/ppermute | solution.py:268
  1.7 0.0 copy-start.3
  1.8 0.8 %copy-done.3 = bf16[1,256,128]{2,1,0:T(8,128)(2,1)S(1)} copy-done((bf16[1,256,128]{2,1,0:T(8,128)(2,1)S(1)}, bf16[1,256,128]{2,1,0:T(8,128)(2,1)}, u32[]{:S(2)}) %copy-start.3) | copy-done | bytes 65560
  2.6 0.0 copy-start
  2.6 0.0 copy-start.1
  2.6 0.0 copy-start.2
  2.6 0.1 pack.1
  2.7 3.7 %collective-permute-start.3 = (bf16[136,256]{1,0:T(8,128)(2,1)S(1)}, bf16[136,256]{1,0:T(8,128)(2,1)S(1)}, u32[]{:S(2)}, u32[]{:S(2)}) collective-permute-start(bf16[136,256]{1,0:T(8,128)(2,1)S(1)} %get-tuple-element.22), channel_id=1, source_target_pairs={{0,8},{2,10},{4,12},{6,14},{8,0},{10,2},{12,4},{14,6},{1,9},{3,11}... | collective-permute-start | bytes 208904 | tf_op jit(solution)/shard_map/ppermute | solution.py:268
  6.4 1.5 %collective-permute-start.2 = (bf16[136,256]{1,0:T(8,128)(2,1)S(1)}, bf16[136,256]{1,0:T(8,128)(2,1)S(1)}, u32[]{:S(2)}, u32[]{:S(2)}) collective-permute-start(bf16[136,256]{1,0:T(8,128)(2,1)S(1)} %get-tuple-element.22), channel_id=1, source_target_pairs={{0,2},{2,0},{4,6},{6,4},{8,10},{10,8},{12,14},{14,12},{1,3},{3,1},... | collective-permute-start | bytes 208904 | tf_op jit(solution)/shard_map/ppermute | solution.py:268
  7.8 1.6 %collective-permute-start.1 = (bf16[136,256]{1,0:T(8,128)(2,1)S(1)}, bf16[136,256]{1,0:T(8,128)(2,1)S(1)}, u32[]{:S(2)}, u32[]{:S(2)}) collective-permute-start(bf16[136,256]{1,0:T(8,128)(2,1)S(1)} %get-tuple-element.22), channel_id=1, source_target_pairs={{0,4},{2,6},{4,0},{6,2},{8,12},{10,14},{12,8},{14,10},{1,5},{3,7},... | collective-permute-start | bytes 208904 | tf_op jit(solution)/shard_map/ppermute | solution.py:268
  9.4 0.0 collective-permute-done.refs_1_
  9.4 0.0 copy-done
  9.4 0.0 copy-done.1
  9.4 0.0 copy-done.2
  9.4 1.2 %score.4 = (f32[8,64]{1,0:T(8,128)S(1)}, bf16[624,192]{1,0:T(8,128)(2,1)S(1)}, bf16[192,208]{1,0:T(8,128)(2,1)S(1)}) custom-call(bf16[191,5000]{1,0:T(8,128)(2,1)S(1)} %bitcast.7, bf16[191,5000]{1,0:T(8,128)(2,1)S(1)} %collective-permute-done.refs_1_, f32[208,192]{1,0:T(8,128)S(1)} %copy-done.1, f32[64,208]{1,0:T(8,128)S(1)} %copy-done.2, ...), custom_call_target="tpu_custom_call" | custom-call | flops 4194304 | bytes 195584 | tf_op jit(solution)/shard_map/score/pallas_call | solution.py:245
  10.6 0.2 collective-permute-done.3.refs_6_
  10.8 0.0 collective-permute-done.2.refs_4_
  10.8 1.3 %collective-permute-done.1.refs_5_ = bf16[136,256]{1,0:T(8,128)(2,1)S(1)} collective-permute-done((bf16[136,256]{1,0:T(8,128)(2,1)S(1)}, bf16[136,256]{1,0:T(8,128)(2,1)S(1)}, u32[]{:S(2)}, u32[]{:S(2)}) %collective-permute-start.1) | collective-permute-done | bytes 69664 | tf_op jit(solution)/shard_map/ppermute | solution.py:268
  12.2 1.6 %collective-permute-start.4 = (bf16[136,256]{1,0:T(8,128)(2,1)S(1)}, bf16[136,256]{1,0:T(8,128)(2,1)S(1)}, u32[]{:S(2)}, u32[]{:S(2)}) collective-permute-start(bf16[136,256]{1,0:T(8,128)(2,1)S(1)} %collective-permute-done.3.refs_6_), channel_id=1, source_target_pairs={{0,4},{2,6},{4,0},{6,2},{8,12},{10,14},{12,8},{14,10},{1,5},{3,7},... | collective-permute-start | bytes 208904 | tf_op jit(solution)/shard_map/ppermute | solution.py:268
  13.7 0.5 %collective-permute-start.7 = (bf16[136,256]{1,0:T(8,128)(2,1)S(1)}, bf16[136,256]{1,0:T(8,128)(2,1)S(1)}, u32[]{:S(2)}, u32[]{:S(2)}) collective-permute-start(bf16[136,256]{1,0:T(8,128)(2,1)S(1)} %collective-permute-done.3.refs_6_), channel_id=1, source_target_pairs={{0,2},{2,0},{4,6},{6,4},{8,10},{10,8},{12,14},{14,12},{1,3},{3,1},... | collective-permute-start | bytes 208904 | tf_op jit(solution)/shard_map/ppermute | solution.py:268
  14.3 0.6 %collective-permute-start.6 = (bf16[136,256]{1,0:T(8,128)(2,1)S(1)}, bf16[136,256]{1,0:T(8,128)(2,1)S(1)}, u32[]{:S(2)}, u32[]{:S(2)}) collective-permute-start(bf16[136,256]{1,0:T(8,128)(2,1)S(1)} %collective-permute-done.2.refs_4_), channel_id=1, source_target_pairs={{0,4},{2,6},{4,0},{6,2},{8,12},{10,14},{12,8},{14,10},{1,5},{3,7},... | collective-permute-start | bytes 208904 | tf_op jit(solution)/shard_map/ppermute | solution.py:268
  14.9 2.8 %score.5.refs_7_ = f32[8,64]{1,0:T(8,128)S(1)} custom-call(bf16[191,5000]{1,0:T(8,128)(2,1)S(1)} %bitcast.8, bf16[191,5000]{1,0:T(8,128)(2,1)S(1)} %collective-permute-done.refs_1_, bf16[624,192]{1,0:T(8,128)(2,1)S(1)} %get-tuple-element.19.refs_2_, bf16[192,208]{1,0:T(8,128)(2,1)S(1)} %get-tuple-element.20.refs_3_, ...), custom_call_target="tpu_custom_call" | custom-call | flops 12582912 | bytes 586752 | tf_op jit(solution)/shard_map/score/pallas_call | solution.py:245
  17.7 0.0 collective-permute-done.4.refs_6_
  17.7 1.3 %collective-permute-start.5 = (bf16[136,256]{1,0:T(8,128)(2,1)S(1)}, bf16[136,256]{1,0:T(8,128)(2,1)S(1)}, u32[]{:S(2)}, u32[]{:S(2)}) collective-permute-start(bf16[136,256]{1,0:T(8,128)(2,1)S(1)} %collective-permute-done.4.refs_6_), channel_id=1, source_target_pairs={{0,2},{2,0},{4,6},{6,4},{8,10},{10,8},{12,14},{14,12},{1,3},{3,1},... | collective-permute-start | bytes 208904 | tf_op jit(solution)/shard_map/ppermute | solution.py:268
  19.1 0.0 collective-permute-done.6.refs_4_
  19.1 0.0 collective-permute-done.7.refs_5_
  19.1 2.8 %score.6.refs_5_ = f32[8,64]{1,0:T(8,128)S(1)} custom-call(bf16[191,5000]{1,0:T(8,128)(2,1)S(1)} %bitcast.9, bf16[191,5000]{1,0:T(8,128)(2,1)S(1)} %collective-permute-done.refs_1_, bf16[624,192]{1,0:T(8,128)(2,1)S(1)} %get-tuple-element.19.refs_2_, bf16[192,208]{1,0:T(8,128)(2,1)S(1)} %get-tuple-element.20.refs_3_, ...), custom_call_target="tpu_custom_call" | custom-call | flops 12582912 | bytes 586752 | tf_op jit(solution)/shard_map/score/pallas_call | solution.py:245
  21.9 0.2 collective-permute-done.5.refs_4_
  22.1 1.3 %score.7 = (f32[8,32]{1,0:T(8,128)S(1)}, f32[8,32]{1,0:T(8,128)S(1)}) custom-call(bf16[191,5000]{1,0:T(8,128)(2,1)S(1)} %bitcast.10, bf16[191,5000]{1,0:T(8,128)(2,1)S(1)} %collective-permute-done.refs_1_, bf16[624,192]{1,0:T(8,128)(2,1)S(1)} %get-tuple-element.19.refs_2_, bf16[192,208]{1,0:T(8,128)(2,1)S(1)} %get-tuple-element.20.refs_3_, ...), custom_call_target="tpu_custom_call" | custom-call | flops 4194304 | bytes 195584 | tf_op jit(solution)/shard_map/score/pallas_call | solution.py:245
  23.4 0.0 collective-permute-start.8
  23.4 1.2 %collective-permute-done.8 = f32[8,32]{1,0:T(8,128)S(1)} collective-permute-done((f32[8,32]{1,0:T(8,128)S(1)}, f32[8,32]{1,0:T(8,128)S(1)}, u32[]{:S(2)}, u32[]{:S(2)}) %collective-permute-start.8) | collective-permute-done | bytes 1056 | tf_op jit(solution)/shard_map/ppermute | solution.py:268
  24.5 0.6 %add_bitcast_fusion = f32[1,8,32]{2,1,0:T(8,128)} fusion(f32[8,32]{1,0:T(8,128)S(1)} %get-tuple-element.29, f32[8,32]{1,0:T(8,128)S(1)} %collective-permute-done.8), kind=kLoop, calls=%fused_computation | loop fusion | flops 256 | bytes 3072 | tf_op jit(solution)/shard_map/broadcast_in_dim | solution.py:317
Async XLA Ops:
  0.0 9.4 %collective-permute-start = (bf16[191,5000]{1,0:T(8,128)(2,1)}, bf16[191,5000]{1,0:T(8,128)(2,1)S(1)}, u32[]{:S(2)}, u32[]{:S(2)}) collective-permute-start(bf16[191,5000]{1,0:T(8,128)(2,1)} %bitcast.6), channel_id=1, source_target_pairs={{0,1},{1,0},{2,3},{3,2},{4,5},{5,4},{6,7},{7,6},{8,9},{9,8},{10,11... | collective-permute-start | bytes 5730008 | tf_op jit(solution)/shard_map/ppermute | solution.py:268
  1.7 0.8 %copy-start.3 = (bf16[1,256,128]{2,1,0:T(8,128)(2,1)S(1)}, bf16[1,256,128]{2,1,0:T(8,128)(2,1)}, u32[]{:S(2)}) copy-start(bf16[1,256,128]{2,1,0:T(8,128)(2,1)} %param.7) | copy-start | bytes 196612
  2.6 6.8 %copy-start = (bf16[1,5000,191]{1,2,0:T(8,128)(2,1)S(1)}, bf16[1,5000,191]{1,2,0:T(8,128)(2,1)}, u32[]{:S(2)}) copy-start(bf16[1,5000,191]{1,2,0:T(8,128)(2,1)} %param.6) | copy-start | bytes 5730004
  2.6 6.8 %copy-start.1 = (f32[208,192]{1,0:T(8,128)S(1)}, f32[208,192]{1,0:T(8,128)}, u32[]{:S(2)}) copy-start(f32[208,192]{1,0:T(8,128)} %constant.4.clone.refs_2_) | copy-start | bytes 479236
  2.6 6.8 %copy-start.2 = (f32[64,208]{1,0:T(8,128)S(1)}, f32[64,208]{1,0:T(8,128)}, u32[]{:S(2)}) copy-start(f32[64,208]{1,0:T(8,128)} %constant.5.clone.refs_3_) | copy-start | bytes 159748
  2.7 8.1 %collective-permute-start.3 = (bf16[136,256]{1,0:T(8,128)(2,1)S(1)}, bf16[136,256]{1,0:T(8,128)(2,1)S(1)}, u32[]{:S(2)}, u32[]{:S(2)}) collective-permute-start(bf16[136,256]{1,0:T(8,128)(2,1)S(1)} %get-tuple-element.22), channel_id=1, source_target_pairs={{0,8},{2,10},{4,12},{6,14},{8,0},{10,2},{12,4},{14,6},{1,9},{3,11}... | collective-permute-start | bytes 208904 | tf_op jit(solution)/shard_map/ppermute | solution.py:268
  6.4 4.5 %collective-permute-start.2 = (bf16[136,256]{1,0:T(8,128)(2,1)S(1)}, bf16[136,256]{1,0:T(8,128)(2,1)S(1)}, u32[]{:S(2)}, u32[]{:S(2)}) collective-permute-start(bf16[136,256]{1,0:T(8,128)(2,1)S(1)} %get-tuple-element.22), channel_id=1, source_target_pairs={{0,2},{2,0},{4,6},{6,4},{8,10},{10,8},{12,14},{14,12},{1,3},{3,1},... | collective-permute-start | bytes 208904 | tf_op jit(solution)/shard_map/ppermute | solution.py:268
  7.8 4.3 %collective-permute-start.1 = (bf16[136,256]{1,0:T(8,128)(2,1)S(1)}, bf16[136,256]{1,0:T(8,128)(2,1)S(1)}, u32[]{:S(2)}, u32[]{:S(2)}) collective-permute-start(bf16[136,256]{1,0:T(8,128)(2,1)S(1)} %get-tuple-element.22), channel_id=1, source_target_pairs={{0,4},{2,6},{4,0},{6,2},{8,12},{10,14},{12,8},{14,10},{1,5},{3,7},... | collective-permute-start | bytes 208904 | tf_op jit(solution)/shard_map/ppermute | solution.py:268
  12.2 5.6 %collective-permute-start.4 = (bf16[136,256]{1,0:T(8,128)(2,1)S(1)}, bf16[136,256]{1,0:T(8,128)(2,1)S(1)}, u32[]{:S(2)}, u32[]{:S(2)}) collective-permute-start(bf16[136,256]{1,0:T(8,128)(2,1)S(1)} %collective-permute-done.3.refs_6_), channel_id=1, source_target_pairs={{0,4},{2,6},{4,0},{6,2},{8,12},{10,14},{12,8},{14,10},{1,5},{3,7},... | collective-permute-start | bytes 208904 | tf_op jit(solution)/shard_map/ppermute | solution.py:268
  13.7 5.3 %collective-permute-start.7 = (bf16[136,256]{1,0:T(8,128)(2,1)S(1)}, bf16[136,256]{1,0:T(8,128)(2,1)S(1)}, u32[]{:S(2)}, u32[]{:S(2)}) collective-permute-start(bf16[136,256]{1,0:T(8,128)(2,1)S(1)} %collective-permute-done.3.refs_6_), channel_id=1, source_target_pairs={{0,2},{2,0},{4,6},{6,4},{8,10},{10,8},{12,14},{14,12},{1,3},{3,1},... | collective-permute-start | bytes 208904 | tf_op jit(solution)/shard_map/ppermute | solution.py:268
  14.3 4.8 %collective-permute-start.6 = (bf16[136,256]{1,0:T(8,128)(2,1)S(1)}, bf16[136,256]{1,0:T(8,128)(2,1)S(1)}, u32[]{:S(2)}, u32[]{:S(2)}) collective-permute-start(bf16[136,256]{1,0:T(8,128)(2,1)S(1)} %collective-permute-done.2.refs_4_), channel_id=1, source_target_pairs={{0,4},{2,6},{4,0},{6,2},{8,12},{10,14},{12,8},{14,10},{1,5},{3,7},... | collective-permute-start | bytes 208904 | tf_op jit(solution)/shard_map/ppermute | solution.py:268
  17.7 4.3 %collective-permute-start.5 = (bf16[136,256]{1,0:T(8,128)(2,1)S(1)}, bf16[136,256]{1,0:T(8,128)(2,1)S(1)}, u32[]{:S(2)}, u32[]{:S(2)}) collective-permute-start(bf16[136,256]{1,0:T(8,128)(2,1)S(1)} %collective-permute-done.4.refs_6_), channel_id=1, source_target_pairs={{0,2},{2,0},{4,6},{6,4},{8,10},{10,8},{12,14},{14,12},{1,3},{3,1},... | collective-permute-start | bytes 208904 | tf_op jit(solution)/shard_map/ppermute | solution.py:268
  23.4 1.2 %collective-permute-start.8 = (f32[8,32]{1,0:T(8,128)S(1)}, f32[8,32]{1,0:T(8,128)S(1)}, u32[]{:S(2)}, u32[]{:S(2)}) collective-permute-start(f32[8,32]{1,0:T(8,128)S(1)} %get-tuple-element.30), channel_id=1, source_target_pairs={{0,1},{1,0},{2,3},{3,2},{4,5},{5,4},{6,7},{7,6},{8,9},{9,8},{10,11... | collective-permute-start | bytes 3080 | tf_op jit(solution)/shard_map/ppermute | solution.py:268

commit v6 on v5

--- a/solution.py
+++ b/solution.py
@@ -96,10 +96,10 @@
     rows_f[(samples // 8) * 8 :, :] = jnp.zeros_like(rows_f[(samples // 8) * 8 :, :])
     for i in range(n):
         count = jnp.full((1, LANES), ints[i, 1], jnp.int32)
-        ratio = jnp.sqrt(taps / count.astype(jnp.float32)) * (1.0 / taps)
+        ratio = lax.rsqrt(count.astype(jnp.float32)) * (taps**0.5 / taps)
         for g in range(groups):
             at = i * groups + g
-            gain = lax.rsqrt(gains[at : at + 1, :] / taps + 1e-06) * ratio
+            gain = lax.rsqrt(gains[at : at + 1, :] * (1.0 / taps) + 1e-06) * ratio
             gains[at : at + 1, :] = jnp.where(lane_row + (chan * width + g * LANES) < count, gain, 0.0)
 
     wide = lax.broadcasted_iota(jnp.int32, (samples, LANES), 1)
@@ -168,7 +168,7 @@
         window = [before[7]] + [before[7 - b] + after[b - 1] for b in range(1, 8)]
         gain = gains[pl.ds(index, 8, stride=0), :]
         for b in range(8):
-            scale = lax.rsqrt(window[b] / taps + 1e-06) * gain
+            scale = lax.rsqrt(window[b] * (1.0 / taps) + 1e-06) * gain
             scales[pl.ds(index * shifts + b, 8, stride=8), :] = scale
         return 0
 
@@ -186,8 +186,8 @@
     for i in range(n):
         spectra = []
         for value, depth in ((rows_b[i], rows_b.shape[1]), (packed[i][:taps, :], taps)):
-            terms = [dot(forward[m * tall : (m + 1) * tall, :depth], value) for m in range(3)]
-            spectra.append(terms[2] + terms[1] + terms[0])
+            terms = dot(forward[:, :depth], value)
+            spectra.append(terms[2 * tall :] + terms[tall : 2 * tall] + terms[:tall])
         rec, tmpl = spectra
         rec_c, rec_s, tmpl_c, tmpl_s = rec[:bins], rec[bins:], tmpl[:bins], tmpl[bins:]
         spectrum = jnp.concatenate(
@@ -278,8 +278,7 @@
     tables = tuple(jnp.asarray(table) for table in fourier_tables(period, shifts))
     if blk == CHUNK:
         held = {0: own}
-        for mask in (4, 1, 2):
-            held[mask] = exchange(packed, "blk", blk, mask)
+        held[4] = exchange(packed, "blk", blk, 4)
         theirs = exchange(mine, "chan", 2, 1)
 
         def step(masks, rows, last=False, split=False):
@@ -288,17 +287,18 @@
                 blk, taps, shifts, rows, last, split,
             )
 
-        rows, *tables = step((0,), (), split=True)
-        near = lax.optimization_barrier((rows, *(held[m] for m in (2, 1, 4))))
-        rows = near[:1]
-        held.update(zip((2, 1, 4), near[1:]))
+        *rows, forward, inverse = step((0,), (), split=True)
+        tables = (forward, inverse)
+        rows, packed = lax.optimization_barrier((rows[0], packed))
+        held[2] = exchange(packed, "blk", blk, 2)
+        held[1] = exchange(packed, "blk", blk, 1)
         held[6] = exchange(held[4], "blk", blk, 2)
         held[5] = exchange(held[4], "blk", blk, 1)
         held[3] = exchange(held[1], "blk", blk, 2)
-        rows = step((1, 2, 4), rows)
-        rows, held[6] = lax.optimization_barrier((rows, held[6]))
+        rows = step((1, 2, 4), (rows,))
+        rows, held[6] = lax.optimization_barrier((rows[0], held[6]))
         held[7] = exchange(held[6], "blk", blk, 1)
-        rows = step((3, 5, 6), rows)
+        rows = step((3, 5, 6), (rows,))
         rows = step((7,), rows, True)
         keep, send = rows
     else:

time: 25.3 us -> 24.7 us (0.976)
  waiting for transfers between devices: 2.94 us -> 2.14 us
  starting transfers between devices: 11.2 us -> 11.5 us
    ppermute x9, waiting for transfers between devices: 2.94 us -> 2.14 us  [exchange(): return lax.ppermute(value, axis, [(i, i ^ mask) for i in range(size)])]
  transfers between devices with their start and end apart: 9 -> 9, of which waited for: 4 -> 3; matrix products, arithmetic and copies ran while one was open for 0% -> 0% of each run, Pallas kernels for 27% -> 28%
where the time goes in v6:
time: 24.7 us; the launch traced here: 24.5 us
  starting transfers between devices  11.5 us (47%)
  Pallas kernels  8.12 us (33%)
  waiting for transfers between devices  2.14 us (9%)
  between operations  1.34 us (5%)
  local copies, waits for them, and re-layouts  0.84 us (3%)
  other arithmetic  0.6 us (2%)
    ppermute x9, starting transfers between devices, exchange(): return lax.ppermute(value, axis, [(i, i ^ mask) for i in range(size)])  11.5 us
    pallas_call x4, Pallas kernels, score(): pl.pallas_call(functools.partial(score_kernel, taps, shifts, places, len(...  8.02 us
    ppermute x9, waiting for transfers between devices, exchange(): return lax.ppermute(value, axis, [(i, i ^ mask) for i in range(size)])  2.14 us
    unnamed x8, local copies, waits for them, and re-layouts  0.84 us
    broadcast_in_dim x1, other arithmetic, on_device(): return (keep + exchange(send, 'chan', 2, 1))[None]  0.6 us
  transfers between devices with their start and end apart: 9, of which 3 were waited for; matrix products, arithmetic and copies ran while one was open for 0% of the time, Pallas kernels for 28%

profile of v6, /device:TPU:0, one launch (start us, length us, event | category | flops | bytes accessed | tf_op | source)
XLA Modules:
  0.0 24.5 jit_solution(6126194376202385457)
XLA Ops:
  0.0 0.5 %collective-permute-start = (bf16[191,5000]{1,0:T(8,128)(2,1)}, bf16[191,5000]{1,0:T(8,128)(2,1)S(1)}, u32[]{:S(2)}, u32[]{:S(2)}) collective-permute-start(bf16[191,5000]{1,0:T(8,128)(2,1)} %bitcast.6), channel_id=1, source_target_pairs={{0,1},{1,0},{2,3},{3,2},{4,5},{5,4},{6,7},{7,6},{8,9},{9,8},{10,11... | collective-permute-start | bytes 5730008 | tf_op jit(solution)/shard_map/ppermute | solution.py:268
  1.7 0.0 copy-start.3
  1.8 0.8 %copy-done.3 = bf16[1,256,128]{2,1,0:T(8,128)(2,1)S(1)} copy-done((bf16[1,256,128]{2,1,0:T(8,128)(2,1)S(1)}, bf16[1,256,128]{2,1,0:T(8,128)(2,1)}, u32[]{:S(2)}) %copy-start.3) | copy-done | bytes 65560
  2.6 0.0 copy-start
  2.6 0.0 copy-start.1
  2.6 0.0 copy-start.2
  2.6 0.1 pack.1
  2.7 3.7 %collective-permute-start.3 = (bf16[136,256]{1,0:T(8,128)(2,1)S(1)}, bf16[136,256]{1,0:T(8,128)(2,1)S(1)}, u32[]{:S(2)}, u32[]{:S(2)}) collective-permute-start(bf16[136,256]{1,0:T(8,128)(2,1)S(1)} %get-tuple-element.21), channel_id=1, source_target_pairs={{0,8},{2,10},{4,12},{6,14},{8,0},{10,2},{12,4},{14,6},{1,9},{3,11}... | collective-permute-start | bytes 208904 | tf_op jit(solution)/shard_map/ppermute | solution.py:268
  6.4 0.0 collective-permute-done.refs_1_
  6.4 0.0 copy-done
  6.4 0.0 copy-done.1
  6.4 0.0 copy-done.2
  6.4 1.2 %score.4 = (f32[8,64]{1,0:T(8,128)S(1)}, bf16[624,192]{1,0:T(8,128)(2,1)S(1)}, bf16[192,208]{1,0:T(8,128)(2,1)S(1)}) custom-call(bf16[191,5000]{1,0:T(8,128)(2,1)S(1)} %bitcast.7, bf16[191,5000]{1,0:T(8,128)(2,1)S(1)} %collective-permute-done.refs_1_, f32[208,192]{1,0:T(8,128)S(1)} %copy-done.1, f32[64,208]{1,0:T(8,128)S(1)} %copy-done.2, ...), custom_call_target="tpu_custom_call" | custom-call | flops 4194304 | bytes 195584 | tf_op jit(solution)/shard_map/score/pallas_call | solution.py:245
  7.5 1.5 %collective-permute-start.1 = (bf16[136,256]{1,0:T(8,128)(2,1)S(1)}, bf16[136,256]{1,0:T(8,128)(2,1)S(1)}, u32[]{:S(2)}, u32[]{:S(2)}) collective-permute-start(bf16[136,256]{1,0:T(8,128)(2,1)S(1)} %get-tuple-element.21), channel_id=1, source_target_pairs={{0,2},{2,0},{4,6},{6,4},{8,10},{10,8},{12,14},{14,12},{1,3},{3,1},... | collective-permute-start | bytes 208904 | tf_op jit(solution)/shard_map/ppermute | solution.py:268
  9.1 1.6 %collective-permute-start.2 = (bf16[136,256]{1,0:T(8,128)(2,1)S(1)}, bf16[136,256]{1,0:T(8,128)(2,1)S(1)}, u32[]{:S(2)}, u32[]{:S(2)}) collective-permute-start(bf16[136,256]{1,0:T(8,128)(2,1)S(1)} %get-tuple-element.21), channel_id=1, source_target_pairs={{0,4},{2,6},{4,0},{6,2},{8,12},{10,14},{12,8},{14,10},{1,5},{3,7},... | collective-permute-start | bytes 208904 | tf_op jit(solution)/shard_map/ppermute | solution.py:268
  10.6 0.1 collective-permute-done.3.refs_6_
  10.7 0.7 %collective-permute-start.4 = (bf16[136,256]{1,0:T(8,128)(2,1)S(1)}, bf16[136,256]{1,0:T(8,128)(2,1)S(1)}, u32[]{:S(2)}, u32[]{:S(2)}) collective-permute-start(bf16[136,256]{1,0:T(8,128)(2,1)S(1)} %collective-permute-done.3.refs_6_), channel_id=1, source_target_pairs={{0,4},{2,6},{4,0},{6,2},{8,12},{10,14},{12,8},{14,10},{1,5},{3,7},... | collective-permute-start | bytes 208904 | tf_op jit(solution)/shard_map/ppermute | solution.py:268
  11.4 1.5 %collective-permute-start.7 = (bf16[136,256]{1,0:T(8,128)(2,1)S(1)}, bf16[136,256]{1,0:T(8,128)(2,1)S(1)}, u32[]{:S(2)}, u32[]{:S(2)}) collective-permute-start(bf16[136,256]{1,0:T(8,128)(2,1)S(1)} %collective-permute-done.3.refs_6_), channel_id=1, source_target_pairs={{0,2},{2,0},{4,6},{6,4},{8,10},{10,8},{12,14},{14,12},{1,3},{3,1},... | collective-permute-start | bytes 208904 | tf_op jit(solution)/shard_map/ppermute | solution.py:268
  12.9 0.0 collective-permute-done.1.refs_4_
  12.9 1.3 %collective-permute-start.6 = (bf16[136,256]{1,0:T(8,128)(2,1)S(1)}, bf16[136,256]{1,0:T(8,128)(2,1)S(1)}, u32[]{:S(2)}, u32[]{:S(2)}) collective-permute-start(bf16[136,256]{1,0:T(8,128)(2,1)S(1)} %collective-permute-done.1.refs_4_), channel_id=1, source_target_pairs={{0,4},{2,6},{4,0},{6,2},{8,12},{10,14},{12,8},{14,10},{1,5},{3,7},... | collective-permute-start | bytes 208904 | tf_op jit(solution)/shard_map/ppermute | solution.py:268
  14.3 0.0 collective-permute-done.2.refs_5_
  14.3 2.8 %score.5.refs_7_ = f32[8,64]{1,0:T(8,128)S(1)} custom-call(bf16[191,5000]{1,0:T(8,128)(2,1)S(1)} %bitcast.8, bf16[191,5000]{1,0:T(8,128)(2,1)S(1)} %collective-permute-done.refs_1_, bf16[624,192]{1,0:T(8,128)(2,1)S(1)} %get-tuple-element.17.refs_2_, bf16[192,208]{1,0:T(8,128)(2,1)S(1)} %get-tuple-element.18.refs_3_, ...), custom_call_target="tpu_custom_call" | custom-call | flops 12582912 | bytes 586752 | tf_op jit(solution)/shard_map/score/pallas_call | solution.py:245
  17.1 0.0 collective-permute-done.4.refs_6_
  17.1 0.7 %collective-permute-start.5 = (bf16[136,256]{1,0:T(8,128)(2,1)S(1)}, bf16[136,256]{1,0:T(8,128)(2,1)S(1)}, u32[]{:S(2)}, u32[]{:S(2)}) collective-permute-start(bf16[136,256]{1,0:T(8,128)(2,1)S(1)} %collective-permute-done.4.refs_6_), channel_id=1, source_target_pairs={{0,2},{2,0},{4,6},{6,4},{8,10},{10,8},{12,14},{14,12},{1,3},{3,1},... | collective-permute-start | bytes 208904 | tf_op jit(solution)/shard_map/ppermute | solution.py:268
  17.8 0.0 collective-permute-done.7.refs_5_
  17.8 0.0 collective-permute-done.6.refs_4_
  17.8 2.8 %score.6.refs_5_ = f32[8,64]{1,0:T(8,128)S(1)} custom-call(bf16[191,5000]{1,0:T(8,128)(2,1)S(1)} %bitcast.9, bf16[191,5000]{1,0:T(8,128)(2,1)S(1)} %collective-permute-done.refs_1_, bf16[624,192]{1,0:T(8,128)(2,1)S(1)} %get-tuple-element.17.refs_2_, bf16[192,208]{1,0:T(8,128)(2,1)S(1)} %get-tuple-element.18.refs_3_, ...), custom_call_target="tpu_custom_call" | custom-call | flops 12582912 | bytes 586752 | tf_op jit(solution)/shard_map/score/pallas_call | solution.py:245
  20.6 0.9 %collective-permute-done.5.refs_4_ = bf16[136,256]{1,0:T(8,128)(2,1)S(1)} collective-permute-done((bf16[136,256]{1,0:T(8,128)(2,1)S(1)}, bf16[136,256]{1,0:T(8,128)(2,1)S(1)}, u32[]{:S(2)}, u32[]{:S(2)}) %collective-permute-start.5) | collective-permute-done | bytes 69664 | tf_op jit(solution)/shard_map/ppermute | solution.py:268
  21.4 1.3 %score.7 = (f32[8,32]{1,0:T(8,128)S(1)}, f32[8,32]{1,0:T(8,128)S(1)}) custom-call(bf16[191,5000]{1,0:T(8,128)(2,1)S(1)} %bitcast.10, bf16[191,5000]{1,0:T(8,128)(2,1)S(1)} %collective-permute-done.refs_1_, bf16[624,192]{1,0:T(8,128)(2,1)S(1)} %get-tuple-element.17.refs_2_, bf16[192,208]{1,0:T(8,128)(2,1)S(1)} %get-tuple-element.18.refs_3_, ...), custom_call_target="tpu_custom_call" | custom-call | flops 4194304 | bytes 195584 | tf_op jit(solution)/shard_map/score/pallas_call | solution.py:245
  22.7 0.0 collective-permute-start.8
  22.7 1.2 %collective-permute-done.8 = f32[8,32]{1,0:T(8,128)S(1)} collective-permute-done((f32[8,32]{1,0:T(8,128)S(1)}, f32[8,32]{1,0:T(8,128)S(1)}, u32[]{:S(2)}, u32[]{:S(2)}) %collective-permute-start.8) | collective-permute-done | bytes 1056 | tf_op jit(solution)/shard_map/ppermute | solution.py:268
  23.9 0.6 %add_bitcast_fusion = f32[1,8,32]{2,1,0:T(8,128)} fusion(f32[8,32]{1,0:T(8,128)S(1)} %get-tuple-element.25, f32[8,32]{1,0:T(8,128)S(1)} %collective-permute-done.8), kind=kLoop, calls=%fused_computation | loop fusion | flops 256 | bytes 3072 | tf_op jit(solution)/shard_map/broadcast_in_dim | solution.py:317
Async XLA Ops:
  0.0 6.4 %collective-permute-start = (bf16[191,5000]{1,0:T(8,128)(2,1)}, bf16[191,5000]{1,0:T(8,128)(2,1)S(1)}, u32[]{:S(2)}, u32[]{:S(2)}) collective-permute-start(bf16[191,5000]{1,0:T(8,128)(2,1)} %bitcast.6), channel_id=1, source_target_pairs={{0,1},{1,0},{2,3},{3,2},{4,5},{5,4},{6,7},{7,6},{8,9},{9,8},{10,11... | collective-permute-start | bytes 5730008 | tf_op jit(solution)/shard_map/ppermute | solution.py:268
  1.7 0.8 %copy-start.3 = (bf16[1,256,128]{2,1,0:T(8,128)(2,1)S(1)}, bf16[1,256,128]{2,1,0:T(8,128)(2,1)}, u32[]{:S(2)}) copy-start(bf16[1,256,128]{2,1,0:T(8,128)(2,1)} %param.7) | copy-start | bytes 196612
  2.6 3.8 %copy-start = (bf16[1,5000,191]{1,2,0:T(8,128)(2,1)S(1)}, bf16[1,5000,191]{1,2,0:T(8,128)(2,1)}, u32[]{:S(2)}) copy-start(bf16[1,5000,191]{1,2,0:T(8,128)(2,1)} %param.6) | copy-start | bytes 5730004
  2.6 3.8 %copy-start.1 = (f32[208,192]{1,0:T(8,128)S(1)}, f32[208,192]{1,0:T(8,128)}, u32[]{:S(2)}) copy-start(f32[208,192]{1,0:T(8,128)} %constant.4.clone.refs_2_) | copy-start | bytes 479236
  2.6 3.8 %copy-start.2 = (f32[64,208]{1,0:T(8,128)S(1)}, f32[64,208]{1,0:T(8,128)}, u32[]{:S(2)}) copy-start(f32[64,208]{1,0:T(8,128)} %constant.5.clone.refs_3_) | copy-start | bytes 159748
  2.7 8.0 %collective-permute-start.3 = (bf16[136,256]{1,0:T(8,128)(2,1)S(1)}, bf16[136,256]{1,0:T(8,128)(2,1)S(1)}, u32[]{:S(2)}, u32[]{:S(2)}) collective-permute-start(bf16[136,256]{1,0:T(8,128)(2,1)S(1)} %get-tuple-element.21), channel_id=1, source_target_pairs={{0,8},{2,10},{4,12},{6,14},{8,0},{10,2},{12,4},{14,6},{1,9},{3,11}... | collective-permute-start | bytes 208904 | tf_op jit(solution)/shard_map/ppermute | solution.py:268
  7.5 5.4 %collective-permute-start.1 = (bf16[136,256]{1,0:T(8,128)(2,1)S(1)}, bf16[136,256]{1,0:T(8,128)(2,1)S(1)}, u32[]{:S(2)}, u32[]{:S(2)}) collective-permute-start(bf16[136,256]{1,0:T(8,128)(2,1)S(1)} %get-tuple-element.21), channel_id=1, source_target_pairs={{0,2},{2,0},{4,6},{6,4},{8,10},{10,8},{12,14},{14,12},{1,3},{3,1},... | collective-permute-start | bytes 208904 | tf_op jit(solution)/shard_map/ppermute | solution.py:268
  9.1 5.2 %collective-permute-start.2 = (bf16[136,256]{1,0:T(8,128)(2,1)S(1)}, bf16[136,256]{1,0:T(8,128)(2,1)S(1)}, u32[]{:S(2)}, u32[]{:S(2)}) collective-permute-start(bf16[136,256]{1,0:T(8,128)(2,1)S(1)} %get-tuple-element.21), channel_id=1, source_target_pairs={{0,4},{2,6},{4,0},{6,2},{8,12},{10,14},{12,8},{14,10},{1,5},{3,7},... | collective-permute-start | bytes 208904 | tf_op jit(solution)/shard_map/ppermute | solution.py:268
  10.7 6.4 %collective-permute-start.4 = (bf16[136,256]{1,0:T(8,128)(2,1)S(1)}, bf16[136,256]{1,0:T(8,128)(2,1)S(1)}, u32[]{:S(2)}, u32[]{:S(2)}) collective-permute-start(bf16[136,256]{1,0:T(8,128)(2,1)S(1)} %collective-permute-done.3.refs_6_), channel_id=1, source_target_pairs={{0,4},{2,6},{4,0},{6,2},{8,12},{10,14},{12,8},{14,10},{1,5},{3,7},... | collective-permute-start | bytes 208904 | tf_op jit(solution)/shard_map/ppermute | solution.py:268
  11.4 6.3 %collective-permute-start.7 = (bf16[136,256]{1,0:T(8,128)(2,1)S(1)}, bf16[136,256]{1,0:T(8,128)(2,1)S(1)}, u32[]{:S(2)}, u32[]{:S(2)}) collective-permute-start(bf16[136,256]{1,0:T(8,128)(2,1)S(1)} %collective-permute-done.3.refs_6_), channel_id=1, source_target_pairs={{0,2},{2,0},{4,6},{6,4},{8,10},{10,8},{12,14},{14,12},{1,3},{3,1},... | collective-permute-start | bytes 208904 | tf_op jit(solution)/shard_map/ppermute | solution.py:268
  12.9 4.8 %collective-permute-start.6 = (bf16[136,256]{1,0:T(8,128)(2,1)S(1)}, bf16[136,256]{1,0:T(8,128)(2,1)S(1)}, u32[]{:S(2)}, u32[]{:S(2)}) collective-permute-start(bf16[136,256]{1,0:T(8,128)(2,1)S(1)} %collective-permute-done.1.refs_4_), channel_id=1, source_target_pairs={{0,4},{2,6},{4,0},{6,2},{8,12},{10,14},{12,8},{14,10},{1,5},{3,7},... | collective-permute-start | bytes 208904 | tf_op jit(solution)/shard_map/ppermute | solution.py:268
  17.1 4.3 %collective-permute-start.5 = (bf16[136,256]{1,0:T(8,128)(2,1)S(1)}, bf16[136,256]{1,0:T(8,128)(2,1)S(1)}, u32[]{:S(2)}, u32[]{:S(2)}) collective-permute-start(bf16[136,256]{1,0:T(8,128)(2,1)S(1)} %collective-permute-done.4.refs_6_), channel_id=1, source_target_pairs={{0,2},{2,0},{4,6},{6,4},{8,10},{10,8},{12,14},{14,12},{1,3},{3,1},... | collective-permute-start | bytes 208904 | tf_op jit(solution)/shard_map/ppermute | solution.py:268
  22.7 1.2 %collective-permute-start.8 = (f32[8,32]{1,0:T(8,128)S(1)}, f32[8,32]{1,0:T(8,128)S(1)}, u32[]{:S(2)}, u32[]{:S(2)}) collective-permute-start(f32[8,32]{1,0:T(8,128)S(1)} %get-tuple-element.26), channel_id=1, source_target_pairs={{0,1},{1,0},{2,3},{3,2},{4,5},{5,4},{6,7},{7,6},{8,9},{9,8},{10,11... | collective-permute-start | bytes 3080 | tf_op jit(solution)/shard_map/ppermute | solution.py:268

commit v7 on v6

--- a/solution.py
+++ b/solution.py
@@ -93,7 +93,7 @@
     if rest:
         tails[0, :, :rest] = mine[:, whole_tiles * LANES :]
         tails[1, :, :rest] = theirs[:, whole_tiles * LANES :]
-    rows_f[(samples // 8) * 8 :, :] = jnp.zeros_like(rows_f[(samples // 8) * 8 :, :])
+    rows_f[:, (samples // 8) * 8 :, :] = jnp.zeros_like(rows_f[:, (samples // 8) * 8 :, :])
     for i in range(n):
         count = jnp.full((1, LANES), ints[i, 1], jnp.int32)
         ratio = lax.rsqrt(count.astype(jnp.float32)) * (taps**0.5 / taps)
@@ -108,71 +108,75 @@
         mixed = jnp.where(wide < turn, high.astype(jnp.float32), low.astype(jnp.float32))
         return pltpu.roll(mixed, (LANES - turn) & (LANES - 1), 1)
 
-    def item(index, _):
-        i, g = index // groups, index % groups
-        first = ints[i, 0] + chan * width + g * LANES
-        split = channels - first
-        half = jnp.where(split > 0, 0, 1)
+    def item(i, _):
+        first = ints[i, 0] + chan * width
+        half = jnp.where(first < channels, 0, 1)
         local = first - half * channels
         tile = local >> 7
-        fast = ((split >= LANES) | (split <= 0)) & (tile + 1 < whole_tiles)
+        fast = ((first + width <= channels) | (first >= channels)) & (tile + groups < whole_tiles)
 
         for source, here in ((mine, half == chan), (theirs, half != chan)):
 
             @pl.when(fast & here)
             def _():
-                at = pl.multiple_of(tile * LANES, LANES)
-                rows_f[:samples, :] = turned(
-                    source[:, pl.ds(at, LANES)], source[:, pl.ds(at + LANES, LANES)], local & (LANES - 1)
-                )
+                found = [
+                    source[:, pl.ds(pl.multiple_of((tile + m) * LANES, LANES), LANES)].astype(jnp.float32)
+                    for m in range(groups + 1)
+                ]
+                for g in range(groups):
+                    rows_f[g, :samples, :] = turned(found[g], found[g + 1], local & (LANES - 1))
 
         @pl.when(jnp.logical_not(fast))
         def _():
-            sides = []
-            for side in range(2):
-                begin = first - side * channels
-                turn = begin & (LANES - 1)
-                found = []
-                for m in range(2):
-                    want = (begin >> 7) + m
-                    at = pl.multiple_of(jnp.clip(want, 0, whole_tiles - 1) * LANES, LANES)
-                    value = jnp.where(
-                        chan == side,
-                        mine[:, pl.ds(at, LANES)].astype(jnp.float32),
-                        theirs[:, pl.ds(at, LANES)].astype(jnp.float32),
-                    )
-                    if rest:
-                        tail = tails[jnp.where(chan == side, 0, 1)].astype(jnp.float32)
-                        value = jnp.where(want >= whole_tiles, tail, value)
-                    found.append(value)
-                sides.append(turned(found[0], found[1], turn))
-            rows_f[:samples, :] = jnp.where(wide < split, sides[0], sides[1])
-
-        rows_b[i, :, pl.ds(pl.multiple_of(g * LANES, LANES), LANES)] = rows_f[...].astype(jnp.bfloat16)
-
-        origin = index >> 16
-        level = [rows_f[8 * m : 8 * m + 8, :] for m in range(steps + blocks)]
-        level = [v * v for v in level]
-        span = 1
-        while span < steps:
-            level = [level[m] + level[m + span] for m in range(len(level) - span)]
-            span *= 2
-        for m in range(blocks + 1):
-            sums[pl.ds(origin + PITCH * m, 8), :] = level[m]
-        near = [sums[pl.ds(m + m // 8, 8, stride=PITCH), :] for m in range(15)]
-        before, after = [near[7]], [near[8]]
-        for m in range(1, 8):
-            before.append(before[-1] + near[7 - m])
-        for m in range(1, 7):
-            after.append(after[-1] + near[8 + m])
-        window = [before[7]] + [before[7 - b] + after[b - 1] for b in range(1, 8)]
-        gain = gains[pl.ds(index, 8, stride=0), :]
-        for b in range(8):
-            scale = lax.rsqrt(window[b] * (1.0 / taps) + 1e-06) * gain
-            scales[pl.ds(index * shifts + b, 8, stride=8), :] = scale
+            for g in range(groups):
+                sides = []
+                for side in range(2):
+                    begin = first + g * LANES - side * channels
+                    found = []
+                    for m in range(2):
+                        want = (begin >> 7) + m
+                        at = pl.multiple_of(jnp.clip(want, 0, whole_tiles - 1) * LANES, LANES)
+                        value = jnp.where(
+                            chan == side,
+                            mine[:, pl.ds(at, LANES)].astype(jnp.float32),
+                            theirs[:, pl.ds(at, LANES)].astype(jnp.float32),
+                        )
+                        if rest:
+                            tail = tails[jnp.where(chan == side, 0, 1)].astype(jnp.float32)
+                            value = jnp.where(want >= whole_tiles, tail, value)
+                        found.append(value)
+                    sides.append(turned(found[0], found[1], begin & (LANES - 1)))
+                split = channels - first - g * LANES
+                rows_f[g, :samples, :] = jnp.where(wide < split, sides[0], sides[1])
+
+        origin = i >> 16
+        for g in range(groups):
+            index = i * groups + g
+            rows_b[i, :, g * LANES : (g + 1) * LANES] = rows_f[g].astype(jnp.bfloat16)
+
+            level = [rows_f[g, 8 * m : 8 * m + 8, :] for m in range(steps + blocks)]
+            level = [v * v for v in level]
+            span = 1
+            while span < steps:
+                level = [level[m] + level[m + span] for m in range(len(level) - span)]
+                span *= 2
+            for m in range(blocks + 1):
+                sums[g, pl.ds(origin + PITCH * m, 8), :] = level[m]
+            near = [sums[g, pl.ds(m + m // 8, 8, stride=PITCH), :] for m in range(15)]
+            before, after = [near[7]], [near[8]]
+            for m in range(1, 8):
+                before.append(before[-1] + near[7 - m])
+            for m in range(1, 7):
+                after.append(after[-1] + near[8 + m])
+            window = [before[7]] + [before[7 - b] + after[b - 1] for b in range(1, 8)]
+            gain = gains[pl.ds(index, 8, stride=0), :]
+            for b in range(8):
+                scale = lax.rsqrt(window[b] * (1.0 / taps) + 1e-06) * gain
+                scales[pl.ds(index * shifts + b, 8, stride=8), :] = scale
         return 0
 
-    lax.fori_loop(0, n * groups, item, 0)
+    lax.fori_loop(0, n, item, 0)
+
     def dot(left, right):
         return jnp.dot(left, right, preferred_element_type=jnp.float32)
 
@@ -251,9 +255,9 @@
             pltpu.VMEM((-(-items // 8) * 8 + 8, LANES), jnp.float32),
             pltpu.SMEM((n, 2), jnp.int32),
             pltpu.VMEM((2, samples, LANES), records[0].dtype),
-            pltpu.VMEM((padded, LANES), jnp.float32),
+            pltpu.VMEM((groups, padded, LANES), jnp.float32),
             pltpu.VMEM((n, padded, width), jnp.bfloat16),
-            pltpu.VMEM(((shifts // 8 + 2) * PITCH, LANES), jnp.float32),
+            pltpu.VMEM((groups, (shifts // 8 + 2) * PITCH, LANES), jnp.float32),
             pltpu.VMEM((items * shifts + 8, LANES), jnp.float32),
         ],
         compiler_params=pltpu.CompilerParams(vmem_limit_bytes=32 * 2**20),
@@ -278,7 +282,8 @@
     tables = tuple(jnp.asarray(table) for table in fourier_tables(period, shifts))
     if blk == CHUNK:
         held = {0: own}
-        held[4] = exchange(packed, "blk", blk, 4)
+        for mask in (4, 1, 2, 3):
+            held[mask] = exchange(packed, "blk", blk, mask)
         theirs = exchange(mine, "chan", 2, 1)
 
         def step(masks, rows, last=False, split=False):
@@ -289,16 +294,14 @@
 
         *rows, forward, inverse = step((0,), (), split=True)
         tables = (forward, inverse)
-        rows, packed = lax.optimization_barrier((rows[0], packed))
-        held[2] = exchange(packed, "blk", blk, 2)
-        held[1] = exchange(packed, "blk", blk, 1)
+        near = lax.optimization_barrier((rows[0], *(held[m] for m in (3, 2, 1, 4))))
+        held.update(zip((3, 2, 1, 4), near[1:]))
         held[6] = exchange(held[4], "blk", blk, 2)
         held[5] = exchange(held[4], "blk", blk, 1)
-        held[3] = exchange(held[1], "blk", blk, 2)
-        rows = step((1, 2, 4), (rows,))
+        rows = step((1, 2), near[:1])
         rows, held[6] = lax.optimization_barrier((rows[0], held[6]))
         held[7] = exchange(held[6], "blk", blk, 1)
-        rows = step((3, 5, 6), (rows,))
+        rows = step((3, 4, 5, 6), (rows,))
         rows = step((7,), rows, True)
         keep, send = rows
     else:

time: 24.7 us -> 26.3 us (1.065)
  waiting for transfers between devices: 2.14 us -> 6.54 us
  starting transfers between devices: 11.5 us -> 9.91 us
  Pallas kernels: 8.12 us -> 6.89 us
    ppermute x9, waiting for transfers between devices: 2.14 us -> 6.54 us  [exchange(): return lax.ppermute(value, axis, [(i, i ^ mask) for i in range(size)])]
    ppermute x9, starting transfers between devices: 11.5 us -> 9.91 us  [exchange(): return lax.ppermute(value, axis, [(i, i ^ mask) for i in range(size)])]
    pallas_call x4, Pallas kernels: 8.02 us -> 6.79 us  [score(): pl.pallas_call(functools.partial(score_kernel, taps, shifts, places, len(...]
  transfers between devices with their start and end apart: 9 -> 9, of which waited for: 3 -> 6; matrix products, arithmetic and copies ran while one was open for 0% -> 0% of each run, Pallas kernels for 28% -> 22%
where the time goes in v7:
time: 26.3 us; the launch traced here: 26.1 us
  starting transfers between devices  9.91 us (38%)
  Pallas kernels  6.89 us (26%)
  waiting for transfers between devices  6.54 us (25%)
  between operations  1.34 us (5%)
  local copies, waits for them, and re-layouts  0.84 us (3%)
  other arithmetic  0.6 us (2%)
    ppermute x9, starting transfers between devices, exchange(): return lax.ppermute(value, axis, [(i, i ^ mask) for i in range(size)])  9.91 us
    pallas_call x4, Pallas kernels, score(): pl.pallas_call(functools.partial(score_kernel, taps, shifts, places, len(...  6.79 us
    ppermute x9, waiting for transfers between devices, exchange(): return lax.ppermute(value, axis, [(i, i ^ mask) for i in range(size)])  6.54 us
    unnamed x8, local copies, waits for them, and re-layouts  0.84 us
    broadcast_in_dim x1, other arithmetic, on_device(): return (keep + exchange(send, 'chan', 2, 1))[None]  0.6 us
  transfers between devices with their start and end apart: 9, of which 6 were waited for; matrix products, arithmetic and copies ran while one was open for 0% of the time, Pallas kernels for 22%

profile of v7, /device:TPU:0, one launch (start us, length us, event | category | flops | bytes accessed | tf_op | source)
XLA Modules:
  0.0 26.1 jit_solution(17546375631983544206)
XLA Ops:
  0.0 0.5 %collective-permute-start = (bf16[191,5000]{1,0:T(8,128)(2,1)}, bf16[191,5000]{1,0:T(8,128)(2,1)S(1)}, u32[]{:S(2)}, u32[]{:S(2)}) collective-permute-start(bf16[191,5000]{1,0:T(8,128)(2,1)} %bitcast.6), channel_id=1, source_target_pairs={{0,1},{1,0},{2,3},{3,2},{4,5},{5,4},{6,7},{7,6},{8,9},{9,8},{10,11... | collective-permute-start | bytes 5730008 | tf_op jit(solution)/shard_map/ppermute | solution.py:272
  1.7 0.0 copy-start.3
  1.8 0.8 %copy-done.3 = bf16[1,256,128]{2,1,0:T(8,128)(2,1)S(1)} copy-done((bf16[1,256,128]{2,1,0:T(8,128)(2,1)S(1)}, bf16[1,256,128]{2,1,0:T(8,128)(2,1)}, u32[]{:S(2)}) %copy-start.3) | copy-done | bytes 65560
  2.6 0.0 copy-start
  2.6 0.0 copy-start.1
  2.6 0.0 copy-start.2
  2.6 0.1 pack.1
  2.7 3.7 %collective-permute-start.4 = (bf16[136,256]{1,0:T(8,128)(2,1)S(1)}, bf16[136,256]{1,0:T(8,128)(2,1)S(1)}, u32[]{:S(2)}, u32[]{:S(2)}) collective-permute-start(bf16[136,256]{1,0:T(8,128)(2,1)S(1)} %get-tuple-element.23), channel_id=1, source_target_pairs={{0,8},{2,10},{4,12},{6,14},{8,0},{10,2},{12,4},{14,6},{1,9},{3,11}... | collective-permute-start | bytes 208904 | tf_op jit(solution)/shard_map/ppermute | solution.py:272
  6.4 1.5 %collective-permute-start.3 = (bf16[136,256]{1,0:T(8,128)(2,1)S(1)}, bf16[136,256]{1,0:T(8,128)(2,1)S(1)}, u32[]{:S(2)}, u32[]{:S(2)}) collective-permute-start(bf16[136,256]{1,0:T(8,128)(2,1)S(1)} %get-tuple-element.23), channel_id=1, source_target_pairs={{0,2},{2,0},{4,6},{6,4},{8,10},{10,8},{12,14},{14,12},{1,3},{3,1},... | collective-permute-start | bytes 208904 | tf_op jit(solution)/shard_map/ppermute | solution.py:272
  7.8 1.6 %collective-permute-start.2 = (bf16[136,256]{1,0:T(8,128)(2,1)S(1)}, bf16[136,256]{1,0:T(8,128)(2,1)S(1)}, u32[]{:S(2)}, u32[]{:S(2)}) collective-permute-start(bf16[136,256]{1,0:T(8,128)(2,1)S(1)} %get-tuple-element.23), channel_id=1, source_target_pairs={{0,4},{2,6},{4,0},{6,2},{8,12},{10,14},{12,8},{14,10},{1,5},{3,7},... | collective-permute-start | bytes 208904 | tf_op jit(solution)/shard_map/ppermute | solution.py:272
  9.4 0.4 %collective-permute-start.1 = (bf16[136,256]{1,0:T(8,128)(2,1)S(1)}, bf16[136,256]{1,0:T(8,128)(2,1)S(1)}, u32[]{:S(2)}, u32[]{:S(2)}) collective-permute-start(bf16[136,256]{1,0:T(8,128)(2,1)S(1)} %get-tuple-element.23), channel_id=1, source_target_pairs={{0,6},{2,4},{4,2},{6,0},{8,14},{10,12},{12,10},{14,8},{1,7},{3,5},... | collective-permute-start | bytes 208904 | tf_op jit(solution)/shard_map/ppermute | solution.py:272
  9.8 0.0 collective-permute-done.refs_1_
  9.8 0.0 copy-done
  9.8 0.0 copy-done.1
  9.9 0.0 copy-done.2
  9.9 1.0 %score.4 = (f32[8,64]{1,0:T(8,128)S(1)}, bf16[624,192]{1,0:T(8,128)(2,1)S(1)}, bf16[192,208]{1,0:T(8,128)(2,1)S(1)}) custom-call(bf16[191,5000]{1,0:T(8,128)(2,1)S(1)} %bitcast.7, bf16[191,5000]{1,0:T(8,128)(2,1)S(1)} %collective-permute-done.refs_1_, f32[208,192]{1,0:T(8,128)S(1)} %copy-done.1, f32[64,208]{1,0:T(8,128)S(1)} %copy-done.2, ...), custom_call_target="tpu_custom_call" | custom-call | flops 4194304 | bytes 195584 | tf_op jit(solution)/shard_map/score/pallas_call | solution.py:249
  10.8 0.0 collective-permute-done.4.refs_5_
  10.8 0.0 collective-permute-done.3.refs_4_
  10.8 1.8 %collective-permute-done.2.refs_5_ = bf16[136,256]{1,0:T(8,128)(2,1)S(1)} collective-permute-done((bf16[136,256]{1,0:T(8,128)(2,1)S(1)}, bf16[136,256]{1,0:T(8,128)(2,1)S(1)}, u32[]{:S(2)}, u32[]{:S(2)}) %collective-permute-start.2) | collective-permute-done | bytes 69664 | tf_op jit(solution)/shard_map/ppermute | solution.py:272
  12.7 2.0 %collective-permute-done.1.refs_4_ = bf16[136,256]{1,0:T(8,128)(2,1)S(1)} collective-permute-done((bf16[136,256]{1,0:T(8,128)(2,1)S(1)}, bf16[136,256]{1,0:T(8,128)(2,1)S(1)}, u32[]{:S(2)}, u32[]{:S(2)}) %collective-permute-start.1) | collective-permute-done | bytes 69664 | tf_op jit(solution)/shard_map/ppermute | solution.py:272
  14.6 0.6 %collective-permute-start.5 = (bf16[136,256]{1,0:T(8,128)(2,1)S(1)}, bf16[136,256]{1,0:T(8,128)(2,1)S(1)}, u32[]{:S(2)}, u32[]{:S(2)}) collective-permute-start(bf16[136,256]{1,0:T(8,128)(2,1)S(1)} %collective-permute-done.4.refs_5_), channel_id=1, source_target_pairs={{0,4},{2,6},{4,0},{6,2},{8,12},{10,14},{12,8},{14,10},{1,5},{3,7},... | collective-permute-start | bytes 208904 | tf_op jit(solution)/shard_map/ppermute | solution.py:272
  15.2 1.2 %collective-permute-start.7 = (bf16[136,256]{1,0:T(8,128)(2,1)S(1)}, bf16[136,256]{1,0:T(8,128)(2,1)S(1)}, u32[]{:S(2)}, u32[]{:S(2)}) collective-permute-start(bf16[136,256]{1,0:T(8,128)(2,1)S(1)} %collective-permute-done.4.refs_5_), channel_id=1, source_target_pairs={{0,2},{2,0},{4,6},{6,4},{8,10},{10,8},{12,14},{14,12},{1,3},{3,1},... | collective-permute-start | bytes 208904 | tf_op jit(solution)/shard_map/ppermute | solution.py:272
  16.4 1.7 %score.5.refs_8_ = f32[8,64]{1,0:T(8,128)S(1)} custom-call(bf16[191,5000]{1,0:T(8,128)(2,1)S(1)} %bitcast.8, bf16[191,5000]{1,0:T(8,128)(2,1)S(1)} %collective-permute-done.refs_1_, bf16[624,192]{1,0:T(8,128)(2,1)S(1)} %get-tuple-element.20.refs_2_, bf16[192,208]{1,0:T(8,128)(2,1)S(1)} %get-tuple-element.21.refs_3_, ...), custom_call_target="tpu_custom_call" | custom-call | flops 8388608 | bytes 391168 | tf_op jit(solution)/shard_map/score/pallas_call | solution.py:249
  18.1 0.8 %collective-permute-done.5.refs_7_ = bf16[136,256]{1,0:T(8,128)(2,1)S(1)} collective-permute-done((bf16[136,256]{1,0:T(8,128)(2,1)S(1)}, bf16[136,256]{1,0:T(8,128)(2,1)S(1)}, u32[]{:S(2)}, u32[]{:S(2)}) %collective-permute-start.5) | collective-permute-done | bytes 69664 | tf_op jit(solution)/shard_map/ppermute | solution.py:272
  18.9 0.5 %collective-permute-start.6 = (bf16[136,256]{1,0:T(8,128)(2,1)S(1)}, bf16[136,256]{1,0:T(8,128)(2,1)S(1)}, u32[]{:S(2)}, u32[]{:S(2)}) collective-permute-start(bf16[136,256]{1,0:T(8,128)(2,1)S(1)} %collective-permute-done.5.refs_7_), channel_id=1, source_target_pairs={{0,2},{2,0},{4,6},{6,4},{8,10},{10,8},{12,14},{14,12},{1,3},{3,1},... | collective-permute-start | bytes 208904 | tf_op jit(solution)/shard_map/ppermute | solution.py:272
  19.5 0.5 %collective-permute-done.7.refs_6_ = bf16[136,256]{1,0:T(8,128)(2,1)S(1)} collective-permute-done((bf16[136,256]{1,0:T(8,128)(2,1)S(1)}, bf16[136,256]{1,0:T(8,128)(2,1)S(1)}, u32[]{:S(2)}, u32[]{:S(2)}) %collective-permute-start.7) | collective-permute-done | bytes 69664 | tf_op jit(solution)/shard_map/ppermute | solution.py:272
  20.0 3.1 %score.6.refs_5_ = f32[8,64]{1,0:T(8,128)S(1)} custom-call(bf16[191,5000]{1,0:T(8,128)(2,1)S(1)} %bitcast.9, bf16[191,5000]{1,0:T(8,128)(2,1)S(1)} %collective-permute-done.refs_1_, bf16[624,192]{1,0:T(8,128)(2,1)S(1)} %get-tuple-element.20.refs_2_, bf16[192,208]{1,0:T(8,128)(2,1)S(1)} %get-tuple-element.21.refs_3_, ...), custom_call_target="tpu_custom_call" | custom-call | flops 16777216 | bytes 782336 | tf_op jit(solution)/shard_map/score/pallas_call | solution.py:249
  23.1 0.2 collective-permute-done.6.refs_4_
  23.3 1.1 %score.7 = (f32[8,32]{1,0:T(8,128)S(1)}, f32[8,32]{1,0:T(8,128)S(1)}) custom-call(bf16[191,5000]{1,0:T(8,128)(2,1)S(1)} %bitcast.10, bf16[191,5000]{1,0:T(8,128)(2,1)S(1)} %collective-permute-done.refs_1_, bf16[624,192]{1,0:T(8,128)(2,1)S(1)} %get-tuple-element.20.refs_2_, bf16[192,208]{1,0:T(8,128)(2,1)S(1)} %get-tuple-element.21.refs_3_, ...), custom_call_target="tpu_custom_call" | custom-call | flops 4194304 | bytes 195584 | tf_op jit(solution)/shard_map/score/pallas_call | solution.py:249
  24.3 0.0 collective-permute-start.8
  24.3 1.2 %collective-permute-done.8 = f32[8,32]{1,0:T(8,128)S(1)} collective-permute-done((f32[8,32]{1,0:T(8,128)S(1)}, f32[8,32]{1,0:T(8,128)S(1)}, u32[]{:S(2)}, u32[]{:S(2)}) %collective-permute-start.8) | collective-permute-done | bytes 1056 | tf_op jit(solution)/shard_map/ppermute | solution.py:272
  25.5 0.6 %add_bitcast_fusion = f32[1,8,32]{2,1,0:T(8,128)} fusion(f32[8,32]{1,0:T(8,128)S(1)} %get-tuple-element.31, f32[8,32]{1,0:T(8,128)S(1)} %collective-permute-done.8), kind=kLoop, calls=%fused_computation | loop fusion | flops 256 | bytes 3072 | tf_op jit(solution)/shard_map/broadcast_in_dim | solution.py:320
Async XLA Ops:
  0.0 9.8 %collective-permute-start = (bf16[191,5000]{1,0:T(8,128)(2,1)}, bf16[191,5000]{1,0:T(8,128)(2,1)S(1)}, u32[]{:S(2)}, u32[]{:S(2)}) collective-permute-start(bf16[191,5000]{1,0:T(8,128)(2,1)} %bitcast.6), channel_id=1, source_target_pairs={{0,1},{1,0},{2,3},{3,2},{4,5},{5,4},{6,7},{7,6},{8,9},{9,8},{10,11... | collective-permute-start | bytes 5730008 | tf_op jit(solution)/shard_map/ppermute | solution.py:272
  1.7 0.8 %copy-start.3 = (bf16[1,256,128]{2,1,0:T(8,128)(2,1)S(1)}, bf16[1,256,128]{2,1,0:T(8,128)(2,1)}, u32[]{:S(2)}) copy-start(bf16[1,256,128]{2,1,0:T(8,128)(2,1)} %param.7) | copy-start | bytes 196612
  2.6 7.3 %copy-start = (bf16[1,5000,191]{1,2,0:T(8,128)(2,1)S(1)}, bf16[1,5000,191]{1,2,0:T(8,128)(2,1)}, u32[]{:S(2)}) copy-start(bf16[1,5000,191]{1,2,0:T(8,128)(2,1)} %param.6) | copy-start | bytes 5730004
  2.6 7.3 %copy-start.1 = (f32[208,192]{1,0:T(8,128)S(1)}, f32[208,192]{1,0:T(8,128)}, u32[]{:S(2)}) copy-start(f32[208,192]{1,0:T(8,128)} %constant.4.clone.refs_2_) | copy-start | bytes 479236
  2.6 7.3 %copy-start.2 = (f32[64,208]{1,0:T(8,128)S(1)}, f32[64,208]{1,0:T(8,128)}, u32[]{:S(2)}) copy-start(f32[64,208]{1,0:T(8,128)} %constant.5.clone.refs_3_) | copy-start | bytes 159748
  2.7 8.1 %collective-permute-start.4 = (bf16[136,256]{1,0:T(8,128)(2,1)S(1)}, bf16[136,256]{1,0:T(8,128)(2,1)S(1)}, u32[]{:S(2)}, u32[]{:S(2)}) collective-permute-start(bf16[136,256]{1,0:T(8,128)(2,1)S(1)} %get-tuple-element.23), channel_id=1, source_target_pairs={{0,8},{2,10},{4,12},{6,14},{8,0},{10,2},{12,4},{14,6},{1,9},{3,11}... | collective-permute-start | bytes 208904 | tf_op jit(solution)/shard_map/ppermute | solution.py:272
  6.4 4.5 %collective-permute-start.3 = (bf16[136,256]{1,0:T(8,128)(2,1)S(1)}, bf16[136,256]{1,0:T(8,128)(2,1)S(1)}, u32[]{:S(2)}, u32[]{:S(2)}) collective-permute-start(bf16[136,256]{1,0:T(8,128)(2,1)S(1)} %get-tuple-element.23), channel_id=1, source_target_pairs={{0,2},{2,0},{4,6},{6,4},{8,10},{10,8},{12,14},{14,12},{1,3},{3,1},... | collective-permute-start | bytes 208904 | tf_op jit(solution)/shard_map/ppermute | solution.py:272
  7.8 4.8 %collective-permute-start.2 = (bf16[136,256]{1,0:T(8,128)(2,1)S(1)}, bf16[136,256]{1,0:T(8,128)(2,1)S(1)}, u32[]{:S(2)}, u32[]{:S(2)}) collective-permute-start(bf16[136,256]{1,0:T(8,128)(2,1)S(1)} %get-tuple-element.23), channel_id=1, source_target_pairs={{0,4},{2,6},{4,0},{6,2},{8,12},{10,14},{12,8},{14,10},{1,5},{3,7},... | collective-permute-start | bytes 208904 | tf_op jit(solution)/shard_map/ppermute | solution.py:272
  9.4 5.2 %collective-permute-start.1 = (bf16[136,256]{1,0:T(8,128)(2,1)S(1)}, bf16[136,256]{1,0:T(8,128)(2,1)S(1)}, u32[]{:S(2)}, u32[]{:S(2)}) collective-permute-start(bf16[136,256]{1,0:T(8,128)(2,1)S(1)} %get-tuple-element.23), channel_id=1, source_target_pairs={{0,6},{2,4},{4,2},{6,0},{8,14},{10,12},{12,10},{14,8},{1,7},{3,5},... | collective-permute-start | bytes 208904 | tf_op jit(solution)/shard_map/ppermute | solution.py:272
  14.6 4.3 %collective-permute-start.5 = (bf16[136,256]{1,0:T(8,128)(2,1)S(1)}, bf16[136,256]{1,0:T(8,128)(2,1)S(1)}, u32[]{:S(2)}, u32[]{:S(2)}) collective-permute-start(bf16[136,256]{1,0:T(8,128)(2,1)S(1)} %collective-permute-done.4.refs_5_), channel_id=1, source_target_pairs={{0,4},{2,6},{4,0},{6,2},{8,12},{10,14},{12,8},{14,10},{1,5},{3,7},... | collective-permute-start | bytes 208904 | tf_op jit(solution)/shard_map/ppermute | solution.py:272
  15.2 4.8 %collective-permute-start.7 = (bf16[136,256]{1,0:T(8,128)(2,1)S(1)}, bf16[136,256]{1,0:T(8,128)(2,1)S(1)}, u32[]{:S(2)}, u32[]{:S(2)}) collective-permute-start(bf16[136,256]{1,0:T(8,128)(2,1)S(1)} %collective-permute-done.4.refs_5_), channel_id=1, source_target_pairs={{0,2},{2,0},{4,6},{6,4},{8,10},{10,8},{12,14},{14,12},{1,3},{3,1},... | collective-permute-start | bytes 208904 | tf_op jit(solution)/shard_map/ppermute | solution.py:272
  18.9 4.3 %collective-permute-start.6 = (bf16[136,256]{1,0:T(8,128)(2,1)S(1)}, bf16[136,256]{1,0:T(8,128)(2,1)S(1)}, u32[]{:S(2)}, u32[]{:S(2)}) collective-permute-start(bf16[136,256]{1,0:T(8,128)(2,1)S(1)} %collective-permute-done.5.refs_7_), channel_id=1, source_target_pairs={{0,2},{2,0},{4,6},{6,4},{8,10},{10,8},{12,14},{14,12},{1,3},{3,1},... | collective-permute-start | bytes 208904 | tf_op jit(solution)/shard_map/ppermute | solution.py:272
  24.3 1.2 %collective-permute-start.8 = (f32[8,32]{1,0:T(8,128)S(1)}, f32[8,32]{1,0:T(8,128)S(1)}, u32[]{:S(2)}, u32[]{:S(2)}) collective-permute-start(f32[8,32]{1,0:T(8,128)S(1)} %get-tuple-element.32), channel_id=1, source_target_pairs={{0,1},{1,0},{2,3},{3,2},{4,5},{5,4},{6,7},{7,6},{8,9},{9,8},{10,11... | collective-permute-start | bytes 3080 | tf_op jit(solution)/shard_map/ppermute | solution.py:272

commit v8 on v7

--- a/solution.py
+++ b/solution.py
@@ -282,7 +282,7 @@
     tables = tuple(jnp.asarray(table) for table in fourier_tables(period, shifts))
     if blk == CHUNK:
         held = {0: own}
-        for mask in (4, 1, 2, 3):
+        for mask in (4, 1, 2):
             held[mask] = exchange(packed, "blk", blk, mask)
         theirs = exchange(mine, "chan", 2, 1)
 
@@ -294,15 +294,14 @@
 
         *rows, forward, inverse = step((0,), (), split=True)
         tables = (forward, inverse)
-        near = lax.optimization_barrier((rows[0], *(held[m] for m in (3, 2, 1, 4))))
-        held.update(zip((3, 2, 1, 4), near[1:]))
+        near = lax.optimization_barrier((rows[0], *(held[m] for m in (4, 1, 2))))
+        held.update(zip((4, 1, 2), near[1:]))
         held[6] = exchange(held[4], "blk", blk, 2)
         held[5] = exchange(held[4], "blk", blk, 1)
-        rows = step((1, 2), near[:1])
-        rows, held[6] = lax.optimization_barrier((rows[0], held[6]))
+        held[3] = exchange(held[1], "blk", blk, 2)
         held[7] = exchange(held[6], "blk", blk, 1)
-        rows = step((3, 4, 5, 6), (rows,))
-        rows = step((7,), rows, True)
+        rows = step((1, 2, 4, 5, 6), near[:1])
+        rows = step((3, 7), rows, True)
         keep, send = rows
     else:
         theirs = exchange(mine, "chan", 2, 1)

time: 26.3 us -> 26 us (0.989)
  starting transfers between devices: 9.91 us -> 10.8 us
  waiting for transfers between devices: 6.54 us -> 5.72 us
  Pallas kernels: 6.89 us -> 6.51 us
    ppermute x9, starting transfers between devices: 9.91 us -> 10.8 us  [exchange(): return lax.ppermute(value, axis, [(i, i ^ mask) for i in range(size)])]
    ppermute x9, waiting for transfers between devices: 6.54 us -> 5.72 us  [exchange(): return lax.ppermute(value, axis, [(i, i ^ mask) for i in range(size)])]
    pallas_call x4 -> x3, Pallas kernels: 6.79 us -> 6.42 us  [score(): pl.pallas_call(functools.partial(score_kernel, taps, shifts, places, len(...]
  transfers between devices with their start and end apart: 9 -> 9, of which waited for: 6 -> 5; matrix products, arithmetic and copies ran while one was open for 0% -> 0% of each run, Pallas kernels for 22% -> 18%
where the time goes in v8:
time: 26 us; the launch traced here: 25.8 us
  starting transfers between devices  10.8 us (42%)
  Pallas kernels  6.51 us (25%)
  waiting for transfers between devices  5.72 us (22%)
  between operations  1.34 us (5%)
  local copies, waits for them, and re-layouts  0.84 us (3%)
  other arithmetic  0.6 us (2%)
    ppermute x9, starting transfers between devices, exchange(): return lax.ppermute(value, axis, [(i, i ^ mask) for i in range(size)])  10.8 us
    pallas_call x3, Pallas kernels, score(): pl.pallas_call(functools.partial(score_kernel, taps, shifts, places, len(...  6.42 us
    ppermute x9, waiting for transfers between devices, exchange(): return lax.ppermute(value, axis, [(i, i ^ mask) for i in range(size)])  5.72 us
    unnamed x8, local copies, waits for them, and re-layouts  0.84 us
    broadcast_in_dim x1, other arithmetic, on_device(): return (keep + exchange(send, 'chan', 2, 1))[None]  0.6 us
  transfers between devices with their start and end apart: 9, of which 5 were waited for; matrix products, arithmetic and copies ran while one was open for 0% of the time, Pallas kernels for 18%

profile of v8, /device:TPU:0, one launch (start us, length us, event | category | flops | bytes accessed | tf_op | source)
XLA Modules:
  0.0 25.8 jit_solution(17976189677857177687)
XLA Ops:
  0.0 0.5 %collective-permute-start = (bf16[191,5000]{1,0:T(8,128)(2,1)}, bf16[191,5000]{1,0:T(8,128)(2,1)S(1)}, u32[]{:S(2)}, u32[]{:S(2)}) collective-permute-start(bf16[191,5000]{1,0:T(8,128)(2,1)} %bitcast.6), channel_id=1, source_target_pairs={{0,1},{1,0},{2,3},{3,2},{4,5},{5,4},{6,7},{7,6},{8,9},{9,8},{10,11... | collective-permute-start | bytes 5730008 | tf_op jit(solution)/shard_map/ppermute | solution.py:272
  1.7 0.0 copy-start.3
  1.8 0.8 %copy-done.3 = bf16[1,256,128]{2,1,0:T(8,128)(2,1)S(1)} copy-done((bf16[1,256,128]{2,1,0:T(8,128)(2,1)S(1)}, bf16[1,256,128]{2,1,0:T(8,128)(2,1)}, u32[]{:S(2)}) %copy-start.3) | copy-done | bytes 65560
  2.6 0.0 copy-start
  2.6 0.0 copy-start.1
  2.6 0.0 copy-start.2
  2.6 0.1 pack.1
  2.7 3.7 %collective-permute-start.1 = (bf16[136,256]{1,0:T(8,128)(2,1)S(1)}, bf16[136,256]{1,0:T(8,128)(2,1)S(1)}, u32[]{:S(2)}, u32[]{:S(2)}) collective-permute-start(bf16[136,256]{1,0:T(8,128)(2,1)S(1)} %get-tuple-element.20), channel_id=1, source_target_pairs={{0,8},{2,10},{4,12},{6,14},{8,0},{10,2},{12,4},{14,6},{1,9},{3,11}... | collective-permute-start | bytes 208904 | tf_op jit(solution)/shard_map/ppermute | solution.py:272
  6.4 1.5 %collective-permute-start.2 = (bf16[136,256]{1,0:T(8,128)(2,1)S(1)}, bf16[136,256]{1,0:T(8,128)(2,1)S(1)}, u32[]{:S(2)}, u32[]{:S(2)}) collective-permute-start(bf16[136,256]{1,0:T(8,128)(2,1)S(1)} %get-tuple-element.20), channel_id=1, source_target_pairs={{0,2},{2,0},{4,6},{6,4},{8,10},{10,8},{12,14},{14,12},{1,3},{3,1},... | collective-permute-start | bytes 208904 | tf_op jit(solution)/shard_map/ppermute | solution.py:272
  7.8 1.6 %collective-permute-start.3 = (bf16[136,256]{1,0:T(8,128)(2,1)S(1)}, bf16[136,256]{1,0:T(8,128)(2,1)S(1)}, u32[]{:S(2)}, u32[]{:S(2)}) collective-permute-start(bf16[136,256]{1,0:T(8,128)(2,1)S(1)} %get-tuple-element.20), channel_id=1, source_target_pairs={{0,4},{2,6},{4,0},{6,2},{8,12},{10,14},{12,8},{14,10},{1,5},{3,7},... | collective-permute-start | bytes 208904 | tf_op jit(solution)/shard_map/ppermute | solution.py:272
  9.4 0.0 collective-permute-done.refs_1_
  9.4 0.0 copy-done
  9.4 0.0 copy-done.1
  9.4 0.0 copy-done.2
  9.4 0.9 %score.3 = (f32[8,64]{1,0:T(8,128)S(1)}, bf16[624,192]{1,0:T(8,128)(2,1)S(1)}, bf16[192,208]{1,0:T(8,128)(2,1)S(1)}) custom-call(bf16[191,5000]{1,0:T(8,128)(2,1)S(1)} %bitcast.7, bf16[191,5000]{1,0:T(8,128)(2,1)S(1)} %collective-permute-done.refs_1_, f32[208,192]{1,0:T(8,128)S(1)} %copy-done.1, f32[64,208]{1,0:T(8,128)S(1)} %copy-done.2, ...), custom_call_target="tpu_custom_call" | custom-call | flops 4194304 | bytes 195584 | tf_op jit(solution)/shard_map/score/pallas_call | solution.py:249
  10.4 0.4 %collective-permute-done.1.refs_6_ = bf16[136,256]{1,0:T(8,128)(2,1)S(1)} collective-permute-done((bf16[136,256]{1,0:T(8,128)(2,1)S(1)}, bf16[136,256]{1,0:T(8,128)(2,1)S(1)}, u32[]{:S(2)}, u32[]{:S(2)}) %collective-permute-start.1) | collective-permute-done | bytes 69664 | tf_op jit(solution)/shard_map/ppermute | solution.py:272
  10.8 0.0 collective-permute-done.2.refs_4_
  10.8 1.3 %collective-permute-done.3.refs_5_ = bf16[136,256]{1,0:T(8,128)(2,1)S(1)} collective-permute-done((bf16[136,256]{1,0:T(8,128)(2,1)S(1)}, bf16[136,256]{1,0:T(8,128)(2,1)S(1)}, u32[]{:S(2)}, u32[]{:S(2)}) %collective-permute-start.3) | collective-permute-done | bytes 69664 | tf_op jit(solution)/shard_map/ppermute | solution.py:272
  12.2 1.6 %collective-permute-start.5 = (bf16[136,256]{1,0:T(8,128)(2,1)S(1)}, bf16[136,256]{1,0:T(8,128)(2,1)S(1)}, u32[]{:S(2)}, u32[]{:S(2)}) collective-permute-start(bf16[136,256]{1,0:T(8,128)(2,1)S(1)} %collective-permute-done.1.refs_6_), channel_id=1, source_target_pairs={{0,4},{2,6},{4,0},{6,2},{8,12},{10,14},{12,8},{14,10},{1,5},{3,7},... | collective-permute-start | bytes 208904 | tf_op jit(solution)/shard_map/ppermute | solution.py:272
  13.7 0.5 %collective-permute-start.7 = (bf16[136,256]{1,0:T(8,128)(2,1)S(1)}, bf16[136,256]{1,0:T(8,128)(2,1)S(1)}, u32[]{:S(2)}, u32[]{:S(2)}) collective-permute-start(bf16[136,256]{1,0:T(8,128)(2,1)S(1)} %collective-permute-done.1.refs_6_), channel_id=1, source_target_pairs={{0,2},{2,0},{4,6},{6,4},{8,10},{10,8},{12,14},{14,12},{1,3},{3,1},... | collective-permute-start | bytes 208904 | tf_op jit(solution)/shard_map/ppermute | solution.py:272
  14.3 0.6 %collective-permute-start.4 = (bf16[136,256]{1,0:T(8,128)(2,1)S(1)}, bf16[136,256]{1,0:T(8,128)(2,1)S(1)}, u32[]{:S(2)}, u32[]{:S(2)}) collective-permute-start(bf16[136,256]{1,0:T(8,128)(2,1)S(1)} %collective-permute-done.2.refs_4_), channel_id=1, source_target_pairs={{0,4},{2,6},{4,0},{6,2},{8,12},{10,14},{12,8},{14,10},{1,5},{3,7},... | collective-permute-start | bytes 208904 | tf_op jit(solution)/shard_map/ppermute | solution.py:272
  14.9 2.0 %collective-permute-done.5.refs_8_ = bf16[136,256]{1,0:T(8,128)(2,1)S(1)} collective-permute-done((bf16[136,256]{1,0:T(8,128)(2,1)S(1)}, bf16[136,256]{1,0:T(8,128)(2,1)S(1)}, u32[]{:S(2)}, u32[]{:S(2)}) %collective-permute-start.5) | collective-permute-done | bytes 69664 | tf_op jit(solution)/shard_map/ppermute | solution.py:272
  16.9 0.9 %collective-permute-start.6 = (bf16[136,256]{1,0:T(8,128)(2,1)S(1)}, bf16[136,256]{1,0:T(8,128)(2,1)S(1)}, u32[]{:S(2)}, u32[]{:S(2)}) collective-permute-start(bf16[136,256]{1,0:T(8,128)(2,1)S(1)} %collective-permute-done.5.refs_8_), channel_id=1, source_target_pairs={{0,2},{2,0},{4,6},{6,4},{8,10},{10,8},{12,14},{14,12},{1,3},{3,1},... | collective-permute-start | bytes 208904 | tf_op jit(solution)/shard_map/ppermute | solution.py:272
  17.7 0.7 %collective-permute-done.7.refs_7_ = bf16[136,256]{1,0:T(8,128)(2,1)S(1)} collective-permute-done((bf16[136,256]{1,0:T(8,128)(2,1)S(1)}, bf16[136,256]{1,0:T(8,128)(2,1)S(1)}, u32[]{:S(2)}, u32[]{:S(2)}) %collective-permute-start.7) | collective-permute-done | bytes 69664 | tf_op jit(solution)/shard_map/ppermute | solution.py:272
  18.5 3.6 %score.4.refs_6_ = f32[8,64]{1,0:T(8,128)S(1)} custom-call(bf16[191,5000]{1,0:T(8,128)(2,1)S(1)} %bitcast.8, bf16[191,5000]{1,0:T(8,128)(2,1)S(1)} %collective-permute-done.refs_1_, bf16[624,192]{1,0:T(8,128)(2,1)S(1)} %get-tuple-element.17.refs_2_, bf16[192,208]{1,0:T(8,128)(2,1)S(1)} %get-tuple-element.18.refs_3_, ...), custom_call_target="tpu_custom_call" | custom-call | flops 20971520 | bytes 977920 | tf_op jit(solution)/shard_map/score/pallas_call | solution.py:249
  22.1 0.0 collective-permute-done.4.refs_4_
  22.1 0.0 collective-permute-done.6.refs_5_
  22.1 1.8 %score.5 = (f32[8,32]{1,0:T(8,128)S(1)}, f32[8,32]{1,0:T(8,128)S(1)}) custom-call(bf16[191,5000]{1,0:T(8,128)(2,1)S(1)} %bitcast.9, bf16[191,5000]{1,0:T(8,128)(2,1)S(1)} %collective-permute-done.refs_1_, bf16[624,192]{1,0:T(8,128)(2,1)S(1)} %get-tuple-element.17.refs_2_, bf16[192,208]{1,0:T(8,128)(2,1)S(1)} %get-tuple-element.18.refs_3_, ...), custom_call_target="tpu_custom_call" | custom-call | flops 8388608 | bytes 391168 | tf_op jit(solution)/shard_map/score/pallas_call | solution.py:249
  24.0 0.0 collective-permute-start.8
  24.0 1.2 %collective-permute-done.8 = f32[8,32]{1,0:T(8,128)S(1)} collective-permute-done((f32[8,32]{1,0:T(8,128)S(1)}, f32[8,32]{1,0:T(8,128)S(1)}, u32[]{:S(2)}, u32[]{:S(2)}) %collective-permute-start.8) | collective-permute-done | bytes 1056 | tf_op jit(solution)/shard_map/ppermute | solution.py:272
  25.2 0.6 %add_bitcast_fusion = f32[1,8,32]{2,1,0:T(8,128)} fusion(f32[8,32]{1,0:T(8,128)S(1)} %get-tuple-element.25, f32[8,32]{1,0:T(8,128)S(1)} %collective-permute-done.8), kind=kLoop, calls=%fused_computation | loop fusion | flops 256 | bytes 3072 | tf_op jit(solution)/shard_map/broadcast_in_dim | solution.py:319
Async XLA Ops:
  0.0 9.4 %collective-permute-start = (bf16[191,5000]{1,0:T(8,128)(2,1)}, bf16[191,5000]{1,0:T(8,128)(2,1)S(1)}, u32[]{:S(2)}, u32[]{:S(2)}) collective-permute-start(bf16[191,5000]{1,0:T(8,128)(2,1)} %bitcast.6), channel_id=1, source_target_pairs={{0,1},{1,0},{2,3},{3,2},{4,5},{5,4},{6,7},{7,6},{8,9},{9,8},{10,11... | collective-permute-start | bytes 5730008 | tf_op jit(solution)/shard_map/ppermute | solution.py:272
  1.7 0.8 %copy-start.3 = (bf16[1,256,128]{2,1,0:T(8,128)(2,1)S(1)}, bf16[1,256,128]{2,1,0:T(8,128)(2,1)}, u32[]{:S(2)}) copy-start(bf16[1,256,128]{2,1,0:T(8,128)(2,1)} %param.7) | copy-start | bytes 196612
  2.6 6.8 %copy-start = (bf16[1,5000,191]{1,2,0:T(8,128)(2,1)S(1)}, bf16[1,5000,191]{1,2,0:T(8,128)(2,1)}, u32[]{:S(2)}) copy-start(bf16[1,5000,191]{1,2,0:T(8,128)(2,1)} %param.6) | copy-start | bytes 5730004
  2.6 6.8 %copy-start.1 = (f32[208,192]{1,0:T(8,128)S(1)}, f32[208,192]{1,0:T(8,128)}, u32[]{:S(2)}) copy-start(f32[208,192]{1,0:T(8,128)} %constant.4.clone.refs_2_) | copy-start | bytes 479236
  2.6 6.8 %copy-start.2 = (f32[64,208]{1,0:T(8,128)S(1)}, f32[64,208]{1,0:T(8,128)}, u32[]{:S(2)}) copy-start(f32[64,208]{1,0:T(8,128)} %constant.5.clone.refs_3_) | copy-start | bytes 159748
  2.7 8.1 %collective-permute-start.1 = (bf16[136,256]{1,0:T(8,128)(2,1)S(1)}, bf16[136,256]{1,0:T(8,128)(2,1)S(1)}, u32[]{:S(2)}, u32[]{:S(2)}) collective-permute-start(bf16[136,256]{1,0:T(8,128)(2,1)S(1)} %get-tuple-element.20), channel_id=1, source_target_pairs={{0,8},{2,10},{4,12},{6,14},{8,0},{10,2},{12,4},{14,6},{1,9},{3,11}... | collective-permute-start | bytes 208904 | tf_op jit(solution)/shard_map/ppermute | solution.py:272
  6.4 4.5 %collective-permute-start.2 = (bf16[136,256]{1,0:T(8,128)(2,1)S(1)}, bf16[136,256]{1,0:T(8,128)(2,1)S(1)}, u32[]{:S(2)}, u32[]{:S(2)}) collective-permute-start(bf16[136,256]{1,0:T(8,128)(2,1)S(1)} %get-tuple-element.20), channel_id=1, source_target_pairs={{0,2},{2,0},{4,6},{6,4},{8,10},{10,8},{12,14},{14,12},{1,3},{3,1},... | collective-permute-start | bytes 208904 | tf_op jit(solution)/shard_map/ppermute | solution.py:272
  7.8 4.3 %collective-permute-start.3 = (bf16[136,256]{1,0:T(8,128)(2,1)S(1)}, bf16[136,256]{1,0:T(8,128)(2,1)S(1)}, u32[]{:S(2)}, u32[]{:S(2)}) collective-permute-start(bf16[136,256]{1,0:T(8,128)(2,1)S(1)} %get-tuple-element.20), channel_id=1, source_target_pairs={{0,4},{2,6},{4,0},{6,2},{8,12},{10,14},{12,8},{14,10},{1,5},{3,7},... | collective-permute-start | bytes 208904 | tf_op jit(solution)/shard_map/ppermute | solution.py:272
  12.2 4.7 %collective-permute-start.5 = (bf16[136,256]{1,0:T(8,128)(2,1)S(1)}, bf16[136,256]{1,0:T(8,128)(2,1)S(1)}, u32[]{:S(2)}, u32[]{:S(2)}) collective-permute-start(bf16[136,256]{1,0:T(8,128)(2,1)S(1)} %collective-permute-done.1.refs_6_), channel_id=1, source_target_pairs={{0,4},{2,6},{4,0},{6,2},{8,12},{10,14},{12,8},{14,10},{1,5},{3,7},... | collective-permute-start | bytes 208904 | tf_op jit(solution)/shard_map/ppermute | solution.py:272
  13.7 4.7 %collective-permute-start.7 = (bf16[136,256]{1,0:T(8,128)(2,1)S(1)}, bf16[136,256]{1,0:T(8,128)(2,1)S(1)}, u32[]{:S(2)}, u32[]{:S(2)}) collective-permute-start(bf16[136,256]{1,0:T(8,128)(2,1)S(1)} %collective-permute-done.1.refs_6_), channel_id=1, source_target_pairs={{0,2},{2,0},{4,6},{6,4},{8,10},{10,8},{12,14},{14,12},{1,3},{3,1},... | collective-permute-start | bytes 208904 | tf_op jit(solution)/shard_map/ppermute | solution.py:272
  14.3 7.8 %collective-permute-start.4 = (bf16[136,256]{1,0:T(8,128)(2,1)S(1)}, bf16[136,256]{1,0:T(8,128)(2,1)S(1)}, u32[]{:S(2)}, u32[]{:S(2)}) collective-permute-start(bf16[136,256]{1,0:T(8,128)(2,1)S(1)} %collective-permute-done.2.refs_4_), channel_id=1, source_target_pairs={{0,4},{2,6},{4,0},{6,2},{8,12},{10,14},{12,8},{14,10},{1,5},{3,7},... | collective-permute-start | bytes 208904 | tf_op jit(solution)/shard_map/ppermute | solution.py:272
  16.9 5.2 %collective-permute-start.6 = (bf16[136,256]{1,0:T(8,128)(2,1)S(1)}, bf16[136,256]{1,0:T(8,128)(2,1)S(1)}, u32[]{:S(2)}, u32[]{:S(2)}) collective-permute-start(bf16[136,256]{1,0:T(8,128)(2,1)S(1)} %collective-permute-done.5.refs_8_), channel_id=1, source_target_pairs={{0,2},{2,0},{4,6},{6,4},{8,10},{10,8},{12,14},{14,12},{1,3},{3,1},... | collective-permute-start | bytes 208904 | tf_op jit(solution)/shard_map/ppermute | solution.py:272
  24.0 1.2 %collective-permute-start.8 = (f32[8,32]{1,0:T(8,128)S(1)}, f32[8,32]{1,0:T(8,128)S(1)}, u32[]{:S(2)}, u32[]{:S(2)}) collective-permute-start(f32[8,32]{1,0:T(8,128)S(1)} %get-tuple-element.26), channel_id=1, source_target_pairs={{0,1},{1,0},{2,3},{3,2},{4,5},{5,4},{6,7},{7,6},{8,9},{9,8},{10,11... | collective-permute-start | bytes 3080 | tf_op jit(solution)/shard_map/ppermute | solution.py:272

commit v9 on v7

--- a/solution.py
+++ b/solution.py
@@ -282,8 +282,7 @@
     tables = tuple(jnp.asarray(table) for table in fourier_tables(period, shifts))
     if blk == CHUNK:
         held = {0: own}
-        for mask in (4, 1, 2, 3):
-            held[mask] = exchange(packed, "blk", blk, mask)
+        held[4] = exchange(packed, "blk", blk, 4)
         theirs = exchange(mine, "chan", 2, 1)
 
         def step(masks, rows, last=False, split=False):
@@ -294,11 +293,13 @@
 
         *rows, forward, inverse = step((0,), (), split=True)
         tables = (forward, inverse)
-        near = lax.optimization_barrier((rows[0], *(held[m] for m in (3, 2, 1, 4))))
-        held.update(zip((3, 2, 1, 4), near[1:]))
+        rows, packed = lax.optimization_barrier((rows[0], packed))
+        held[2] = exchange(packed, "blk", blk, 2)
+        held[1] = exchange(packed, "blk", blk, 1)
         held[6] = exchange(held[4], "blk", blk, 2)
         held[5] = exchange(held[4], "blk", blk, 1)
-        rows = step((1, 2), near[:1])
+        held[3] = exchange(held[1], "blk", blk, 2)
+        rows = step((1, 2), (rows,))
         rows, held[6] = lax.optimization_barrier((rows[0], held[6]))
         held[7] = exchange(held[6], "blk", blk, 1)
         rows = step((3, 4, 5, 6), (rows,))

time: 26.3 us -> 23.4 us (0.89)
  waiting for transfers between devices: 6.54 us -> 1.73 us
  starting transfers between devices: 9.91 us -> 11.8 us
    ppermute x9, waiting for transfers between devices: 6.54 us -> 1.73 us  [exchange(): return lax.ppermute(value, axis, [(i, i ^ mask) for i in range(size)])]
    ppermute x9, starting transfers between devices: 9.91 us -> 11.8 us  [exchange(): return lax.ppermute(value, axis, [(i, i ^ mask) for i in range(size)])]
  transfers between devices with their start and end apart: 9 -> 9, of which waited for: 6 -> 4; matrix products, arithmetic and copies ran while one was open for 0% -> 0% of each run, Pallas kernels for 22% -> 25%
where the time goes in v9:
time: 23.4 us; the launch traced here: 23.3 us
  starting transfers between devices  11.8 us (50%)
  Pallas kernels  6.91 us (30%)
  waiting for transfers between devices  1.73 us (7%)
  between operations  1.34 us (6%)
  local copies, waits for them, and re-layouts  0.84 us (4%)
  other arithmetic  0.6 us (3%)
    ppermute x9, starting transfers between devices, exchange(): return lax.ppermute(value, axis, [(i, i ^ mask) for i in range(size)])  11.8 us
    pallas_call x4, Pallas kernels, score(): pl.pallas_call(functools.partial(score_kernel, taps, shifts, places, len(...  6.81 us
    ppermute x9, waiting for transfers between devices, exchange(): return lax.ppermute(value, axis, [(i, i ^ mask) for i in range(size)])  1.73 us
    unnamed x8, local copies, waits for them, and re-layouts  0.84 us
    broadcast_in_dim x1, other arithmetic, on_device(): return (keep + exchange(send, 'chan', 2, 1))[None]  0.6 us
  transfers between devices with their start and end apart: 9, of which 4 were waited for; matrix products, arithmetic and copies ran while one was open for 0% of the time, Pallas kernels for 25%

profile of v9, /device:TPU:0, one launch (start us, length us, event | category | flops | bytes accessed | tf_op | source)
XLA Modules:
  0.0 23.3 jit_solution(10841217016712227382)
XLA Ops:
  0.0 0.5 %collective-permute-start = (bf16[191,5000]{1,0:T(8,128)(2,1)}, bf16[191,5000]{1,0:T(8,128)(2,1)S(1)}, u32[]{:S(2)}, u32[]{:S(2)}) collective-permute-start(bf16[191,5000]{1,0:T(8,128)(2,1)} %bitcast.6), channel_id=1, source_target_pairs={{0,1},{1,0},{2,3},{3,2},{4,5},{5,4},{6,7},{7,6},{8,9},{9,8},{10,11... | collective-permute-start | bytes 5730008 | tf_op jit(solution)/shard_map/ppermute | solution.py:272
  1.7 0.0 copy-start.3
  1.8 0.8 %copy-done.3 = bf16[1,256,128]{2,1,0:T(8,128)(2,1)S(1)} copy-done((bf16[1,256,128]{2,1,0:T(8,128)(2,1)S(1)}, bf16[1,256,128]{2,1,0:T(8,128)(2,1)}, u32[]{:S(2)}) %copy-start.3) | copy-done | bytes 65560
  2.6 0.0 copy-start
  2.6 0.0 copy-start.1
  2.6 0.0 copy-start.2
  2.6 0.1 pack.1
  2.7 3.7 %collective-permute-start.3 = (bf16[136,256]{1,0:T(8,128)(2,1)S(1)}, bf16[136,256]{1,0:T(8,128)(2,1)S(1)}, u32[]{:S(2)}, u32[]{:S(2)}) collective-permute-start(bf16[136,256]{1,0:T(8,128)(2,1)S(1)} %get-tuple-element.21), channel_id=1, source_target_pairs={{0,8},{2,10},{4,12},{6,14},{8,0},{10,2},{12,4},{14,6},{1,9},{3,11}... | collective-permute-start | bytes 208904 | tf_op jit(solution)/shard_map/ppermute | solution.py:272
  6.4 0.0 collective-permute-done.refs_1_
  6.4 0.0 copy-done
  6.4 0.0 copy-done.1
  6.4 0.0 copy-done.2
  6.4 1.0 %score.4 = (f32[8,64]{1,0:T(8,128)S(1)}, bf16[624,192]{1,0:T(8,128)(2,1)S(1)}, bf16[192,208]{1,0:T(8,128)(2,1)S(1)}) custom-call(bf16[191,5000]{1,0:T(8,128)(2,1)S(1)} %bitcast.7, bf16[191,5000]{1,0:T(8,128)(2,1)S(1)} %collective-permute-done.refs_1_, f32[208,192]{1,0:T(8,128)S(1)} %copy-done.1, f32[64,208]{1,0:T(8,128)S(1)} %copy-done.2, ...), custom_call_target="tpu_custom_call" | custom-call | flops 4194304 | bytes 195584 | tf_op jit(solution)/shard_map/score/pallas_call | solution.py:249
  7.3 1.5 %collective-permute-start.1 = (bf16[136,256]{1,0:T(8,128)(2,1)S(1)}, bf16[136,256]{1,0:T(8,128)(2,1)S(1)}, u32[]{:S(2)}, u32[]{:S(2)}) collective-permute-start(bf16[136,256]{1,0:T(8,128)(2,1)S(1)} %get-tuple-element.21), channel_id=1, source_target_pairs={{0,2},{2,0},{4,6},{6,4},{8,10},{10,8},{12,14},{14,12},{1,3},{3,1},... | collective-permute-start | bytes 208904 | tf_op jit(solution)/shard_map/ppermute | solution.py:272
  8.9 1.6 %collective-permute-start.2 = (bf16[136,256]{1,0:T(8,128)(2,1)S(1)}, bf16[136,256]{1,0:T(8,128)(2,1)S(1)}, u32[]{:S(2)}, u32[]{:S(2)}) collective-permute-start(bf16[136,256]{1,0:T(8,128)(2,1)S(1)} %get-tuple-element.21), channel_id=1, source_target_pairs={{0,4},{2,6},{4,0},{6,2},{8,12},{10,14},{12,8},{14,10},{1,5},{3,7},... | collective-permute-start | bytes 208904 | tf_op jit(solution)/shard_map/ppermute | solution.py:272
  10.4 0.3 %collective-permute-done.3.refs_5_ = bf16[136,256]{1,0:T(8,128)(2,1)S(1)} collective-permute-done((bf16[136,256]{1,0:T(8,128)(2,1)S(1)}, bf16[136,256]{1,0:T(8,128)(2,1)S(1)}, u32[]{:S(2)}, u32[]{:S(2)}) %collective-permute-start.3) | collective-permute-done | bytes 69664 | tf_op jit(solution)/shard_map/ppermute | solution.py:272
  10.7 0.7 %collective-permute-start.4 = (bf16[136,256]{1,0:T(8,128)(2,1)S(1)}, bf16[136,256]{1,0:T(8,128)(2,1)S(1)}, u32[]{:S(2)}, u32[]{:S(2)}) collective-permute-start(bf16[136,256]{1,0:T(8,128)(2,1)S(1)} %collective-permute-done.3.refs_5_), channel_id=1, source_target_pairs={{0,4},{2,6},{4,0},{6,2},{8,12},{10,14},{12,8},{14,10},{1,5},{3,7},... | collective-permute-start | bytes 208904 | tf_op jit(solution)/shard_map/ppermute | solution.py:272
  11.4 1.5 %collective-permute-start.7 = (bf16[136,256]{1,0:T(8,128)(2,1)S(1)}, bf16[136,256]{1,0:T(8,128)(2,1)S(1)}, u32[]{:S(2)}, u32[]{:S(2)}) collective-permute-start(bf16[136,256]{1,0:T(8,128)(2,1)S(1)} %collective-permute-done.3.refs_5_), channel_id=1, source_target_pairs={{0,2},{2,0},{4,6},{6,4},{8,10},{10,8},{12,14},{14,12},{1,3},{3,1},... | collective-permute-start | bytes 208904 | tf_op jit(solution)/shard_map/ppermute | solution.py:272
  12.9 0.0 collective-permute-done.1.refs_4_
  12.9 1.4 %collective-permute-start.6 = (bf16[136,256]{1,0:T(8,128)(2,1)S(1)}, bf16[136,256]{1,0:T(8,128)(2,1)S(1)}, u32[]{:S(2)}, u32[]{:S(2)}) collective-permute-start(bf16[136,256]{1,0:T(8,128)(2,1)S(1)} %collective-permute-done.1.refs_4_), channel_id=1, source_target_pairs={{0,4},{2,6},{4,0},{6,2},{8,12},{10,14},{12,8},{14,10},{1,5},{3,7},... | collective-permute-start | bytes 208904 | tf_op jit(solution)/shard_map/ppermute | solution.py:272
  14.3 0.0 collective-permute-done.2.refs_5_
  14.3 1.7 %score.5.refs_8_ = f32[8,64]{1,0:T(8,128)S(1)} custom-call(bf16[191,5000]{1,0:T(8,128)(2,1)S(1)} %bitcast.8, bf16[191,5000]{1,0:T(8,128)(2,1)S(1)} %collective-permute-done.refs_1_, bf16[624,192]{1,0:T(8,128)(2,1)S(1)} %get-tuple-element.17.refs_2_, bf16[192,208]{1,0:T(8,128)(2,1)S(1)} %get-tuple-element.18.refs_3_, ...), custom_call_target="tpu_custom_call" | custom-call | flops 8388608 | bytes 391168 | tf_op jit(solution)/shard_map/score/pallas_call | solution.py:249
  16.0 0.0 collective-permute-done.4.refs_7_
  16.0 1.0 %collective-permute-start.5 = (bf16[136,256]{1,0:T(8,128)(2,1)S(1)}, bf16[136,256]{1,0:T(8,128)(2,1)S(1)}, u32[]{:S(2)}, u32[]{:S(2)}) collective-permute-start(bf16[136,256]{1,0:T(8,128)(2,1)S(1)} %collective-permute-done.4.refs_7_), channel_id=1, source_target_pairs={{0,2},{2,0},{4,6},{6,4},{8,10},{10,8},{12,14},{14,12},{1,3},{3,1},... | collective-permute-start | bytes 208904 | tf_op jit(solution)/shard_map/ppermute | solution.py:272
  17.1 0.0 collective-permute-done.7.refs_6_
  17.1 0.2 collective-permute-done.6.refs_4_
  17.3 3.1 %score.6.refs_5_ = f32[8,64]{1,0:T(8,128)S(1)} custom-call(bf16[191,5000]{1,0:T(8,128)(2,1)S(1)} %bitcast.9, bf16[191,5000]{1,0:T(8,128)(2,1)S(1)} %collective-permute-done.refs_1_, bf16[624,192]{1,0:T(8,128)(2,1)S(1)} %get-tuple-element.17.refs_2_, bf16[192,208]{1,0:T(8,128)(2,1)S(1)} %get-tuple-element.18.refs_3_, ...), custom_call_target="tpu_custom_call" | custom-call | flops 16777216 | bytes 782336 | tf_op jit(solution)/shard_map/score/pallas_call | solution.py:249
  20.3 0.1 collective-permute-done.5.refs_4_
  20.4 1.1 %score.7 = (f32[8,32]{1,0:T(8,128)S(1)}, f32[8,32]{1,0:T(8,128)S(1)}) custom-call(bf16[191,5000]{1,0:T(8,128)(2,1)S(1)} %bitcast.10, bf16[191,5000]{1,0:T(8,128)(2,1)S(1)} %collective-permute-done.refs_1_, bf16[624,192]{1,0:T(8,128)(2,1)S(1)} %get-tuple-element.17.refs_2_, bf16[192,208]{1,0:T(8,128)(2,1)S(1)} %get-tuple-element.18.refs_3_, ...), custom_call_target="tpu_custom_call" | custom-call | flops 4194304 | bytes 195584 | tf_op jit(solution)/shard_map/score/pallas_call | solution.py:249
  21.5 0.0 collective-permute-start.8
  21.5 1.2 %collective-permute-done.8 = f32[8,32]{1,0:T(8,128)S(1)} collective-permute-done((f32[8,32]{1,0:T(8,128)S(1)}, f32[8,32]{1,0:T(8,128)S(1)}, u32[]{:S(2)}, u32[]{:S(2)}) %collective-permute-start.8) | collective-permute-done | bytes 1056 | tf_op jit(solution)/shard_map/ppermute | solution.py:272
  22.7 0.6 %add_bitcast_fusion = f32[1,8,32]{2,1,0:T(8,128)} fusion(f32[8,32]{1,0:T(8,128)S(1)} %get-tuple-element.25, f32[8,32]{1,0:T(8,128)S(1)} %collective-permute-done.8), kind=kLoop, calls=%fused_computation | loop fusion | flops 256 | bytes 3072 | tf_op jit(solution)/shard_map/broadcast_in_dim | solution.py:321
Async XLA Ops:
  0.0 6.4 %collective-permute-start = (bf16[191,5000]{1,0:T(8,128)(2,1)}, bf16[191,5000]{1,0:T(8,128)(2,1)S(1)}, u32[]{:S(2)}, u32[]{:S(2)}) collective-permute-start(bf16[191,5000]{1,0:T(8,128)(2,1)} %bitcast.6), channel_id=1, source_target_pairs={{0,1},{1,0},{2,3},{3,2},{4,5},{5,4},{6,7},{7,6},{8,9},{9,8},{10,11... | collective-permute-start | bytes 5730008 | tf_op jit(solution)/shard_map/ppermute | solution.py:272
  1.7 0.8 %copy-start.3 = (bf16[1,256,128]{2,1,0:T(8,128)(2,1)S(1)}, bf16[1,256,128]{2,1,0:T(8,128)(2,1)}, u32[]{:S(2)}) copy-start(bf16[1,256,128]{2,1,0:T(8,128)(2,1)} %param.7) | copy-start | bytes 196612
  2.6 3.8 %copy-start = (bf16[1,5000,191]{1,2,0:T(8,128)(2,1)S(1)}, bf16[1,5000,191]{1,2,0:T(8,128)(2,1)}, u32[]{:S(2)}) copy-start(bf16[1,5000,191]{1,2,0:T(8,128)(2,1)} %param.6) | copy-start | bytes 5730004
  2.6 3.8 %copy-start.1 = (f32[208,192]{1,0:T(8,128)S(1)}, f32[208,192]{1,0:T(8,128)}, u32[]{:S(2)}) copy-start(f32[208,192]{1,0:T(8,128)} %constant.4.clone.refs_2_) | copy-start | bytes 479236
  2.6 3.8 %copy-start.2 = (f32[64,208]{1,0:T(8,128)S(1)}, f32[64,208]{1,0:T(8,128)}, u32[]{:S(2)}) copy-start(f32[64,208]{1,0:T(8,128)} %constant.5.clone.refs_3_) | copy-start | bytes 159748
  2.7 8.0 %collective-permute-start.3 = (bf16[136,256]{1,0:T(8,128)(2,1)S(1)}, bf16[136,256]{1,0:T(8,128)(2,1)S(1)}, u32[]{:S(2)}, u32[]{:S(2)}) collective-permute-start(bf16[136,256]{1,0:T(8,128)(2,1)S(1)} %get-tuple-element.21), channel_id=1, source_target_pairs={{0,8},{2,10},{4,12},{6,14},{8,0},{10,2},{12,4},{14,6},{1,9},{3,11}... | collective-permute-start | bytes 208904 | tf_op jit(solution)/shard_map/ppermute | solution.py:272
  7.3 5.6 %collective-permute-start.1 = (bf16[136,256]{1,0:T(8,128)(2,1)S(1)}, bf16[136,256]{1,0:T(8,128)(2,1)S(1)}, u32[]{:S(2)}, u32[]{:S(2)}) collective-permute-start(bf16[136,256]{1,0:T(8,128)(2,1)S(1)} %get-tuple-element.21), channel_id=1, source_target_pairs={{0,2},{2,0},{4,6},{6,4},{8,10},{10,8},{12,14},{14,12},{1,3},{3,1},... | collective-permute-start | bytes 208904 | tf_op jit(solution)/shard_map/ppermute | solution.py:272
  8.9 5.4 %collective-permute-start.2 = (bf16[136,256]{1,0:T(8,128)(2,1)S(1)}, bf16[136,256]{1,0:T(8,128)(2,1)S(1)}, u32[]{:S(2)}, u32[]{:S(2)}) collective-permute-start(bf16[136,256]{1,0:T(8,128)(2,1)S(1)} %get-tuple-element.21), channel_id=1, source_target_pairs={{0,4},{2,6},{4,0},{6,2},{8,12},{10,14},{12,8},{14,10},{1,5},{3,7},... | collective-permute-start | bytes 208904 | tf_op jit(solution)/shard_map/ppermute | solution.py:272
  10.7 5.3 %collective-permute-start.4 = (bf16[136,256]{1,0:T(8,128)(2,1)S(1)}, bf16[136,256]{1,0:T(8,128)(2,1)S(1)}, u32[]{:S(2)}, u32[]{:S(2)}) collective-permute-start(bf16[136,256]{1,0:T(8,128)(2,1)S(1)} %collective-permute-done.3.refs_5_), channel_id=1, source_target_pairs={{0,4},{2,6},{4,0},{6,2},{8,12},{10,14},{12,8},{14,10},{1,5},{3,7},... | collective-permute-start | bytes 208904 | tf_op jit(solution)/shard_map/ppermute | solution.py:272
  11.4 5.6 %collective-permute-start.7 = (bf16[136,256]{1,0:T(8,128)(2,1)S(1)}, bf16[136,256]{1,0:T(8,128)(2,1)S(1)}, u32[]{:S(2)}, u32[]{:S(2)}) collective-permute-start(bf16[136,256]{1,0:T(8,128)(2,1)S(1)} %collective-permute-done.3.refs_5_), channel_id=1, source_target_pairs={{0,2},{2,0},{4,6},{6,4},{8,10},{10,8},{12,14},{14,12},{1,3},{3,1},... | collective-permute-start | bytes 208904 | tf_op jit(solution)/shard_map/ppermute | solution.py:272
  12.9 4.3 %collective-permute-start.6 = (bf16[136,256]{1,0:T(8,128)(2,1)S(1)}, bf16[136,256]{1,0:T(8,128)(2,1)S(1)}, u32[]{:S(2)}, u32[]{:S(2)}) collective-permute-start(bf16[136,256]{1,0:T(8,128)(2,1)S(1)} %collective-permute-done.1.refs_4_), channel_id=1, source_target_pairs={{0,4},{2,6},{4,0},{6,2},{8,12},{10,14},{12,8},{14,10},{1,5},{3,7},... | collective-permute-start | bytes 208904 | tf_op jit(solution)/shard_map/ppermute | solution.py:272
  16.0 4.4 %collective-permute-start.5 = (bf16[136,256]{1,0:T(8,128)(2,1)S(1)}, bf16[136,256]{1,0:T(8,128)(2,1)S(1)}, u32[]{:S(2)}, u32[]{:S(2)}) collective-permute-start(bf16[136,256]{1,0:T(8,128)(2,1)S(1)} %collective-permute-done.4.refs_7_), channel_id=1, source_target_pairs={{0,2},{2,0},{4,6},{6,4},{8,10},{10,8},{12,14},{14,12},{1,3},{3,1},... | collective-permute-start | bytes 208904 | tf_op jit(solution)/shard_map/ppermute | solution.py:272
  21.5 1.2 %collective-permute-start.8 = (f32[8,32]{1,0:T(8,128)S(1)}, f32[8,32]{1,0:T(8,128)S(1)}, u32[]{:S(2)}, u32[]{:S(2)}) collective-permute-start(f32[8,32]{1,0:T(8,128)S(1)} %get-tuple-element.26), channel_id=1, source_target_pairs={{0,1},{1,0},{2,3},{3,2},{4,5},{5,4},{6,7},{7,6},{8,9},{9,8},{10,11... | collective-permute-start | bytes 3080 | tf_op jit(solution)/shard_map/ppermute | solution.py:272

commit v10 on v9

--- a/solution.py
+++ b/solution.py
@@ -283,6 +283,7 @@
     if blk == CHUNK:
         held = {0: own}
         held[4] = exchange(packed, "blk", blk, 4)
+        held[1] = exchange(packed, "blk", blk, 1)
         theirs = exchange(mine, "chan", 2, 1)
 
         def step(masks, rows, last=False, split=False):
@@ -295,14 +296,13 @@
         tables = (forward, inverse)
         rows, packed = lax.optimization_barrier((rows[0], packed))
         held[2] = exchange(packed, "blk", blk, 2)
-        held[1] = exchange(packed, "blk", blk, 1)
         held[6] = exchange(held[4], "blk", blk, 2)
         held[5] = exchange(held[4], "blk", blk, 1)
         held[3] = exchange(held[1], "blk", blk, 2)
-        rows = step((1, 2), (rows,))
+        rows = step((1, 2, 3), (rows,))
         rows, held[6] = lax.optimization_barrier((rows[0], held[6]))
         held[7] = exchange(held[6], "blk", blk, 1)
-        rows = step((3, 4, 5, 6), (rows,))
+        rows = step((4, 5, 6), (rows,))
         rows = step((7,), rows, True)
         keep, send = rows
     else:

time: 23.4 us -> 25 us (1.068)
  waiting for transfers between devices: 1.73 us -> 3.47 us
    ppermute x9, waiting for transfers between devices: 1.73 us -> 3.47 us  [exchange(): return lax.ppermute(value, axis, [(i, i ^ mask) for i in range(size)])]
  transfers between devices with their start and end apart: 9 -> 9, of which waited for: 4 -> 5; matrix products, arithmetic and copies ran while one was open for 0% -> 0% of each run, Pallas kernels for 25% -> 24%
where the time goes in v10:
time: 25 us; the launch traced here: 24.9 us
  starting transfers between devices  11.7 us (47%)
  Pallas kernels  6.94 us (28%)
  waiting for transfers between devices  3.47 us (14%)
  between operations  1.34 us (5%)
  local copies, waits for them, and re-layouts  0.84 us (3%)
  other arithmetic  0.6 us (2%)
    ppermute x9, starting transfers between devices, exchange(): return lax.ppermute(value, axis, [(i, i ^ mask) for i in range(size)])  11.7 us
    pallas_call x4, Pallas kernels, score(): pl.pallas_call(functools.partial(score_kernel, taps, shifts, places, len(...  6.85 us
    ppermute x9, waiting for transfers between devices, exchange(): return lax.ppermute(value, axis, [(i, i ^ mask) for i in range(size)])  3.47 us
    unnamed x8, local copies, waits for them, and re-layouts  0.84 us
    broadcast_in_dim x1, other arithmetic, on_device(): return (keep + exchange(send, 'chan', 2, 1))[None]  0.6 us
  transfers between devices with their start and end apart: 9, of which 5 were waited for; matrix products, arithmetic and copies ran while one was open for 0% of the time, Pallas kernels for 24%

profile of v10, /device:TPU:0, one launch (start us, length us, event | category | flops | bytes accessed | tf_op | source)
XLA Modules:
  0.0 24.9 jit_solution(14538143498798574928)
XLA Ops:
  0.0 0.5 %collective-permute-start = (bf16[191,5000]{1,0:T(8,128)(2,1)}, bf16[191,5000]{1,0:T(8,128)(2,1)S(1)}, u32[]{:S(2)}, u32[]{:S(2)}) collective-permute-start(bf16[191,5000]{1,0:T(8,128)(2,1)} %bitcast.6), channel_id=1, source_target_pairs={{0,1},{1,0},{2,3},{3,2},{4,5},{5,4},{6,7},{7,6},{8,9},{9,8},{10,11... | collective-permute-start | bytes 5730008 | tf_op jit(solution)/shard_map/ppermute | solution.py:272
  1.7 0.0 copy-start.3
  1.8 0.8 %copy-done.3 = bf16[1,256,128]{2,1,0:T(8,128)(2,1)S(1)} copy-done((bf16[1,256,128]{2,1,0:T(8,128)(2,1)S(1)}, bf16[1,256,128]{2,1,0:T(8,128)(2,1)}, u32[]{:S(2)}) %copy-start.3) | copy-done | bytes 65560
  2.6 0.0 copy-start
  2.6 0.0 copy-start.1
  2.6 0.0 copy-start.2
  2.6 0.1 pack.1
  2.7 2.6 %collective-permute-start.1 = (bf16[136,256]{1,0:T(8,128)(2,1)S(1)}, bf16[136,256]{1,0:T(8,128)(2,1)S(1)}, u32[]{:S(2)}, u32[]{:S(2)}) collective-permute-start(bf16[136,256]{1,0:T(8,128)(2,1)S(1)} %get-tuple-element.21), channel_id=1, source_target_pairs={{0,2},{2,0},{4,6},{6,4},{8,10},{10,8},{12,14},{14,12},{1,3},{3,1},... | collective-permute-start | bytes 208904 | tf_op jit(solution)/shard_map/ppermute | solution.py:272
  5.3 2.6 %collective-permute-start.4 = (bf16[136,256]{1,0:T(8,128)(2,1)S(1)}, bf16[136,256]{1,0:T(8,128)(2,1)S(1)}, u32[]{:S(2)}, u32[]{:S(2)}) collective-permute-start(bf16[136,256]{1,0:T(8,128)(2,1)S(1)} %get-tuple-element.21), channel_id=1, source_target_pairs={{0,8},{2,10},{4,12},{6,14},{8,0},{10,2},{12,4},{14,6},{1,9},{3,11}... | collective-permute-start | bytes 208904 | tf_op jit(solution)/shard_map/ppermute | solution.py:272
  7.8 0.3 %collective-permute-done.1.refs_4_ = bf16[136,256]{1,0:T(8,128)(2,1)S(1)} collective-permute-done((bf16[136,256]{1,0:T(8,128)(2,1)S(1)}, bf16[136,256]{1,0:T(8,128)(2,1)S(1)}, u32[]{:S(2)}, u32[]{:S(2)}) %collective-permute-start.1) | collective-permute-done | bytes 69664 | tf_op jit(solution)/shard_map/ppermute | solution.py:272
  8.1 1.8 %collective-permute-start.3 = (bf16[136,256]{1,0:T(8,128)(2,1)S(1)}, bf16[136,256]{1,0:T(8,128)(2,1)S(1)}, u32[]{:S(2)}, u32[]{:S(2)}) collective-permute-start(bf16[136,256]{1,0:T(8,128)(2,1)S(1)} %collective-permute-done.1.refs_4_), channel_id=1, source_target_pairs={{0,4},{2,6},{4,0},{6,2},{8,12},{10,14},{12,8},{14,10},{1,5},{3,7},... | collective-permute-start | bytes 208904 | tf_op jit(solution)/shard_map/ppermute | solution.py:272
  9.9 0.0 collective-permute-done.refs_1_
  9.9 0.0 copy-done
  9.9 0.0 copy-done.1
  9.9 0.0 copy-done.2
  10.0 0.9 %score.4 = (f32[8,64]{1,0:T(8,128)S(1)}, bf16[624,192]{1,0:T(8,128)(2,1)S(1)}, bf16[192,208]{1,0:T(8,128)(2,1)S(1)}) custom-call(bf16[191,5000]{1,0:T(8,128)(2,1)S(1)} %bitcast.7, bf16[191,5000]{1,0:T(8,128)(2,1)S(1)} %collective-permute-done.refs_1_, f32[208,192]{1,0:T(8,128)S(1)} %copy-done.1, f32[64,208]{1,0:T(8,128)S(1)} %copy-done.2, ...), custom_call_target="tpu_custom_call" | custom-call | flops 4194304 | bytes 195584 | tf_op jit(solution)/shard_map/score/pallas_call | solution.py:249
  10.9 0.2 collective-permute-start.2
  11.1 0.9 %collective-permute-done.4.refs_4_ = bf16[136,256]{1,0:T(8,128)(2,1)S(1)} collective-permute-done((bf16[136,256]{1,0:T(8,128)(2,1)S(1)}, bf16[136,256]{1,0:T(8,128)(2,1)S(1)}, u32[]{:S(2)}, u32[]{:S(2)}) %collective-permute-start.4) | collective-permute-done | bytes 69664 | tf_op jit(solution)/shard_map/ppermute | solution.py:272
  12.0 1.0 %collective-permute-start.5 = (bf16[136,256]{1,0:T(8,128)(2,1)S(1)}, bf16[136,256]{1,0:T(8,128)(2,1)S(1)}, u32[]{:S(2)}, u32[]{:S(2)}) collective-permute-start(bf16[136,256]{1,0:T(8,128)(2,1)S(1)} %collective-permute-done.4.refs_4_), channel_id=1, source_target_pairs={{0,4},{2,6},{4,0},{6,2},{8,12},{10,14},{12,8},{14,10},{1,5},{3,7},... | collective-permute-start | bytes 208904 | tf_op jit(solution)/shard_map/ppermute | solution.py:272
  13.0 1.5 %collective-permute-start.7 = (bf16[136,256]{1,0:T(8,128)(2,1)S(1)}, bf16[136,256]{1,0:T(8,128)(2,1)S(1)}, u32[]{:S(2)}, u32[]{:S(2)}) collective-permute-start(bf16[136,256]{1,0:T(8,128)(2,1)S(1)} %collective-permute-done.4.refs_4_), channel_id=1, source_target_pairs={{0,2},{2,0},{4,6},{6,4},{8,10},{10,8},{12,14},{14,12},{1,3},{3,1},... | collective-permute-start | bytes 208904 | tf_op jit(solution)/shard_map/ppermute | solution.py:272
  14.5 0.0 collective-permute-done.3.refs_6_
  14.5 0.8 %collective-permute-done.2.refs_5_ = bf16[136,256]{1,0:T(8,128)(2,1)S(1)} collective-permute-done((bf16[136,256]{1,0:T(8,128)(2,1)S(1)}, bf16[136,256]{1,0:T(8,128)(2,1)S(1)}, u32[]{:S(2)}, u32[]{:S(2)}) %collective-permute-start.2) | collective-permute-done | bytes 69664 | tf_op jit(solution)/shard_map/ppermute | solution.py:272
  15.2 2.4 %score.5.refs_7_ = f32[8,64]{1,0:T(8,128)S(1)} custom-call(bf16[191,5000]{1,0:T(8,128)(2,1)S(1)} %bitcast.8, bf16[191,5000]{1,0:T(8,128)(2,1)S(1)} %collective-permute-done.refs_1_, bf16[624,192]{1,0:T(8,128)(2,1)S(1)} %get-tuple-element.17.refs_2_, bf16[192,208]{1,0:T(8,128)(2,1)S(1)} %get-tuple-element.18.refs_3_, ...), custom_call_target="tpu_custom_call" | custom-call | flops 12582912 | bytes 586752 | tf_op jit(solution)/shard_map/score/pallas_call | solution.py:249
  17.7 0.0 collective-permute-done.5.refs_6_
  17.7 1.5 %collective-permute-start.6 = (bf16[136,256]{1,0:T(8,128)(2,1)S(1)}, bf16[136,256]{1,0:T(8,128)(2,1)S(1)}, u32[]{:S(2)}, u32[]{:S(2)}) collective-permute-start(bf16[136,256]{1,0:T(8,128)(2,1)S(1)} %collective-permute-done.5.refs_6_), channel_id=1, source_target_pairs={{0,2},{2,0},{4,6},{6,4},{8,10},{10,8},{12,14},{14,12},{1,3},{3,1},... | collective-permute-start | bytes 208904 | tf_op jit(solution)/shard_map/ppermute | solution.py:272
  19.2 0.0 collective-permute-done.7.refs_5_
  19.2 2.4 %score.6.refs_5_ = f32[8,64]{1,0:T(8,128)S(1)} custom-call(bf16[191,5000]{1,0:T(8,128)(2,1)S(1)} %bitcast.9, bf16[191,5000]{1,0:T(8,128)(2,1)S(1)} %collective-permute-done.refs_1_, bf16[624,192]{1,0:T(8,128)(2,1)S(1)} %get-tuple-element.17.refs_2_, bf16[192,208]{1,0:T(8,128)(2,1)S(1)} %get-tuple-element.18.refs_3_, ...), custom_call_target="tpu_custom_call" | custom-call | flops 12582912 | bytes 586752 | tf_op jit(solution)/shard_map/score/pallas_call | solution.py:249
  21.6 0.4 %collective-permute-done.6.refs_4_ = bf16[136,256]{1,0:T(8,128)(2,1)S(1)} collective-permute-done((bf16[136,256]{1,0:T(8,128)(2,1)S(1)}, bf16[136,256]{1,0:T(8,128)(2,1)S(1)}, u32[]{:S(2)}, u32[]{:S(2)}) %collective-permute-start.6) | collective-permute-done | bytes 69664 | tf_op jit(solution)/shard_map/ppermute | solution.py:272
  22.0 1.1 %score.7 = (f32[8,32]{1,0:T(8,128)S(1)}, f32[8,32]{1,0:T(8,128)S(1)}) custom-call(bf16[191,5000]{1,0:T(8,128)(2,1)S(1)} %bitcast.10, bf16[191,5000]{1,0:T(8,128)(2,1)S(1)} %collective-permute-done.refs_1_, bf16[624,192]{1,0:T(8,128)(2,1)S(1)} %get-tuple-element.17.refs_2_, bf16[192,208]{1,0:T(8,128)(2,1)S(1)} %get-tuple-element.18.refs_3_, ...), custom_call_target="tpu_custom_call" | custom-call | flops 4194304 | bytes 195584 | tf_op jit(solution)/shard_map/score/pallas_call | solution.py:249
  23.1 0.0 collective-permute-start.8
  23.1 1.2 %collective-permute-done.8 = f32[8,32]{1,0:T(8,128)S(1)} collective-permute-done((f32[8,32]{1,0:T(8,128)S(1)}, f32[8,32]{1,0:T(8,128)S(1)}, u32[]{:S(2)}, u32[]{:S(2)}) %collective-permute-start.8) | collective-permute-done | bytes 1056 | tf_op jit(solution)/shard_map/ppermute | solution.py:272
  24.3 0.6 %add_bitcast_fusion = f32[1,8,32]{2,1,0:T(8,128)} fusion(f32[8,32]{1,0:T(8,128)S(1)} %get-tuple-element.25, f32[8,32]{1,0:T(8,128)S(1)} %collective-permute-done.8), kind=kLoop, calls=%fused_computation | loop fusion | flops 256 | bytes 3072 | tf_op jit(solution)/shard_map/broadcast_in_dim | solution.py:321
Async XLA Ops:
  0.0 9.9 %collective-permute-start = (bf16[191,5000]{1,0:T(8,128)(2,1)}, bf16[191,5000]{1,0:T(8,128)(2,1)S(1)}, u32[]{:S(2)}, u32[]{:S(2)}) collective-permute-start(bf16[191,5000]{1,0:T(8,128)(2,1)} %bitcast.6), channel_id=1, source_target_pairs={{0,1},{1,0},{2,3},{3,2},{4,5},{5,4},{6,7},{7,6},{8,9},{9,8},{10,11... | collective-permute-start | bytes 5730008 | tf_op jit(solution)/shard_map/ppermute | solution.py:272
  1.7 0.8 %copy-start.3 = (bf16[1,256,128]{2,1,0:T(8,128)(2,1)S(1)}, bf16[1,256,128]{2,1,0:T(8,128)(2,1)}, u32[]{:S(2)}) copy-start(bf16[1,256,128]{2,1,0:T(8,128)(2,1)} %param.7) | copy-start | bytes 196612
  2.6 7.3 %copy-start = (bf16[1,5000,191]{1,2,0:T(8,128)(2,1)S(1)}, bf16[1,5000,191]{1,2,0:T(8,128)(2,1)}, u32[]{:S(2)}) copy-start(bf16[1,5000,191]{1,2,0:T(8,128)(2,1)} %param.6) | copy-start | bytes 5730004
  2.6 7.4 %copy-start.1 = (f32[208,192]{1,0:T(8,128)S(1)}, f32[208,192]{1,0:T(8,128)}, u32[]{:S(2)}) copy-start(f32[208,192]{1,0:T(8,128)} %constant.4.clone.refs_2_) | copy-start | bytes 479236
  2.6 7.4 %copy-start.2 = (f32[64,208]{1,0:T(8,128)S(1)}, f32[64,208]{1,0:T(8,128)}, u32[]{:S(2)}) copy-start(f32[64,208]{1,0:T(8,128)} %constant.5.clone.refs_3_) | copy-start | bytes 159748
  2.7 5.4 %collective-permute-start.1 = (bf16[136,256]{1,0:T(8,128)(2,1)S(1)}, bf16[136,256]{1,0:T(8,128)(2,1)S(1)}, u32[]{:S(2)}, u32[]{:S(2)}) collective-permute-start(bf16[136,256]{1,0:T(8,128)(2,1)S(1)} %get-tuple-element.21), channel_id=1, source_target_pairs={{0,2},{2,0},{4,6},{6,4},{8,10},{10,8},{12,14},{14,12},{1,3},{3,1},... | collective-permute-start | bytes 208904 | tf_op jit(solution)/shard_map/ppermute | solution.py:272
  5.3 6.7 %collective-permute-start.4 = (bf16[136,256]{1,0:T(8,128)(2,1)S(1)}, bf16[136,256]{1,0:T(8,128)(2,1)S(1)}, u32[]{:S(2)}, u32[]{:S(2)}) collective-permute-start(bf16[136,256]{1,0:T(8,128)(2,1)S(1)} %get-tuple-element.21), channel_id=1, source_target_pairs={{0,8},{2,10},{4,12},{6,14},{8,0},{10,2},{12,4},{14,6},{1,9},{3,11}... | collective-permute-start | bytes 208904 | tf_op jit(solution)/shard_map/ppermute | solution.py:272
  8.1 6.4 %collective-permute-start.3 = (bf16[136,256]{1,0:T(8,128)(2,1)S(1)}, bf16[136,256]{1,0:T(8,128)(2,1)S(1)}, u32[]{:S(2)}, u32[]{:S(2)}) collective-permute-start(bf16[136,256]{1,0:T(8,128)(2,1)S(1)} %collective-permute-done.1.refs_4_), channel_id=1, source_target_pairs={{0,4},{2,6},{4,0},{6,2},{8,12},{10,14},{12,8},{14,10},{1,5},{3,7},... | collective-permute-start | bytes 208904 | tf_op jit(solution)/shard_map/ppermute | solution.py:272
  10.9 4.3 %collective-permute-start.2 = (bf16[136,256]{1,0:T(8,128)(2,1)S(1)}, bf16[136,256]{1,0:T(8,128)(2,1)S(1)}, u32[]{:S(2)}, u32[]{:S(2)}) collective-permute-start(bf16[136,256]{1,0:T(8,128)(2,1)S(1)} %get-tuple-element.21), channel_id=1, source_target_pairs={{0,4},{2,6},{4,0},{6,2},{8,12},{10,14},{12,8},{14,10},{1,5},{3,7},... | collective-permute-start | bytes 208904 | tf_op jit(solution)/shard_map/ppermute | solution.py:272
  12.0 5.7 %collective-permute-start.5 = (bf16[136,256]{1,0:T(8,128)(2,1)S(1)}, bf16[136,256]{1,0:T(8,128)(2,1)S(1)}, u32[]{:S(2)}, u32[]{:S(2)}) collective-permute-start(bf16[136,256]{1,0:T(8,128)(2,1)S(1)} %collective-permute-done.4.refs_4_), channel_id=1, source_target_pairs={{0,4},{2,6},{4,0},{6,2},{8,12},{10,14},{12,8},{14,10},{1,5},{3,7},... | collective-permute-start | bytes 208904 | tf_op jit(solution)/shard_map/ppermute | solution.py:272
  13.0 6.2 %collective-permute-start.7 = (bf16[136,256]{1,0:T(8,128)(2,1)S(1)}, bf16[136,256]{1,0:T(8,128)(2,1)S(1)}, u32[]{:S(2)}, u32[]{:S(2)}) collective-permute-start(bf16[136,256]{1,0:T(8,128)(2,1)S(1)} %collective-permute-done.4.refs_4_), channel_id=1, source_target_pairs={{0,2},{2,0},{4,6},{6,4},{8,10},{10,8},{12,14},{14,12},{1,3},{3,1},... | collective-permute-start | bytes 208904 | tf_op jit(solution)/shard_map/ppermute | solution.py:272
  17.7 4.3 %collective-permute-start.6 = (bf16[136,256]{1,0:T(8,128)(2,1)S(1)}, bf16[136,256]{1,0:T(8,128)(2,1)S(1)}, u32[]{:S(2)}, u32[]{:S(2)}) collective-permute-start(bf16[136,256]{1,0:T(8,128)(2,1)S(1)} %collective-permute-done.5.refs_6_), channel_id=1, source_target_pairs={{0,2},{2,0},{4,6},{6,4},{8,10},{10,8},{12,14},{14,12},{1,3},{3,1},... | collective-permute-start | bytes 208904 | tf_op jit(solution)/shard_map/ppermute | solution.py:272
  23.1 1.2 %collective-permute-start.8 = (f32[8,32]{1,0:T(8,128)S(1)}, f32[8,32]{1,0:T(8,128)S(1)}, u32[]{:S(2)}, u32[]{:S(2)}) collective-permute-start(f32[8,32]{1,0:T(8,128)S(1)} %get-tuple-element.26), channel_id=1, source_target_pairs={{0,1},{1,0},{2,3},{3,2},{4,5},{5,4},{6,7},{7,6},{8,9},{9,8},{10,11... | collective-permute-start | bytes 3080 | tf_op jit(solution)/shard_map/ppermute | solution.py:272
